TPU v7x, 256 devices: a whole 4x4x8 slice. The times are simulated.
256 devices in a mesh: pipe: 4 (over y), ctx: 8 (over z), tp: 8 (over x, core).
Axes of the slice: x: 4, y: 4, z: 8, core: 2. Of those that a mesh axis runs over, the one named last changes fastest.
Arguments:
- query_in: bfloat16 [4, 1024, 16384], P('pipe', 'ctx', 'tp'), may hold values from -200 to 200
- key_in: bfloat16 [4, 1024, 1024], P('pipe', ('ctx', 'tp')), may hold values from -7 to 7
- value_in: bfloat16 [4, 1024, 1024], P('pipe', ('ctx', 'tp')), may hold values from -6 to 6
- doc_ids: int32 [1024], replicated, may hold values from 0 to 7, never falling along the last dimension, each value on 1 to 512 neighbouring positions
- stretch_order: int32 [8], replicated, may hold values from 0 to 7, each once
- out_cot: bfloat16 [4, 1024, 16384], P('pipe', 'ctx', 'tp'), may hold values from -6 to 6
Outputs:
- attn_out: bfloat16 [4, 1024, 16384], P('pipe', 'ctx', 'tp')
- grad_query: bfloat16 [4, 1024, 16384], P('pipe', 'ctx', 'tp')
- grad_key: bfloat16 [4, 1024, 1024], P('pipe', ('ctx', 'tp'))
- grad_value: bfloat16 [4, 1024, 1024], P('pipe', ('ctx', 'tp'))
Inputs may be any that keep to these rules, and one draw needn't show every extreme that they name: `doc_ids`: never falling along positions; each document spans 1 to 512 positions, one exactly 512. `stretch_order`: each block number appears once.
All inputs are finite; a program needn't handle non-finite values.
Results may differ from a plain program's by a relative error of at most 0.04.
Values may be sent and summed in bfloat16 or wider, within the bound.
No kernel may reach another device: no remote copies, remote signals or barrier semaphores. Data moves between devices by JAX's collectives and lax.ppermute only.
A program may use at most 128 MiB of HBM per device.

v0:
```python
import jax
import jax.numpy as jnp
from jax import lax
from jax.sharding import PartitionSpec as P

KV_HEADS = 8
HEAD_DIM = 128
GROUP = 16


masked_score = -1e30


def shifted(block, axis, distance):
    devices = range(lax.axis_size(axis))
    route = [(i - distance, i) for i in devices if i - distance in devices]
    return lax.ppermute(block, axis, route)


def block_probs(query_block, keys3, allowed_block):
    row_count = query_block.shape[0]
    query4 = query_block.reshape(row_count, keys3.shape[1], GROUP, HEAD_DIM)
    scores = jnp.einsum(
        "qngd,knd->ngqk", query4, keys3, preferred_element_type=jnp.float32
    ) * HEAD_DIM ** (-0.5)
    scores = jnp.where(allowed_block[None, None], scores, masked_score)
    top = jnp.max(scores, axis=-1, keepdims=True)
    expo = jnp.exp(scores - top)
    return (expo / jnp.sum(expo, axis=-1, keepdims=True), query4)


def block_forward(query_block, keys3, values3, allowed_block):
    probs, query4 = block_probs(query_block, keys3, allowed_block)
    mixed = jnp.einsum(
        "ngqk,knd->qngd", probs.astype(jnp.bfloat16), values3, preferred_element_type=jnp.float32
    )
    return mixed.astype(jnp.bfloat16).reshape(query_block.shape[0], -1)


def block_backward(query_block, grad_block, out_block, keys3, values3, allowed_block):
    scale = HEAD_DIM ** (-0.5)
    row_count = query_block.shape[0]
    probs, query4 = block_probs(query_block, keys3, allowed_block)
    grad4 = grad_block.reshape(query4.shape)
    out4 = out_block.reshape(query4.shape)
    grad_probs = jnp.einsum("qngd,knd->ngqk", grad4, values3, preferred_element_type=jnp.float32)
    delta = jnp.sum(grad4.astype(jnp.float32) * out4.astype(jnp.float32), axis=-1).transpose(
        1, 2, 0
    )[..., None]
    grad_scores = (probs * (grad_probs - delta)).astype(jnp.bfloat16)
    grad_q = (
        jnp.einsum("ngqk,knd->qngd", grad_scores, keys3, preferred_element_type=jnp.float32) * scale
    )
    grad_k = (
        jnp.einsum("ngqk,qngd->knd", grad_scores, query4, preferred_element_type=jnp.float32)
        * scale
    )
    grad_v = jnp.einsum(
        "ngqk,qngd->knd", probs.astype(jnp.bfloat16), grad4, preferred_element_type=jnp.float32
    )
    seq_rows = keys3.shape[0]
    return (
        grad_q.astype(jnp.bfloat16).reshape(row_count, -1),
        grad_k.reshape(seq_rows, -1),
        grad_v.reshape(seq_rows, -1),
    )


def shards(query_in, key_in, value_in, doc_ids, stretch_order, out_cot):
    tp_count = lax.axis_size("tp")
    ctx_count = lax.axis_size("ctx")
    pipe_count = lax.axis_size("pipe")
    ctx_index = lax.axis_index("ctx")
    tp_index = lax.axis_index("tp")
    section_index = lax.axis_index("pipe")
    tok_rows = query_in.shape[1]
    seq_rows = tok_rows * ctx_count
    head_width = query_in.shape[2]
    kv_width = KV_HEADS * HEAD_DIM // tp_count
    keys_all, values_all = (
        lax.all_gather(key_in[0], ("ctx", "tp"), axis=0, tiled=True),
        lax.all_gather(value_in[0], ("ctx", "tp"), axis=0, tiled=True),
    )
    keys = lax.dynamic_slice_in_dim(keys_all, tp_index * kv_width, kv_width, 1)
    values = lax.dynamic_slice_in_dim(values_all, tp_index * kv_width, kv_width, 1)
    keys3 = keys.reshape(seq_rows, kv_width // HEAD_DIM, HEAD_DIM)
    values3 = values.reshape(seq_rows, kv_width // HEAD_DIM, HEAD_DIM)
    row_ids = jnp.arange(seq_rows, dtype=jnp.int32)
    block_table = (row_ids // tok_rows)[:, None] == jnp.arange(ctx_count, dtype=jnp.int32)[None, :]
    block_start = jnp.sum(jnp.where(block_table, stretch_order[None, :], 0), axis=1)
    key_position = block_start * tok_rows + row_ids % tok_rows
    key_document = jnp.take(doc_ids, key_position)
    query_position = lax.dynamic_slice_in_dim(key_position, ctx_index * tok_rows, tok_rows)
    query_document = lax.dynamic_slice_in_dim(key_document, ctx_index * tok_rows, tok_rows)
    allowed = (key_position[None, :] <= query_position[:, None]) & (
        key_document[None, :] == query_document[:, None]
    )
    own_query = query_in[0]
    own_cot = out_cot[0]
    query = jnp.zeros((tok_rows, head_width), jnp.bfloat16)
    section_out = jnp.zeros((tok_rows, head_width), jnp.bfloat16)
    incoming = jnp.zeros((tok_rows, head_width), jnp.bfloat16)
    for sweep in range(pipe_count):
        if sweep > 0:
            incoming = shifted(section_out, "pipe", 1)
        active = section_index == sweep
        query_new = (own_query.astype(jnp.float32) + incoming.astype(jnp.float32)).astype(
            jnp.bfloat16
        )
        query = jnp.where(active, query_new, query)
        previous = section_out
        section_out = lax.cond(
            active,
            lambda q: block_forward(q, keys3, values3, allowed),
            lambda q: previous,
            query_new,
        )
    grad_query = jnp.zeros((tok_rows, head_width), jnp.bfloat16)
    key_terms = jnp.zeros((seq_rows, kv_width), jnp.float32)
    value_terms = jnp.zeros((seq_rows, kv_width), jnp.float32)
    returned = jnp.zeros((tok_rows, head_width), jnp.bfloat16)
    for sweep in range(pipe_count):
        if sweep > 0:
            returned = shifted(grad_query, "pipe", -1)
        active = section_index == pipe_count - 1 - sweep
        grad_out = (own_cot.astype(jnp.float32) + returned.astype(jnp.float32)).astype(jnp.bfloat16)
        kept = (grad_query, key_terms, value_terms)
        grad_query, key_terms, value_terms = lax.cond(
            active,
            lambda g: block_backward(query, g, section_out, keys3, values3, allowed),
            lambda g: kept,
            grad_out,
        )
    key_part, value_part = (
        lax.psum_scatter(
            key_terms.astype(jnp.bfloat16), "ctx", scatter_dimension=0, tiled=True
        ).astype(jnp.float32),
        lax.psum_scatter(
            value_terms.astype(jnp.bfloat16), "ctx", scatter_dimension=0, tiled=True
        ).astype(jnp.float32),
    )
    key_grad, value_grad = (
        lax.all_to_all(
            key_part.astype(jnp.bfloat16), "tp", split_axis=0, concat_axis=1, tiled=True
        ),
        lax.all_to_all(
            value_part.astype(jnp.bfloat16), "tp", split_axis=0, concat_axis=1, tiled=True
        ),
    )
    return (section_out[None], grad_query[None], key_grad[None], value_grad[None])


def solution(mesh):
    return jax.shard_map(
        shards,
        mesh=mesh,
        in_specs=(
            P("pipe", "ctx", "tp"),
            P("pipe", ("ctx", "tp"), None),
            P("pipe", ("ctx", "tp"), None),
            P(),
            P(),
            P("pipe", "ctx", "tp"),
        ),
        out_specs=(
            P("pipe", "ctx", "tp"),
            P("pipe", "ctx", "tp"),
            P("pipe", ("ctx", "tp"), None),
            P("pipe", ("ctx", "tp"), None),
        ),
        check_vma=False,
    )
```

profile of v0, /device:TPU:1, one launch (start us, length us, event | category | flops | bytes accessed | tf_op | source)
XLA Modules:
  0.0 427.5 jit_solution(2089120865820092478)
XLA Ops:
  9.5 4.5 %gather_fusion = s32[1024]{0:T(1024)S(1)} fusion(s32[1024]{0:T(1024)S(1)} %copy-done, s32[1024]{0:T(1024)S(1)} %broadcast_clamp_fusion), kind=kCustom, calls=%fused_computation | custom fusion | bytes 12288 | tf_op jit(solution)/shard_map/jit(_take)/gather | solution.py:92
  14.6 77.6 %all-gather.5.cloned.1.call-done = bf16[1,1024,1024]{2,1,0:T(8,128)(2,1)} async-done(((bf16[1,16,1024]{2,1,0:T(8,128)(2,1)}), bf16[1,1024,1024]{2,1,0:T(8,128)(2,1)}) %all-gather.5.cloned.1.call-update) | async-done | bytes 2097168 | tf_op jit(solution)/shard_map/all_gather | solution.py:81
  92.2 77.7 %all-gather.7.cloned.1.call-done = bf16[1,1024,1024]{2,1,0:T(8,128)(2,1)} async-done(((bf16[1,16,1024]{2,1,0:T(8,128)(2,1)}), bf16[1,1024,1024]{2,1,0:T(8,128)(2,1)}) %all-gather.7.cloned.1.call-update) | async-done | bytes 2097168 | tf_op jit(solution)/shard_map/all_gather | solution.py:82
  171.2 7.5 %conditional.8 = (bf16[128,2048]{0,1:T(8,128)(2,1)}) conditional(s32[]{:T(128)} %convert_element_type.310, () %tuple.65, (pred[128,1024]{0,1:T(8,128)(4,1)S(1)}, bf16[1024,1,128]{0,2,1:T(8,128)(2,1)S(1)}, bf16[128,2048]{1,0:T(8,128)(2,1)}, bf16[1024,1,128]{2,0,1:T(8,128)(2,1)S(1)}) %tuple.171), branch_computations={%region_1.2_spmd, %region_2.5_spmd} | conditional | flops 1099165696 | bytes 27172872 | solution.py:112
  171.2 2.5 fusion.1
  173.7 1.7 fusion
  175.4 3.2 fusion.4
  179.9 1.3 collective-permute-start
  181.2 11.3 %collective-permute-done = bf16[128,2048]{1,0:T(8,128)(2,1)S(1)} collective-permute-done((bf16[128,2048]{1,0:T(8,128)(2,1)S(1)}, bf16[128,2048]{1,0:T(8,128)(2,1)S(1)}, u32[]{:S(2)}, u32[]{:S(2)}) %collective-permute-start) | collective-permute-done | bytes 524320 | tf_op jit(solution)/shard_map/ppermute | solution.py:17
  193.8 1.3 copy.278
  195.1 10.5 %collective-permute-start.1 = (bf16[128,2048]{1,0:T(8,128)(2,1)S(1)}, bf16[128,2048]{1,0:T(8,128)(2,1)S(1)}, u32[]{:S(2)}, u32[]{:S(2)}) collective-permute-start(bf16[128,2048]{1,0:T(8,128)(2,1)S(1)} %copy.278), channel_id=1, source_target_pairs={{0,64},{64,128},{128,192},{1,65},{65,129},{129,193},{2,66},{66,130... | collective-permute-start | bytes 1572872 | tf_op jit(solution)/shard_map/ppermute | solution.py:17
  205.6 10.5 %collective-permute-done.1 = bf16[128,2048]{1,0:T(8,128)(2,1)S(1)} collective-permute-done((bf16[128,2048]{1,0:T(8,128)(2,1)S(1)}, bf16[128,2048]{1,0:T(8,128)(2,1)S(1)}, u32[]{:S(2)}, u32[]{:S(2)}) %collective-permute-start.1) | collective-permute-done | bytes 524320 | tf_op jit(solution)/shard_map/ppermute | solution.py:17
  217.7 4.1 collective-permute-start.2
  221.9 9.5 %collective-permute-done.2 = bf16[128,2048]{1,0:T(8,128)(2,1)S(1)} collective-permute-done((bf16[128,2048]{1,0:T(8,128)(2,1)S(1)}, bf16[128,2048]{1,0:T(8,128)(2,1)S(1)}, u32[]{:S(2)}, u32[]{:S(2)}) %collective-permute-start.2) | collective-permute-done | bytes 524320 | tf_op jit(solution)/shard_map/ppermute | solution.py:17
  231.6 2.1 conditional.11
  231.6 2.1 copy.311
  234.9 1.3 collective-permute-start.3
  236.2 17.7 %collective-permute-done.3 = bf16[128,2048]{1,0:T(8,128)(2,1)S(1)} collective-permute-done((bf16[128,2048]{1,0:T(8,128)(2,1)S(1)}, bf16[128,2048]{1,0:T(8,128)(2,1)S(1)}, u32[]{:S(2)}, u32[]{:S(2)}) %collective-permute-start.3) | collective-permute-done | bytes 524320 | tf_op jit(solution)/shard_map/ppermute | solution.py:17
  254.5 1.3 collective-permute-start.4
  255.8 12.2 %collective-permute-done.4 = bf16[128,2048]{1,0:T(8,128)(2,1)S(1)} collective-permute-done((bf16[128,2048]{1,0:T(8,128)(2,1)S(1)}, bf16[128,2048]{1,0:T(8,128)(2,1)S(1)}, u32[]{:S(2)}, u32[]{:S(2)}) %collective-permute-start.4) | collective-permute-done | bytes 524320 | tf_op jit(solution)/shard_map/ppermute | solution.py:17
  268.5 1.3 collective-permute-start.5
  269.8 53.3 %collective-permute-done.5 = bf16[128,2048]{1,0:T(8,128)(2,1)S(1)} collective-permute-done((bf16[128,2048]{1,0:T(8,128)(2,1)S(1)}, bf16[128,2048]{1,0:T(8,128)(2,1)S(1)}, u32[]{:S(2)}, u32[]{:S(2)}) %collective-permute-start.5) | collective-permute-done | bytes 524320 | tf_op jit(solution)/shard_map/ppermute | solution.py:17
  323.3 12.9 %conditional.15 = (bf16[1024,128]{1,0:T(8,128)(2,1)S(1)}, bf16[1024,128]{1,0:T(8,128)(2,1)S(1)}, bf16[1,128,2048]{2,1,0:T(8,128)(2,1)S(1)}) conditional(s32[]{:T(128)} %convert_element_type.310, (bf16[128,2048]{0,1:T(8,128)(2,1)S(1)}, bf16[1024,128]{1,0:T(8,128)(2,1)S(1)}, bf16[1024,128]{1,0:T(8,128)(2,1)S(1)}) %get-tuple-element.454, ...), branch_computations={%region_32.33_spmd, %region_33.37_spmd} | conditional | flops 2726029312 | bytes 59072568 | solution.py:128
  325.5 1.5 fusion.147
  327.0 1.7 fusion.146
  328.8 2.1 fusion.155
  330.9 3.0 fusion.148
  337.5 29.2 %reduce-scatter.5.cloned.1.call-done = bf16[128,128]{1,0:T(8,128)(2,1)} async-done(((bf16[1024,128]{1,0:T(8,128)(2,1)}), bf16[128,128]{1,0:T(8,128)(2,1)}) %reduce-scatter.5.cloned.1.call-update) | async-done | bytes 32784 | tf_op jit(solution)/shard_map/reduce_scatter | solution.py:138
  366.7 10.4 %all-to-all-start.1 = ((bf16[8,16,128]{2,1,0:T(8,128)(2,1)}), bf16[8,16,128]{2,1,0:T(8,128)(2,1)S(1)}, u32[]{:S(2)}, u32[]{:S(2)}) async-start(bf16[8,16,128]{2,1,0:T(8,128)(2,1)} %bitcast.634), calls=%async_computation.3 | async-start | bytes 65536 | tf_op jit(solution)/shard_map/all_to_all | solution.py:146
  377.1 27.6 %reduce-scatter.3.cloned.1.call-done = bf16[128,128]{1,0:T(8,128)(2,1)} async-done(((bf16[1024,128]{1,0:T(8,128)(2,1)}), bf16[128,128]{1,0:T(8,128)(2,1)}) %reduce-scatter.3.cloned.1.call-update) | async-done | bytes 32784 | tf_op jit(solution)/shard_map/reduce_scatter | solution.py:135
  404.7 10.4 %all-to-all-start = ((bf16[8,16,128]{2,1,0:T(8,128)(2,1)}), bf16[8,16,128]{2,1,0:T(8,128)(2,1)S(1)}, u32[]{:S(2)}, u32[]{:S(2)}) async-start(bf16[8,16,128]{2,1,0:T(8,128)(2,1)} %bitcast.633), calls=%async_computation.1 | async-start | bytes 65536 | tf_op jit(solution)/shard_map/all_to_all | solution.py:143
  415.8 4.1 all-to-all-done
  (70 shorter events, 17.4 us)
Async XLA Ops:
  7.2 2.4 copy-start
  7.2 85.0 %all-gather.5.cloned.1.call-start = ((), (), s32[]{:S(2)}) async-start(), calls=%async_computation.6 | async-start | bytes 2129920 | tf_op jit(solution)/shard_map/all_gather | solution.py:81
  7.9 162.0 %all-gather.7.cloned.1.call-start = ((), (), s32[]{:S(2)}) async-start(), calls=%async_computation.7 | async-start | bytes 2129920 | tf_op jit(solution)/shard_map/all_gather | solution.py:82
  8.7 358.0 %reduce-scatter.5.cloned.1.call-start = ((), (), s32[]{:S(2)}) async-start(), calls=%async_computation.5 | async-start | bytes 294912 | tf_op jit(solution)/shard_map/reduce_scatter | solution.py:138
  171.0 45.2 %copy-start.7 = (bf16[1024,1,128]{2,0,1:T(8,128)(2,1)}, bf16[1024,1,128]{2,0,1:T(8,128)(2,1)S(1)}, u32[]{:S(2)}) copy-start(bf16[1024,1,128]{2,0,1:T(8,128)(2,1)S(1)} %get-tuple-element.420) | copy-start | bytes 786436
  179.9 12.7 %collective-permute-start = (bf16[128,2048]{1,0:T(8,128)(2,1)S(1)}, bf16[128,2048]{1,0:T(8,128)(2,1)S(1)}, u32[]{:S(2)}, u32[]{:S(2)}) collective-permute-start(bf16[128,2048]{1,0:T(8,128)(2,1)S(1)} %copy.275), channel_id=1, source_target_pairs={{0,64},{64,128},{128,192},{1,65},{65,129},{129,193},{2,66},{66,130... | collective-permute-start | bytes 1572872 | tf_op jit(solution)/shard_map/ppermute | solution.py:17
  193.8 22.4 %copy-start.2 = (bf16[1,128,2048]{2,1,0:T(8,128)(2,1)S(1)}, bf16[1,128,2048]{2,1,0:T(8,128)(2,1)}, u32[]{:S(2)}) copy-start(bf16[1,128,2048]{2,1,0:T(8,128)(2,1)} %param.22) | copy-start | bytes 1572868
  195.1 21.0 %collective-permute-start.1 = (bf16[128,2048]{1,0:T(8,128)(2,1)S(1)}, bf16[128,2048]{1,0:T(8,128)(2,1)S(1)}, u32[]{:S(2)}, u32[]{:S(2)}) collective-permute-start(bf16[128,2048]{1,0:T(8,128)(2,1)S(1)} %copy.278), channel_id=1, source_target_pairs={{0,64},{64,128},{128,192},{1,65},{65,129},{129,193},{2,66},{66,130... | collective-permute-start | bytes 1572872 | tf_op jit(solution)/shard_map/ppermute | solution.py:17
  217.7 13.7 %collective-permute-start.2 = (bf16[128,2048]{1,0:T(8,128)(2,1)S(1)}, bf16[128,2048]{1,0:T(8,128)(2,1)S(1)}, u32[]{:S(2)}, u32[]{:S(2)}) collective-permute-start(bf16[128,2048]{1,0:T(8,128)(2,1)S(1)} %copy.281), channel_id=1, source_target_pairs={{0,64},{64,128},{128,192},{1,65},{65,129},{129,193},{2,66},{66,130... | collective-permute-start | bytes 1572872 | tf_op jit(solution)/shard_map/ppermute | solution.py:17
  231.6 2.5 copy-start.3
  234.9 19.0 %collective-permute-start.3 = (bf16[128,2048]{1,0:T(8,128)(2,1)S(1)}, bf16[128,2048]{1,0:T(8,128)(2,1)S(1)}, u32[]{:S(2)}, u32[]{:S(2)}) collective-permute-start(bf16[128,2048]{1,0:T(8,128)(2,1)S(1)} %copy.285), channel_id=1, source_target_pairs={{64,0},{128,64},{192,128},{65,1},{129,65},{193,129},{66,2},{130,66... | collective-permute-start | bytes 1572872 | tf_op jit(solution)/shard_map/ppermute | solution.py:17
  254.5 13.5 %collective-permute-start.4 = (bf16[128,2048]{1,0:T(8,128)(2,1)S(1)}, bf16[128,2048]{1,0:T(8,128)(2,1)S(1)}, u32[]{:S(2)}, u32[]{:S(2)}) collective-permute-start(bf16[128,2048]{1,0:T(8,128)(2,1)S(1)} %copy.287), channel_id=1, source_target_pairs={{64,0},{128,64},{192,128},{65,1},{129,65},{193,129},{66,2},{130,66... | collective-permute-start | bytes 1572872 | tf_op jit(solution)/shard_map/ppermute | solution.py:17
  268.5 54.6 %collective-permute-start.5 = (bf16[128,2048]{1,0:T(8,128)(2,1)S(1)}, bf16[128,2048]{1,0:T(8,128)(2,1)S(1)}, u32[]{:S(2)}, u32[]{:S(2)}) collective-permute-start(bf16[128,2048]{1,0:T(8,128)(2,1)S(1)} %copy.289), channel_id=1, source_target_pairs={{64,0},{128,64},{192,128},{65,1},{129,65},{193,129},{66,2},{130,66... | collective-permute-start | bytes 1572872 | tf_op jit(solution)/shard_map/ppermute | solution.py:17
  328.8 2.2 copy-start.12
  336.2 0.7 copy-start.4
  336.2 0.8 copy-start.5
  336.2 84.3 %copy-start.6 = (bf16[1,128,2048]{2,1,0:T(8,128)(2,1)}, bf16[1,128,2048]{2,1,0:T(8,128)(2,1)S(1)}, u32[]{:S(2)}) copy-start(bf16[1,128,2048]{2,1,0:T(8,128)(2,1)S(1)} %get-tuple-element.401) | copy-start | bytes 1572868
  336.2 84.3 %copy-start.1 = (s32[1024]{0:T(1024)S(1)}, s32[1024]{0:T(1024)}, u32[]{:S(2)}) copy-start(s32[1024]{0:T(1024)} %param.25) | copy-start | bytes 12292
  336.9 67.8 %reduce-scatter.3.cloned.1.call-start = ((), (), s32[]{:S(2)}) async-start(), calls=%async_computation.4 | async-start | bytes 294912 | tf_op jit(solution)/shard_map/reduce_scatter | solution.py:135
  366.7 38.0 %all-to-all-start.1 = ((bf16[8,16,128]{2,1,0:T(8,128)(2,1)}), bf16[8,16,128]{2,1,0:T(8,128)(2,1)S(1)}, u32[]{:S(2)}, u32[]{:S(2)}) async-start(bf16[8,16,128]{2,1,0:T(8,128)(2,1)} %bitcast.634), calls=%async_computation.3 | async-start | bytes 65536 | tf_op jit(solution)/shard_map/all_to_all | solution.py:146
  404.7 15.2 %all-to-all-start = ((bf16[8,16,128]{2,1,0:T(8,128)(2,1)}), bf16[8,16,128]{2,1,0:T(8,128)(2,1)S(1)}, u32[]{:S(2)}, u32[]{:S(2)}) async-start(bf16[8,16,128]{2,1,0:T(8,128)(2,1)} %bitcast.633), calls=%async_computation.1 | async-start | bytes 65536 | tf_op jit(solution)/shard_map/all_to_all | solution.py:143
Sparse Core Ops, SparseCore 0:
  10.8 81.3 all-gather.4
  95.0 74.9 all-gather.6
  337.0 29.6 reduce-scatter.4
  369.2 35.4 reduce-scatter.2
where the time goes:
time: 436 us; the launch traced here: 427 us
  waiting for transfers between devices  333 us (76%)
  starting transfers between devices  40.9 us (9%)
  local copies, waits for them, and re-layouts  16.3 us (4%)
  between operations  14.6 us (3%)
  matrix products  14.4 us (3%)
  other arithmetic  7.24 us (2%)
    ppermute x6, waiting for transfers between devices, shifted(): return lax.ppermute(block, axis, route)  115 us
    all_gather x1, waiting for transfers between devices, shards(): lax.all_gather(value_in[0], ('ctx', 'tp'), axis=0, tiled=True)  77.7 us
    all_gather x1, waiting for transfers between devices, shards(): lax.all_gather(key_in[0], ('ctx', 'tp'), axis=0, tiled=True)  77.6 us
    reduce_scatter x1, waiting for transfers between devices, shards(): lax.psum_scatter(value_terms.astype(jnp.bfloat16), 'ctx', scatter_dimensi...  29.2 us
    reduce_scatter x1, waiting for transfers between devices, shards(): lax.psum_scatter(key_terms.astype(jnp.bfloat16), 'ctx', scatter_dimension...  27.6 us
    ppermute x6, starting transfers between devices, shifted(): return lax.ppermute(block, axis, route)  19.9 us
    all_to_all x1, starting transfers between devices, shards(): lax.all_to_all(key_part.astype(jnp.bfloat16), 'tp', split_axis=0, concat_...  10.4 us
    all_to_all x1, starting transfers between devices, shards(): lax.all_to_all(value_part.astype(jnp.bfloat16), 'tp', split_axis=0, conca...  10.4 us
  transfers between devices with their start and end apart: 12, of which 11 were waited for; matrix products, arithmetic and copies ran while one was open for 2% of the time, Pallas kernels for 0%

commit v1 on v0

v1 whole, which is shorter than its diff:
```python
import functools
import math

import jax
import jax.numpy as jnp
from jax import lax
from jax.experimental import pallas as pl
from jax.experimental.pallas import tpu as pltpu
from jax.sharding import PartitionSpec as P

HEAD_DIM = 128
BLOCK = 128
REACH = 4
SPAN = (REACH + 1) * BLOCK
SCALE = HEAD_DIM ** (-0.5)
EXP2_SCALE = SCALE * math.log2(math.e)

masked_score = -1e30


def nt(a, b):
    return lax.dot_general(a, b, (((1,), (1,)), ((), ())), preferred_element_type=jnp.float32)


def nn(a, b):
    return lax.dot_general(a, b, (((1,), (0,)), ((), ())), preferred_element_type=jnp.float32)


def layers_kernel(
    place, query, cot, bias,
    k_own, k_next, k_far_a, k_far_b, k_prev, v_own, v_next, v_far_a, v_far_b, v_prev,
    out, grad_query, grad_kv,
    keys, values, expo, queries, scale_rows, gs_all, ds_all,
):
    layers, rows, width = query.shape
    heads = width // HEAD_DIM
    bf16, f32 = jnp.bfloat16, jnp.float32
    me = place[0]
    half = SPAN // 2
    for store, own, after, far_a, far_b, before in (
        (keys, k_own, k_next, k_far_a, k_far_b, k_prev),
        (values, v_own, v_next, v_far_a, v_far_b, v_prev),
    ):
        store[me] = own[...]
        store[(me + 1) % layers] = after[...]
        store[(me + 2) % layers, :half] = far_a[...]
        store[(me + 2) % layers, half:] = far_b[...]
        store[(me + 3) % layers] = before[...]

    def cols(h):
        return slice(h * HEAD_DIM, (h + 1) * HEAD_DIM)

    def span(h):
        return slice(h * rows, (h + 1) * rows)

    for l in range(layers):
        for h in range(heads):
            q = query[l, :, cols(h)]
            if l > 0:
                q = (q.astype(f32) + out[l - 1, :, cols(h)].astype(f32)).astype(bf16)
            queries[l, span(h)] = q
            t = nt(q, keys[l]) * EXP2_SCALE + bias[...]
            e = jnp.exp2(t - jnp.max(t, axis=-1, keepdims=True))
            r = 1.0 / jnp.sum(e, axis=-1, keepdims=True)
            e = e.astype(bf16)
            expo[l, span(h)] = e
            scale_rows[l, span(h)] = jnp.broadcast_to(r, (rows, HEAD_DIM))
            out[l, :, cols(h)] = (nn(e, values[l]) * r).astype(bf16)

    for l in reversed(range(layers)):
        for h in range(heads):
            g = cot[l, :, cols(h)]
            if l < layers - 1:
                g = (g.astype(f32) + grad_query[l + 1, :, cols(h)].astype(f32)).astype(bf16)
            gs = (g.astype(f32) * scale_rows[l, span(h)]).astype(bf16)
            gs_all[span(h)] = gs
            delta = jnp.sum(
                gs.astype(f32) * out[l, :, cols(h)].astype(f32), axis=-1, keepdims=True
            )
            ds = (expo[l, span(h)].astype(f32) * (nt(gs, values[l]) - delta)).astype(bf16)
            ds_all[span(h)] = ds
            grad_query[l, :, cols(h)] = (nn(ds, keys[l]) * SCALE).astype(bf16)
        gk = nn(queries[l].T, ds_all[...]) * SCALE
        gv = nn(gs_all[...].T, expo[l])
        grad_kv[l, :SPAN] = gk.T.astype(bf16)
        grad_kv[l, SPAN:] = gv.T.astype(bf16)


def run_layers(place, query, cot, bias, k_parts, v_parts):
    layers, rows, width = query.shape
    stacked = rows * width // HEAD_DIM
    bf16, f32 = jnp.bfloat16, jnp.float32
    vmem = pl.BlockSpec(memory_space=pltpu.VMEM)
    return pl.pallas_call(
        layers_kernel,
        out_shape=(
            jax.ShapeDtypeStruct((layers, rows, width), bf16),
            jax.ShapeDtypeStruct((layers, rows, width), bf16),
            jax.ShapeDtypeStruct((layers, 2 * SPAN, HEAD_DIM), bf16),
        ),
        in_specs=[pl.BlockSpec(memory_space=pltpu.SMEM)] + [vmem] * 13,
        out_specs=(vmem, vmem, vmem),
        scratch_shapes=[
            pltpu.VMEM((layers, SPAN, HEAD_DIM), bf16),
            pltpu.VMEM((layers, SPAN, HEAD_DIM), bf16),
            pltpu.VMEM((layers, stacked, SPAN), bf16),
            pltpu.VMEM((layers, stacked, HEAD_DIM), bf16),
            pltpu.VMEM((layers, stacked, HEAD_DIM), f32),
            pltpu.VMEM((stacked, HEAD_DIM), bf16),
            pltpu.VMEM((stacked, SPAN), bf16),
        ],
        compiler_params=pltpu.CompilerParams(vmem_limit_bytes=48 * 1024 * 1024),
        name="layers",
    )(place, query, cot, bias, *k_parts, *v_parts)


def moved(block, distance):
    size = lax.axis_size("pipe")
    return lax.ppermute(block, "pipe", [(i, (i + distance) % size) for i in range(size)])


def shards(query_in, key_in, value_in, doc_ids, stretch_order, out_cot):
    bf16, f32 = jnp.bfloat16, jnp.float32
    tp_count = lax.axis_size("tp")
    ctx_count = lax.axis_size("ctx")
    layers = lax.axis_size("pipe")
    layer = lax.axis_index("pipe")
    rows = query_in.shape[1]
    width = query_in.shape[2]
    part = width // layers
    kv_rows = key_in.shape[1]

    def spread(block):
        heads = block.reshape(kv_rows, tp_count, HEAD_DIM).transpose(1, 0, 2)
        sent = jnp.broadcast_to(heads[None], (ctx_count,) + heads.shape)
        sent = sent.reshape(ctx_count * tp_count, kv_rows, HEAD_DIM)
        got = lax.all_to_all(sent, ("ctx", "tp"), split_axis=0, concat_axis=0, tiled=True)
        return got.reshape(ctx_count, BLOCK, HEAD_DIM)

    keys_all = spread(key_in[0])
    values_all = spread(value_in[0])

    position = stretch_order[lax.axis_index("ctx")]
    block_ids = jnp.arange(ctx_count, dtype=jnp.int32)
    holder = jnp.sum(
        jnp.where(stretch_order[None, :] == block_ids[:, None], block_ids[None, :], 0), axis=1
    )

    def window(blocks):
        return jnp.concatenate(
            [
                lax.dynamic_index_in_dim(
                    blocks, holder[jnp.maximum(position - REACH + j, 0)], 0, keepdims=False
                )
                for j in range(REACH + 1)
            ]
        )

    def gathered(own):
        half = SPAN // 2
        before = moved(own, 1)
        after = moved(own, -1)
        far_a = moved(before[:half], 1)
        far_b = moved(after[half:], -1)
        return (own, after, far_a, far_b, before)

    k_parts = gathered(window(keys_all))
    v_parts = gathered(window(values_all))

    offsets = jnp.arange(SPAN, dtype=jnp.int32)
    row_ids = jnp.arange(rows, dtype=jnp.int32)
    documents = jnp.concatenate([jnp.full((REACH * BLOCK,), -1, jnp.int32), doc_ids])
    near_documents = lax.dynamic_slice_in_dim(documents, position * BLOCK, SPAN)
    own_documents = near_documents[REACH * BLOCK:]
    allowed = (offsets[None, :] <= row_ids[:, None] + REACH * BLOCK) & (
        near_documents[None, :] == own_documents[:, None]
    )
    bias = jnp.where(allowed, 0.0, masked_score).astype(f32)

    def to_layers(block):
        return lax.all_to_all(
            block.reshape(rows, layers, part).transpose(1, 0, 2), "pipe", 0, 0, tiled=True
        )

    def to_owner(blocks):
        got = lax.all_to_all(blocks, "pipe", 0, 0, tiled=True)
        return got.transpose(1, 0, 2).reshape(1, rows, width)

    query = to_layers(query_in[0])
    cot = to_layers(out_cot[0])
    out, grad_query, grad_kv = run_layers(
        layer.reshape(1), query, cot, bias, k_parts, v_parts
    )

    def part_of(distance):
        return lax.dynamic_index_in_dim(grad_kv, (layer + distance) % layers, 0, keepdims=False)

    own, after, far, before = (part_of(d) for d in range(4))
    half = SPAN
    from_before = moved(far[:half], 1)
    from_after = moved(far[half:], -1)

    def add(a, b):
        return (a.astype(f32) + b.astype(f32)).astype(bf16)

    up = jnp.concatenate([add(after[:half], from_before), after[half:]])
    down = jnp.concatenate([before[:half], add(before[half:], from_after)])
    total = own.astype(f32) + moved(up, 1).astype(f32) + moved(down, -1).astype(f32)
    total = total.astype(bf16).reshape(2, REACH + 1, BLOCK, HEAD_DIM)

    def placed(b):
        j = stretch_order[b] - (position - REACH)
        block = lax.dynamic_index_in_dim(total, jnp.clip(j, 0, REACH), 1, keepdims=False)
        return jnp.where((j >= 0) & (j <= REACH), block, jnp.zeros_like(block))

    sent = jnp.stack([placed(b) for b in range(ctx_count)])
    sent = sent.reshape(ctx_count, 2, tp_count, kv_rows, HEAD_DIM).transpose(0, 2, 1, 3, 4)
    sent = sent.reshape(ctx_count * tp_count, 2 * kv_rows, HEAD_DIM)
    got = lax.all_to_all(sent, ("ctx", "tp"), split_axis=0, concat_axis=0, tiled=True)
    got = got.reshape(ctx_count, tp_count, 2, kv_rows, HEAD_DIM)
    grads = jnp.sum(got.astype(f32), axis=0).astype(bf16)
    grads = grads.transpose(1, 2, 0, 3).reshape(2, 1, kv_rows, tp_count * HEAD_DIM)
    return (to_owner(out), to_owner(grad_query), grads[0], grads[1])


def solution(mesh):
    return jax.shard_map(
        shards,
        mesh=mesh,
        in_specs=(
            P("pipe", "ctx", "tp"),
            P("pipe", ("ctx", "tp"), None),
            P("pipe", ("ctx", "tp"), None),
            P(),
            P(),
            P("pipe", "ctx", "tp"),
        ),
        out_specs=(
            P("pipe", "ctx", "tp"),
            P("pipe", "ctx", "tp"),
            P("pipe", ("ctx", "tp"), None),
            P("pipe", ("ctx", "tp"), None),
        ),
        check_vma=False,
    )
```

time: 436 us -> 167 us (0.38); the launches traced: 427 us -> 166 us
  waiting for transfers between devices: 333 us -> 51.5 us
  starting transfers between devices: 40.9 us -> 65.6 us
  matrix products: 14.4 us -> 0 us
  Pallas kernels: 0 us -> 9.77 us
  other arithmetic: 7.24 us -> 0.64 us
  between operations: 14.6 us -> 19.3 us
    all_gather x2 -> x0, waiting for transfers between devices: 155 us -> none  [the longest x1 77.7 us: shards(): lax.all_gather(value_in[0], ('ctx', 'tp'), axis=0, tiled=True)]
    ppermute x6 -> x12, waiting for transfers between devices: 115 us -> 7.34 us  [moved(): lax.ppermute(block, 'pipe', [(i, (i + distance) % size) for i in range(si...]
    reduce_scatter x2 -> x0, waiting for transfers between devices: 56.8 us -> none  [the longest x1 29.2 us: shards(): lax.psum_scatter(value_terms.astype(jnp.bfloat16), 'ctx', scatter_dimensi...]
    all_to_all x2 -> x7, waiting for transfers between devices: 4.08 us -> 44.2 us  [the longest x1 15.1 us: shards(): lax.all_to_all(sent, ('ctx', 'tp'), split_axis=0, concat_axis=0, tiled=True)]
    all_to_all x2 -> x7, starting transfers between devices: 20.9 us -> 49 us  [the longest x2 17.8 us: spread(): lax.all_to_all(sent, ('ctx', 'tp'), split_axis=0, concat_axis=0, tiled=True)]
    dot_general x7 -> x0, matrix products: 14.4 us -> none  [the longest x2 3.95 us: block_probs(): jnp.einsum('qngd,knd->ngqk', query4, keys3, preferred_element_type=jnp.fl...]
    unnamed x16 -> x49, local copies, waits for them, and re-layouts: 0.72 us -> 11.4 us
    pallas_call x0 -> x1, Pallas kernels: none -> 9.77 us  [run_layers(): pl.pallas_call(layers_kernel, out_shape=(jax.ShapeDtypeStruct((layers, ro...]
  transfers between devices with their start and end apart: 12 -> 19, of which waited for: 11 -> 11; matrix products, arithmetic and copies ran while one was open for 2% -> 5% of each run, Pallas kernels for 0% -> 0%
where the time goes in v1:
time: 167 us; the launch traced here: 166 us
  starting transfers between devices  65.6 us (39%)
  waiting for transfers between devices  51.5 us (31%)
  between operations  19.3 us (12%)
  local copies, waits for them, and re-layouts  19 us (11%)
  Pallas kernels  9.77 us (6%)
    all_to_all x2, starting transfers between devices, spread(): lax.all_to_all(sent, ('ctx', 'tp'), split_axis=0, concat_axis=0, tiled=True)  17.8 us
    ppermute x12, starting transfers between devices, moved(): lax.ppermute(block, 'pipe', [(i, (i + distance) % size) for i in range(si...  16.6 us
    all_to_all x1, starting transfers between devices, shards(): lax.all_to_all(sent, ('ctx', 'tp'), split_axis=0, concat_axis=0, tiled=True)  16.5 us
    all_to_all x1, waiting for transfers between devices, shards(): lax.all_to_all(sent, ('ctx', 'tp'), split_axis=0, concat_axis=0, tiled=True)  15.1 us
    all_to_all x2, waiting for transfers between devices, to_owner(): got = lax.all_to_all(blocks, 'pipe', 0, 0, tiled=True)  12.6 us
    all_to_all x2, waiting for transfers between devices, spread(): lax.all_to_all(sent, ('ctx', 'tp'), split_axis=0, concat_axis=0, tiled=True)  12.4 us
    unnamed x49, local copies, waits for them, and re-layouts  11.4 us
    pallas_call x1, Pallas kernels, run_layers(): pl.pallas_call(layers_kernel, out_shape=(jax.ShapeDtypeStruct((layers, ro...  9.77 us
  transfers between devices with their start and end apart: 19, of which 11 were waited for; matrix products, arithmetic and copies ran while one was open for 5% of the time, Pallas kernels for 0%

profile of v1, /device:TPU:1, one launch (start us, length us, event | category | flops | bytes accessed | tf_op | source)
XLA Modules:
  0.0 165.9 jit_solution(17856441328850050321)
XLA Ops:
  2.2 13.0 %all-to-all-start.3 = ((bf16[64,16,128]{2,1,0:T(8,128)(2,1)}), bf16[64,16,128]{2,1,0:T(8,128)(2,1)S(1)}, u32[]{:S(2)}, u32[]{:S(2)}) async-start(bf16[64,16,128]{2,1,0:T(8,128)(2,1)} %bitcast.25), calls=%async_computation.3 | async-start | bytes 524288 | tf_op jit(solution)/shard_map/all_to_all | solution.py:137
  16.0 12.4 %all-to-all-done.3 = bf16[64,16,128]{2,1,0:T(8,128)(2,1)S(1)} async-done(((bf16[64,16,128]{2,1,0:T(8,128)(2,1)}), bf16[64,16,128]{2,1,0:T(8,128)(2,1)S(1)}, u32[]{:S(2)}, u32[]{:S(2)}) %all-to-all-start.3) | async-done | bytes 262176 | tf_op jit(solution)/shard_map/all_to_all | solution.py:137
  29.1 4.8 %all-to-all-start.2 = ((bf16[64,16,128]{2,1,0:T(8,128)(2,1)}), bf16[64,16,128]{2,1,0:T(8,128)(2,1)S(1)}, u32[]{:S(2)}, u32[]{:S(2)}) async-start(bf16[64,16,128]{2,1,0:T(8,128)(2,1)} %bitcast.7), calls=%async_computation.2 | async-start | bytes 524288 | tf_op jit(solution)/shard_map/all_to_all | solution.py:137
  45.7 1.0 copy.82
  47.0 1.0 copy.84
  51.1 4.2 %all-to-all-start = ((bf16[4,128,512]{2,1,0:T(8,128)(2,1)}), bf16[4,128,512]{2,1,0:T(8,128)(2,1)S(1)}, u32[]{:S(2)}, u32[]{:S(2)}) async-start(bf16[4,128,512]{2,1,0:T(8,128)(2,1)} %bitcast.2), calls=%async_computation | async-start | bytes 1048576 | tf_op jit(solution)/shard_map/all_to_all | solution.py:181
  55.4 1.5 collective-permute-start.1
  57.0 1.3 collective-permute-start
  58.6 2.5 %collective-permute-start.4 = (bf16[640,128]{1,0:T(8,128)(2,1)S(1)}, bf16[640,128]{1,0:T(8,128)(2,1)S(1)}, u32[]{:S(2)}, u32[]{:S(2)}) collective-permute-start(bf16[640,128]{1,0:T(8,128)(2,1)S(1)} %constant_dynamic-update-slice_fusion.5.v_own), channel_id=1, source_target_pairs={{0,192},{64,0},{128,64},{192,128},{1,193},{65,1},{129,65},{193,129... | collective-permute-start | bytes 491528 | tf_op jit(solution)/shard_map/ppermute | solution.py:119
  61.1 3.1 %all-to-all-done.query = bf16[4,128,512]{2,1,0:T(8,128)(2,1)S(1)} async-done(((bf16[4,128,512]{2,1,0:T(8,128)(2,1)}), bf16[4,128,512]{2,1,0:T(8,128)(2,1)S(1)}, u32[]{:S(2)}, u32[]{:S(2)}) %all-to-all-start) | async-done | bytes 524320 | tf_op jit(solution)/shard_map/all_to_all | solution.py:181
  64.1 3.5 %all-to-all-start.1 = ((bf16[4,128,512]{2,1,0:T(8,128)(2,1)}), bf16[4,128,512]{2,1,0:T(8,128)(2,1)S(1)}, u32[]{:S(2)}, u32[]{:S(2)}) async-start(bf16[4,128,512]{2,1,0:T(8,128)(2,1)} %bitcast.4), calls=%async_computation.1 | async-start | bytes 1048576 | tf_op jit(solution)/shard_map/all_to_all | solution.py:181
  67.7 1.5 collective-permute-start.2
  69.2 1.3 collective-permute-start.3
  70.9 2.9 %collective-permute-start.7 = (bf16[320,128]{1,0:T(8,128)(2,1)S(1)}, bf16[320,128]{1,0:T(8,128)(2,1)S(1)}, u32[]{:S(2)}, u32[]{:S(2)}) collective-permute-start(bf16[320,128]{1,0:T(8,128)(2,1)S(1)} %slice.107), channel_id=1, source_target_pairs={{0,192},{64,0},{128,64},{192,128},{1,193},{65,1},{129,65},{193,129... | collective-permute-start | bytes 245768 | tf_op jit(solution)/shard_map/ppermute | solution.py:119
  74.0 1.0 all-to-all-done.1.cot
  75.0 1.2 collective-permute-done.2.k_far_a
  79.2 0.9 copy-done.1
  80.1 0.9 copy-done.3
  81.0 0.9 copy-done.5
  83.7 9.8 %layers.1 = (bf16[4,128,512]{2,1,0:T(8,128)(2,1)}, bf16[4,128,512]{2,1,0:T(8,128)(2,1)}, bf16[4,1280,128]{2,1,0:T(8,128)(2,1)S(1)}) custom-call(s32[1]{0:T(128)} %bitcast.place, bf16[4,128,512]{2,1,0:T(8,128)(2,1)S(1)} %all-to-all-done.query, bf16[4,128,512]{2,1,0:T(8,128)(2,1)S(1)} %all-to-all-done.1.cot, f32[128,640]{1,0:T(8,128)S(1)} %fusion.5.bias, ...), custom_call_target="tpu_custom_call" | custom-call | tf_op jit(solution)/shard_map/layers/pallas_call | solution.py:94
  93.5 2.5 %collective-permute-start.10 = (bf16[640,128]{1,0:T(8,128)(2,1)S(1)}, bf16[640,128]{1,0:T(8,128)(2,1)S(1)}, u32[]{:S(2)}, u32[]{:S(2)}) collective-permute-start(bf16[640,128]{1,0:T(8,128)(2,1)S(1)} %get-tuple-element.34), channel_id=1, source_target_pairs={{0,192},{64,0},{128,64},{192,128},{1,193},{65,1},{129,65},{193,129... | collective-permute-start | bytes 491528 | tf_op jit(solution)/shard_map/ppermute | solution.py:119
  96.0 2.3 %collective-permute-done.10 = bf16[640,128]{1,0:T(8,128)(2,1)S(1)} collective-permute-done((bf16[640,128]{1,0:T(8,128)(2,1)S(1)}, bf16[640,128]{1,0:T(8,128)(2,1)S(1)}, u32[]{:S(2)}, u32[]{:S(2)}) %collective-permute-start.10) | collective-permute-done | bytes 163872 | tf_op jit(solution)/shard_map/ppermute | solution.py:119
  98.3 3.1 %collective-permute-done.8 = bf16[640,128]{1,0:T(8,128)(2,1)S(1)} collective-permute-done((bf16[640,128]{1,0:T(8,128)(2,1)S(1)}, bf16[640,128]{1,0:T(8,128)(2,1)S(1)}, u32[]{:S(2)}, u32[]{:S(2)}) %collective-permute-start.8) | collective-permute-done | bytes 163872 | tf_op jit(solution)/shard_map/ppermute | solution.py:119
  101.6 2.7 %collective-permute-start.11 = (bf16[1280,128]{1,0:T(8,128)(2,1)S(1)}, bf16[1280,128]{1,0:T(8,128)(2,1)S(1)}, u32[]{:S(2)}, u32[]{:S(2)}) collective-permute-start(bf16[1280,128]{1,0:T(8,128)(2,1)S(1)} %pad_maximum_fusion.1), channel_id=1, source_target_pairs={{0,192},{64,0},{128,64},{192,128},{1,193},{65,1},{129,65},{193,129... | collective-permute-start | bytes 983048 | tf_op jit(solution)/shard_map/ppermute | solution.py:119
  109.5 3.5 %all-to-all-start.4 = ((bf16[4,128,512]{2,1,0:T(8,128)(2,1)}), bf16[4,128,512]{2,1,0:T(8,128)(2,1)S(1)}, u32[]{:S(2)}, u32[]{:S(2)}) async-start(bf16[4,128,512]{2,1,0:T(8,128)(2,1)} %get-tuple-element.7), calls=%async_computation.4 | async-start | bytes 1048576 | tf_op jit(solution)/shard_map/all_to_all | solution.py:186
  113.3 6.6 %all-to-all-done.4 = bf16[4,128,512]{2,1,0:T(8,128)(2,1)S(1)} async-done(((bf16[4,128,512]{2,1,0:T(8,128)(2,1)}), bf16[4,128,512]{2,1,0:T(8,128)(2,1)S(1)}, u32[]{:S(2)}, u32[]{:S(2)}) %all-to-all-start.4) | async-done | bytes 524320 | tf_op jit(solution)/shard_map/all_to_all | solution.py:186
  119.9 3.5 %all-to-all-start.5 = ((bf16[4,128,512]{2,1,0:T(8,128)(2,1)}), bf16[4,128,512]{2,1,0:T(8,128)(2,1)S(1)}, u32[]{:S(2)}, u32[]{:S(2)}) async-start(bf16[4,128,512]{2,1,0:T(8,128)(2,1)} %get-tuple-element.8), calls=%async_computation.5 | async-start | bytes 1048576 | tf_op jit(solution)/shard_map/all_to_all | solution.py:186
  124.3 6.0 %all-to-all-done.5 = bf16[4,128,512]{2,1,0:T(8,128)(2,1)S(1)} async-done(((bf16[4,128,512]{2,1,0:T(8,128)(2,1)}), bf16[4,128,512]{2,1,0:T(8,128)(2,1)S(1)}, u32[]{:S(2)}, u32[]{:S(2)}) %all-to-all-start.5) | async-done | bytes 524320 | tf_op jit(solution)/shard_map/all_to_all | solution.py:186
  130.3 16.5 %all-to-all-start.6 = ((bf16[64,32,128]{2,1,0:T(8,128)(2,1)}), bf16[64,32,128]{2,1,0:T(8,128)(2,1)S(1)}, u32[]{:S(2)}, u32[]{:S(2)}) async-start(bf16[64,32,128]{2,1,0:T(8,128)(2,1)} %bitcast.69), calls=%async_computation.6 | async-start | bytes 1048576 | tf_op jit(solution)/shard_map/all_to_all | solution.py:219
  147.1 1.0 copy.100
  148.4 1.0 copy.101
  149.4 15.1 %all-to-all-done.6 = bf16[64,32,128]{2,1,0:T(8,128)(2,1)S(1)} async-done(((bf16[64,32,128]{2,1,0:T(8,128)(2,1)}), bf16[64,32,128]{2,1,0:T(8,128)(2,1)S(1)}, u32[]{:S(2)}, u32[]{:S(2)}) %all-to-all-start.6) | async-done | bytes 524320 | tf_op jit(solution)/shard_map/all_to_all | solution.py:219
  (88 shorter events, 14.0 us)
Async XLA Ops:
  0.6 33.3 %copy-start.12 = (s32[8]{0:T(128)S(1)}, s32[8]{0:T(128)}, u32[]{:S(2)}) copy-start(s32[8]{0:T(128)} %param.10) | copy-start | bytes 100
  0.6 44.8 %copy-start.10 = (bf16[1,128,2048]{2,1,0:T(8,128)(2,1)S(1)}, bf16[1,128,2048]{2,1,0:T(8,128)(2,1)}, u32[]{:S(2)}) copy-start(bf16[1,128,2048]{2,1,0:T(8,128)(2,1)} %param.6) | copy-start | bytes 1572868
  2.2 26.2 %all-to-all-start.3 = ((bf16[64,16,128]{2,1,0:T(8,128)(2,1)}), bf16[64,16,128]{2,1,0:T(8,128)(2,1)S(1)}, u32[]{:S(2)}, u32[]{:S(2)}) async-start(bf16[64,16,128]{2,1,0:T(8,128)(2,1)} %bitcast.25), calls=%async_computation.3 | async-start | bytes 524288 | tf_op jit(solution)/shard_map/all_to_all | solution.py:137
  29.1 17.6 %copy-start.11 = (bf16[1,128,2048]{2,1,0:T(8,128)(2,1)S(1)}, bf16[1,128,2048]{2,1,0:T(8,128)(2,1)}, u32[]{:S(2)}) copy-start(bf16[1,128,2048]{2,1,0:T(8,128)(2,1)} %param.11) | copy-start | bytes 1572868
  29.1 22.0 %all-to-all-start.2 = ((bf16[64,16,128]{2,1,0:T(8,128)(2,1)}), bf16[64,16,128]{2,1,0:T(8,128)(2,1)S(1)}, u32[]{:S(2)}, u32[]{:S(2)}) async-start(bf16[64,16,128]{2,1,0:T(8,128)(2,1)} %bitcast.7), calls=%async_computation.2 | async-start | bytes 524288 | tf_op jit(solution)/shard_map/all_to_all | solution.py:137
  51.1 16.5 %copy-start.13 = (s32[1024]{0:T(1024)S(1)}, s32[1024]{0:T(1024)}, u32[]{:S(2)}) copy-start(s32[1024]{0:T(1024)} %param.9) | copy-start | bytes 12292
  51.1 13.0 %all-to-all-start = ((bf16[4,128,512]{2,1,0:T(8,128)(2,1)}), bf16[4,128,512]{2,1,0:T(8,128)(2,1)S(1)}, u32[]{:S(2)}, u32[]{:S(2)}) async-start(bf16[4,128,512]{2,1,0:T(8,128)(2,1)} %bitcast.2), calls=%async_computation | async-start | bytes 1048576 | tf_op jit(solution)/shard_map/all_to_all | solution.py:181
  55.4 23.2 %copy-start = (bf16[640,128]{1,0:T(8,128)(2,1)}, bf16[640,128]{1,0:T(8,128)(2,1)S(1)}, u32[]{:S(2)}) copy-start(bf16[640,128]{1,0:T(8,128)(2,1)S(1)} %constant_dynamic-update-slice_fusion.k_own) | copy-start | bytes 491524
  55.4 12.3 %collective-permute-start.1 = (bf16[640,128]{1,0:T(8,128)(2,1)S(1)}, bf16[640,128]{1,0:T(8,128)(2,1)S(1)}, u32[]{:S(2)}, u32[]{:S(2)}) collective-permute-start(bf16[640,128]{1,0:T(8,128)(2,1)S(1)} %constant_dynamic-update-slice_fusion.k_own), channel_id=1, source_target_pairs={{0,64},{64,128},{128,192},{192,0},{1,65},{65,129},{129,193},{193,1... | collective-permute-start | bytes 491528 | tf_op jit(solution)/shard_map/ppermute | solution.py:119
  57.0 12.3 %collective-permute-start = (bf16[640,128]{1,0:T(8,128)(2,1)S(1)}, bf16[640,128]{1,0:T(8,128)(2,1)S(1)}, u32[]{:S(2)}, u32[]{:S(2)}) collective-permute-start(bf16[640,128]{1,0:T(8,128)(2,1)S(1)} %constant_dynamic-update-slice_fusion.k_own), channel_id=1, source_target_pairs={{0,192},{64,0},{128,64},{192,128},{1,193},{65,1},{129,65},{193,129... | collective-permute-start | bytes 491528 | tf_op jit(solution)/shard_map/ppermute | solution.py:119
  58.3 12.5 %collective-permute-start.5 = (bf16[640,128]{1,0:T(8,128)(2,1)S(1)}, bf16[640,128]{1,0:T(8,128)(2,1)S(1)}, u32[]{:S(2)}, u32[]{:S(2)}) collective-permute-start(bf16[640,128]{1,0:T(8,128)(2,1)S(1)} %constant_dynamic-update-slice_fusion.5.v_own), channel_id=1, source_target_pairs={{0,64},{64,128},{128,192},{192,0},{1,65},{65,129},{129,193},{193,1... | collective-permute-start | bytes 491528 | tf_op jit(solution)/shard_map/ppermute | solution.py:119
  58.6 12.3 %collective-permute-start.4 = (bf16[640,128]{1,0:T(8,128)(2,1)S(1)}, bf16[640,128]{1,0:T(8,128)(2,1)S(1)}, u32[]{:S(2)}, u32[]{:S(2)}) collective-permute-start(bf16[640,128]{1,0:T(8,128)(2,1)S(1)} %constant_dynamic-update-slice_fusion.5.v_own), channel_id=1, source_target_pairs={{0,192},{64,0},{128,64},{192,128},{1,193},{65,1},{129,65},{193,129... | collective-permute-start | bytes 491528 | tf_op jit(solution)/shard_map/ppermute | solution.py:119
  64.1 10.9 %all-to-all-start.1 = ((bf16[4,128,512]{2,1,0:T(8,128)(2,1)}), bf16[4,128,512]{2,1,0:T(8,128)(2,1)S(1)}, u32[]{:S(2)}, u32[]{:S(2)}) async-start(bf16[4,128,512]{2,1,0:T(8,128)(2,1)} %bitcast.4), calls=%async_computation.1 | async-start | bytes 1048576 | tf_op jit(solution)/shard_map/all_to_all | solution.py:181
  67.7 8.5 %collective-permute-start.2 = (bf16[320,128]{1,0:T(8,128)(2,1)S(1)}, bf16[320,128]{1,0:T(8,128)(2,1)S(1)}, u32[]{:S(2)}, u32[]{:S(2)}) collective-permute-start(bf16[320,128]{1,0:T(8,128)(2,1)S(1)} %slice.104), channel_id=1, source_target_pairs={{0,64},{64,128},{128,192},{192,0},{1,65},{65,129},{129,193},{193,1... | collective-permute-start | bytes 245768 | tf_op jit(solution)/shard_map/ppermute | solution.py:119
  69.2 7.6 %collective-permute-start.3 = (bf16[320,128]{1,0:T(8,128)(2,1)S(1)}, bf16[320,128]{1,0:T(8,128)(2,1)S(1)}, u32[]{:S(2)}, u32[]{:S(2)}) collective-permute-start(bf16[320,128]{1,0:T(8,128)(2,1)S(1)} %slice.105), channel_id=1, source_target_pairs={{0,192},{64,0},{128,64},{192,128},{1,193},{65,1},{129,65},{193,129... | collective-permute-start | bytes 245768 | tf_op jit(solution)/shard_map/ppermute | solution.py:119
  70.9 7.1 %collective-permute-start.6 = (bf16[320,128]{1,0:T(8,128)(2,1)S(1)}, bf16[320,128]{1,0:T(8,128)(2,1)S(1)}, u32[]{:S(2)}, u32[]{:S(2)}) collective-permute-start(bf16[320,128]{1,0:T(8,128)(2,1)S(1)} %slice.106), channel_id=1, source_target_pairs={{0,64},{64,128},{128,192},{192,0},{1,65},{65,129},{129,193},{193,1... | collective-permute-start | bytes 245768 | tf_op jit(solution)/shard_map/ppermute | solution.py:119
  70.9 7.7 %collective-permute-start.7 = (bf16[320,128]{1,0:T(8,128)(2,1)S(1)}, bf16[320,128]{1,0:T(8,128)(2,1)S(1)}, u32[]{:S(2)}, u32[]{:S(2)}) collective-permute-start(bf16[320,128]{1,0:T(8,128)(2,1)S(1)} %slice.107), channel_id=1, source_target_pairs={{0,192},{64,0},{128,64},{192,128},{1,193},{65,1},{129,65},{193,129... | collective-permute-start | bytes 245768 | tf_op jit(solution)/shard_map/ppermute | solution.py:119
  76.2 0.6 copy-start.2
  76.8 0.6 copy-start.4
  78.6 0.6 copy-start.8
  79.2 0.9 copy-start.1
  80.1 0.9 copy-start.3
  81.0 0.9 copy-start.5
  81.9 0.9 copy-start.7
  82.8 0.9 copy-start.9
  93.5 4.7 %collective-permute-start.10 = (bf16[640,128]{1,0:T(8,128)(2,1)S(1)}, bf16[640,128]{1,0:T(8,128)(2,1)S(1)}, u32[]{:S(2)}, u32[]{:S(2)}) collective-permute-start(bf16[640,128]{1,0:T(8,128)(2,1)S(1)} %get-tuple-element.34), channel_id=1, source_target_pairs={{0,192},{64,0},{128,64},{192,128},{1,193},{65,1},{129,65},{193,129... | collective-permute-start | bytes 491528 | tf_op jit(solution)/shard_map/ppermute | solution.py:119
  96.0 5.4 %collective-permute-start.8 = (bf16[640,128]{1,0:T(8,128)(2,1)S(1)}, bf16[640,128]{1,0:T(8,128)(2,1)S(1)}, u32[]{:S(2)}, u32[]{:S(2)}) collective-permute-start(bf16[640,128]{1,0:T(8,128)(2,1)S(1)} %get-tuple-element.32), channel_id=1, source_target_pairs={{0,64},{64,128},{128,192},{192,0},{1,65},{65,129},{129,193},{193,1... | collective-permute-start | bytes 491528 | tf_op jit(solution)/shard_map/ppermute | solution.py:119
  101.5 11.5 %collective-permute-start.9 = (bf16[1280,128]{1,0:T(8,128)(2,1)S(1)}, bf16[1280,128]{1,0:T(8,128)(2,1)S(1)}, u32[]{:S(2)}, u32[]{:S(2)}) collective-permute-start(bf16[1280,128]{1,0:T(8,128)(2,1)S(1)} %pad_maximum_fusion), channel_id=1, source_target_pairs={{0,64},{64,128},{128,192},{192,0},{1,65},{65,129},{129,193},{193,1... | collective-permute-start | bytes 983048 | tf_op jit(solution)/shard_map/ppermute | solution.py:119
  101.6 11.4 %collective-permute-start.11 = (bf16[1280,128]{1,0:T(8,128)(2,1)S(1)}, bf16[1280,128]{1,0:T(8,128)(2,1)S(1)}, u32[]{:S(2)}, u32[]{:S(2)}) collective-permute-start(bf16[1280,128]{1,0:T(8,128)(2,1)S(1)} %pad_maximum_fusion.1), channel_id=1, source_target_pairs={{0,192},{64,0},{128,64},{192,128},{1,193},{65,1},{129,65},{193,129... | collective-permute-start | bytes 983048 | tf_op jit(solution)/shard_map/ppermute | solution.py:119
  109.5 10.4 %all-to-all-start.4 = ((bf16[4,128,512]{2,1,0:T(8,128)(2,1)}), bf16[4,128,512]{2,1,0:T(8,128)(2,1)S(1)}, u32[]{:S(2)}, u32[]{:S(2)}) async-start(bf16[4,128,512]{2,1,0:T(8,128)(2,1)} %get-tuple-element.7), calls=%async_computation.4 | async-start | bytes 1048576 | tf_op jit(solution)/shard_map/all_to_all | solution.py:186
  119.9 10.4 %all-to-all-start.5 = ((bf16[4,128,512]{2,1,0:T(8,128)(2,1)}), bf16[4,128,512]{2,1,0:T(8,128)(2,1)S(1)}, u32[]{:S(2)}, u32[]{:S(2)}) async-start(bf16[4,128,512]{2,1,0:T(8,128)(2,1)} %get-tuple-element.8), calls=%async_computation.5 | async-start | bytes 1048576 | tf_op jit(solution)/shard_map/all_to_all | solution.py:186
  130.3 34.3 %all-to-all-start.6 = ((bf16[64,32,128]{2,1,0:T(8,128)(2,1)}), bf16[64,32,128]{2,1,0:T(8,128)(2,1)S(1)}, u32[]{:S(2)}, u32[]{:S(2)}) async-start(bf16[64,32,128]{2,1,0:T(8,128)(2,1)} %bitcast.69), calls=%async_computation.6 | async-start | bytes 1048576 | tf_op jit(solution)/shard_map/all_to_all | solution.py:219
  (1 other events, 0.6 us)

commit v2 on v1

v2 whole, which is shorter than its diff:
```python
import math

import jax
import jax.numpy as jnp
from jax import lax
from jax.experimental import pallas as pl
from jax.experimental.pallas import tpu as pltpu
from jax.sharding import PartitionSpec as P

HEAD_DIM = 128
BLOCK = 128
REACH = 4
NEAR = REACH + 1
SPAN = NEAR * BLOCK
LAYERS = 4
TILE = 16
SUBS = BLOCK // TILE
SCALE = HEAD_DIM ** (-0.5)
EXP2_SCALE = SCALE * math.log2(math.e)

masked_score = -1e30
bf16 = jnp.bfloat16
f32 = jnp.float32
ANY = pl.BlockSpec(memory_space=pl.ANY)
VMEM = pl.BlockSpec(memory_space=pltpu.VMEM)
SMEM = pl.BlockSpec(memory_space=pltpu.SMEM)
PARAMS = pltpu.CompilerParams(vmem_limit_bytes=48 * 1024 * 1024)


def shape(*dims, dtype=bf16):
    return jax.ShapeDtypeStruct(dims, dtype)


def nt(a, b):
    return lax.dot_general(a, b, (((1,), (1,)), ((), ())), preferred_element_type=f32)


def nn(a, b):
    return lax.dot_general(a, b, (((1,), (0,)), ((), ())), preferred_element_type=f32)


def spread_kernel(key, value, sent):
    ctx_count = sent.shape[0] // SUBS
    for t in range(SUBS):
        cols = slice(t * HEAD_DIM, (t + 1) * HEAD_DIM)
        k, v = key[:, cols], value[:, cols]
        for c in range(ctx_count):
            sent[c * SUBS + t, :TILE] = k
            sent[c * SUBS + t, TILE:] = v


def spread(key, value, ctx_count):
    return pl.pallas_call(
        spread_kernel,
        out_shape=shape(ctx_count * SUBS, 2 * TILE, HEAD_DIM),
        in_specs=[VMEM, VMEM],
        out_specs=VMEM,
        compiler_params=PARAMS,
        name="spread",
    )(key, value)


def layers_kernel(
    bias_in, kv_own, kv_next, kv_far_a, kv_far_b, kv_prev, qc_own, qc_next, qc_far, qc_prev,
    dkv_own, dkv_next, dkv_far_a, dkv_far_b, dkv_prev, og_own, og_next, og_far, og_prev,
    bias, kv, qc, og, dkv, keys, values, expo, queries, scale_rows, gs_all, ds_all, sems, out_sems,
):
    layers, _, rows, width = qc.shape
    heads = width // HEAD_DIM
    me = lax.axis_index("pipe")
    half = kv.shape[1] // 2

    def slot(d):
        return lax.rem(me + d, layers)

    pairs = [
        (kv_own, kv.at[slot(0)]),
        (kv_next, kv.at[slot(1)]),
        (kv_far_a, kv.at[slot(2), pl.ds(0, half)]),
        (kv_far_b, kv.at[slot(2), pl.ds(half, half)]),
        (kv_prev, kv.at[slot(3)]),
        (qc_own, qc.at[slot(0)]),
        (qc_next, qc.at[slot(1)]),
        (qc_far, qc.at[slot(2)]),
        (qc_prev, qc.at[slot(3)]),
        (bias_in, bias),
    ]
    copies = [pltpu.make_async_copy(a, b, sems.at[i]) for i, (a, b) in enumerate(pairs)]
    for copy in copies:
        copy.start()
    for copy in copies:
        copy.wait()
    for l in range(layers):
        keys[l] = kv[l, :, :TILE].reshape(SPAN, HEAD_DIM)
        values[l] = kv[l, :, TILE:].reshape(SPAN, HEAD_DIM)

    def cols(h):
        return slice(h * HEAD_DIM, (h + 1) * HEAD_DIM)

    def span(h):
        return slice(h * rows, (h + 1) * rows)

    for l in range(layers):
        for h in range(heads):
            q = qc[l, 0, :, cols(h)]
            if l > 0:
                q = (q.astype(f32) + og[l - 1, 0, :, cols(h)].astype(f32)).astype(bf16)
            queries[l, span(h)] = q
            t = nt(q, keys[l]) * EXP2_SCALE + bias[...]
            e = jnp.exp2(t - jnp.max(t, axis=-1, keepdims=True))
            r = 1.0 / jnp.sum(e, axis=-1, keepdims=True)
            e = e.astype(bf16)
            expo[l, span(h)] = e
            scale_rows[l, span(h)] = jnp.broadcast_to(r, (rows, HEAD_DIM))
            og[l, 0, :, cols(h)] = (nn(e, values[l]) * r).astype(bf16)

    for l in reversed(range(layers)):
        for h in range(heads):
            g = qc[l, 1, :, cols(h)]
            if l < layers - 1:
                g = (g.astype(f32) + og[l + 1, 1, :, cols(h)].astype(f32)).astype(bf16)
            gs = (g.astype(f32) * scale_rows[l, span(h)]).astype(bf16)
            gs_all[span(h)] = gs
            delta = jnp.sum(
                gs.astype(f32) * og[l, 0, :, cols(h)].astype(f32), axis=-1, keepdims=True
            )
            ds = (expo[l, span(h)].astype(f32) * (nt(gs, values[l]) - delta)).astype(bf16)
            ds_all[span(h)] = ds
            og[l, 1, :, cols(h)] = (nn(ds, keys[l]) * SCALE).astype(bf16)
        gk = nn(queries[l].T, ds_all[...]) * SCALE
        gv = nn(gs_all[...].T, expo[l])
        dkv[l, :, :TILE] = gk.T.astype(bf16).reshape(SPAN // TILE, TILE, HEAD_DIM)
        dkv[l, :, TILE:] = gv.T.astype(bf16).reshape(SPAN // TILE, TILE, HEAD_DIM)

    pairs = [
        (dkv.at[slot(2), pl.ds(0, half)], dkv_far_a),
        (dkv.at[slot(2), pl.ds(half, half)], dkv_far_b),
        (dkv.at[slot(1)], dkv_next),
        (dkv.at[slot(3)], dkv_prev),
        (dkv.at[slot(0)], dkv_own),
        (og.at[slot(0)], og_own),
        (og.at[slot(1)], og_next),
        (og.at[slot(2)], og_far),
        (og.at[slot(3)], og_prev),
    ]
    copies = [pltpu.make_async_copy(a, b, out_sems.at[i]) for i, (a, b) in enumerate(pairs)]
    for copy in copies:
        copy.start()
    for copy in copies:
        copy.wait()


def run_layers(bias, kv_parts, qc_parts):
    _, rows, width = qc_parts[0].shape
    stacked = rows * width // HEAD_DIM
    tiles = SPAN // TILE
    kv_shape = shape(tiles, 2 * TILE, HEAD_DIM)
    kv_half = shape(tiles // 2, 2 * TILE, HEAD_DIM)
    qc_shape = shape(2, rows, width)
    return pl.pallas_call(
        layers_kernel,
        out_shape=(kv_shape, kv_shape, kv_half, kv_half, kv_shape) + (qc_shape,) * LAYERS,
        in_specs=[ANY] * 10,
        out_specs=(ANY,) * 9,
        scratch_shapes=[
            pltpu.VMEM((rows, SPAN), f32),
            pltpu.VMEM((LAYERS, tiles, 2 * TILE, HEAD_DIM), bf16),
            pltpu.VMEM((LAYERS, 2, rows, width), bf16),
            pltpu.VMEM((LAYERS, 2, rows, width), bf16),
            pltpu.VMEM((LAYERS, tiles, 2 * TILE, HEAD_DIM), bf16),
            pltpu.VMEM((LAYERS, SPAN, HEAD_DIM), bf16),
            pltpu.VMEM((LAYERS, SPAN, HEAD_DIM), bf16),
            pltpu.VMEM((LAYERS, stacked, SPAN), bf16),
            pltpu.VMEM((LAYERS, stacked, HEAD_DIM), bf16),
            pltpu.VMEM((LAYERS, stacked, HEAD_DIM), f32),
            pltpu.VMEM((stacked, HEAD_DIM), bf16),
            pltpu.VMEM((stacked, SPAN), bf16),
            pltpu.SemaphoreType.DMA((10,)),
            pltpu.SemaphoreType.DMA((9,)),
        ],
        compiler_params=PARAMS,
        name="layers",
    )(bias, *kv_parts, *qc_parts)


def place_kernel(order, own_in, up_in, down_in, sent, own, up, down, sems):
    pairs = [(own_in, own), (up_in, up), (down_in, down)]
    copies = [pltpu.make_async_copy(a, b, sems.at[i]) for i, (a, b) in enumerate(pairs)]
    for copy in copies:
        copy.start()
    for copy in copies:
        copy.wait()
    first = order[lax.axis_index("ctx")] - REACH
    for c in range(sent.shape[0] // SUBS):
        j = order[c] - first
        near = (j >= 0) & (j <= REACH)
        at = pl.ds(pl.multiple_of(jnp.clip(j, 0, REACH) * SUBS, SUBS), SUBS)

        @pl.when(near)
        def _():
            total = own[at].astype(f32) + up[at].astype(f32) + down[at].astype(f32)
            sent[c * SUBS:(c + 1) * SUBS] = total.astype(bf16)

        @pl.when(jnp.logical_not(near))
        def _():
            sent[c * SUBS:(c + 1) * SUBS] = jnp.zeros((SUBS, 2 * TILE, HEAD_DIM), bf16)


def place(order, own, up, down):
    return pl.pallas_call(
        place_kernel,
        out_shape=shape(order.shape[0] * SUBS, 2 * TILE, HEAD_DIM),
        in_specs=[SMEM, ANY, ANY, ANY],
        out_specs=VMEM,
        scratch_shapes=[pltpu.VMEM(own.shape, bf16)] * 3 + [pltpu.SemaphoreType.DMA((3,))],
        compiler_params=PARAMS,
        name="place",
    )(order, own, up, down)


def total_kernel(got_in, grad_key, grad_value, got, sem):
    copy = pltpu.make_async_copy(got_in, got, sem)
    copy.start()
    copy.wait()
    for t in range(SUBS):
        total = got[t].astype(f32)
        for c in range(1, got.shape[0] // SUBS):
            total = total + got[c * SUBS + t].astype(f32)
        total = total.astype(bf16)
        cols = slice(t * HEAD_DIM, (t + 1) * HEAD_DIM)
        grad_key[:, cols] = total[:TILE]
        grad_value[:, cols] = total[TILE:]


def total(got):
    return pl.pallas_call(
        total_kernel,
        out_shape=(shape(TILE, SUBS * HEAD_DIM),) * 2,
        in_specs=[ANY],
        out_specs=(VMEM, VMEM),
        scratch_shapes=[pltpu.VMEM(got.shape, bf16), pltpu.SemaphoreType.DMA],
        compiler_params=PARAMS,
        name="total",
    )(got)


def assemble_kernel(own, prev, far, after, out, grad_query, sems):
    me = lax.axis_index("pipe")
    width = own.shape[2]
    copies = []
    for d, piece in enumerate((own, prev, far, after)):
        column = pl.multiple_of(lax.rem(me + LAYERS - d, LAYERS) * width, width)
        for i, whole in enumerate((out, grad_query)):
            copies.append(
                pltpu.make_async_copy(
                    piece.at[i], whole.at[:, pl.ds(column, width)], sems.at[2 * d + i]
                )
            )
    for copy in copies:
        copy.start()
    for copy in copies:
        copy.wait()


def assemble(pieces):
    _, rows, width = pieces[0].shape
    return pl.pallas_call(
        assemble_kernel,
        out_shape=(shape(rows, LAYERS * width),) * 2,
        in_specs=[ANY] * 4,
        out_specs=(ANY, ANY),
        scratch_shapes=[pltpu.SemaphoreType.DMA((8,))],
        compiler_params=PARAMS,
        name="assemble",
    )(*pieces)


def moved(block, distance):
    size = lax.axis_size("pipe")
    return lax.ppermute(block, "pipe", [(i, (i + distance) % size) for i in range(size)])


def exchanged(block, axes):
    return lax.all_to_all(block, axes, split_axis=0, concat_axis=0, tiled=True)


def shards(query_in, key_in, value_in, doc_ids, stretch_order, out_cot):
    ctx_count = lax.axis_size("ctx")
    layer = lax.axis_index("pipe")
    rows = query_in.shape[1]
    part = query_in.shape[2] // LAYERS

    got = exchanged(spread(key_in[0], value_in[0], ctx_count), ("ctx", "tp"))

    def piece(distance):
        start = lax.rem(layer + distance, LAYERS) * part
        return jnp.stack(
            [
                lax.dynamic_slice(
                    x[0], (0, start), (rows, part), allow_negative_indices=False
                )
                for x in (query_in, out_cot)
            ]
        )

    qc_parts = [piece(0), moved(piece(3), 3), moved(piece(2), 2), moved(piece(1), 1)]

    position = stretch_order[lax.axis_index("ctx")]
    block_ids = jnp.arange(ctx_count, dtype=jnp.int32)
    wanted = jnp.maximum(position - REACH + jnp.arange(NEAR, dtype=jnp.int32), 0)
    holder = jnp.sum(
        jnp.where(stretch_order[None, :] == wanted[:, None], block_ids[None, :], 0), axis=1
    )
    own = jnp.concatenate(
        [
            lax.dynamic_slice(
                got, (holder[j] * SUBS, 0, 0), (SUBS, 2 * TILE, HEAD_DIM),
                allow_negative_indices=False,
            )
            for j in range(NEAR)
        ]
    )
    half = own.shape[0] // 2
    before = moved(own, 1)
    after = moved(own, -1)
    far_a = moved(before[:half], 1)
    far_b = moved(after[half:], -1)

    offsets = jnp.arange(SPAN, dtype=jnp.int32)
    row_ids = jnp.arange(rows, dtype=jnp.int32)
    documents = jnp.concatenate([jnp.full((REACH * BLOCK,), -1, jnp.int32), doc_ids])
    near_documents = lax.dynamic_slice(
        documents, (position * BLOCK,), (SPAN,), allow_negative_indices=False
    )
    own_documents = near_documents[REACH * BLOCK:]
    allowed = (offsets[None, :] <= row_ids[:, None] + REACH * BLOCK) & (
        near_documents[None, :] == own_documents[:, None]
    )
    bias = jnp.where(allowed, 0.0, masked_score).astype(f32)

    (
        dkv_own, dkv_next, dkv_far_a, dkv_far_b, dkv_prev, og_own, og_next, og_far, og_prev
    ) = run_layers(bias, (own, after, far_a, far_b, before), qc_parts)

    from_before = moved(dkv_far_a, 1)
    from_after = moved(dkv_far_b, -1)

    def add(a, b):
        return (a.astype(f32) + b.astype(f32)).astype(bf16)

    up = jnp.concatenate([add(dkv_next[:half], from_before), dkv_next[half:]])
    down = jnp.concatenate([dkv_prev[:half], add(dkv_prev[half:], from_after)])
    sent = place(stretch_order, dkv_own, moved(up, 1), moved(down, -1))
    grad_key, grad_value = total(exchanged(sent, ("ctx", "tp")))
    out, grad_query = assemble([og_own, moved(og_next, 1), moved(og_far, 2), moved(og_prev, 3)])
    return (out[None], grad_query[None], grad_key[None], grad_value[None])


def solution(mesh):
    return jax.shard_map(
        shards,
        mesh=mesh,
        in_specs=(
            P("pipe", "ctx", "tp"),
            P("pipe", ("ctx", "tp"), None),
            P("pipe", ("ctx", "tp"), None),
            P(),
            P(),
            P("pipe", "ctx", "tp"),
        ),
        out_specs=(
            P("pipe", "ctx", "tp"),
            P("pipe", "ctx", "tp"),
            P("pipe", ("ctx", "tp"), None),
            P("pipe", ("ctx", "tp"), None),
        ),
        check_vma=False,
    )
```

time: 167 us -> 110 us (0.66)
  starting transfers between devices: 65.6 us -> 39.1 us
  local copies, waits for them, and re-layouts: 19 us -> 3.77 us
  between operations: 19.3 us -> 5.56 us
  waiting for transfers between devices: 51.5 us -> 44.7 us
  Pallas kernels: 9.77 us -> 15.7 us
    all_to_all x7 -> x2, waiting for transfers between devices: 44.2 us -> 9.71 us  [exchanged(): return lax.all_to_all(block, axes, split_axis=0, concat_axis=0, tiled=True)]
    ppermute x12 -> x14, waiting for transfers between devices: 7.34 us -> 35 us  [moved(): lax.ppermute(block, 'pipe', [(i, (i + distance) % size) for i in range(si...]
    all_to_all x7 -> x2, starting transfers between devices: 49 us -> 22.5 us  [exchanged(): return lax.all_to_all(block, axes, split_axis=0, concat_axis=0, tiled=True)]
    unnamed x49 -> x16, local copies, waits for them, and re-layouts: 11.4 us -> 2.24 us
    pallas_call x1 -> x5, Pallas kernels: 9.77 us -> 15.7 us  [the longest x1 11.2 us: run_layers(): pl.pallas_call(layers_kernel, out_shape=(kv_shape, kv_shape, kv_half, kv_...]
    another operation x3 -> x0, local copies, waits for them, and re-layouts: 2.04 us -> none  [the longest x2 2.03 us: to_layers(): block.reshape(rows, layers, part).transpose(1, 0, 2)]
    ppermute x12 -> x14, starting transfers between devices: 16.6 us -> 16.6 us  [moved(): lax.ppermute(block, 'pipe', [(i, (i + distance) % size) for i in range(si...]
  transfers between devices with their start and end apart: 19 -> 16, of which waited for: 11 -> 10; matrix products, arithmetic and copies ran while one was open for 5% -> 2% of each run, Pallas kernels for 0% -> 1%
where the time goes in v2:
time: 110 us; the launch traced here: 109 us
  waiting for transfers between devices  44.7 us (41%)
  starting transfers between devices  39.1 us (36%)
  Pallas kernels  15.7 us (14%)
  between operations  5.56 us (5%)
  local copies, waits for them, and re-layouts  3.77 us (3%)
    ppermute x14, waiting for transfers between devices, moved(): lax.ppermute(block, 'pipe', [(i, (i + distance) % size) for i in range(si...  35 us
    all_to_all x2, starting transfers between devices, exchanged(): return lax.all_to_all(block, axes, split_axis=0, concat_axis=0, tiled=True)  22.5 us
    ppermute x14, starting transfers between devices, moved(): lax.ppermute(block, 'pipe', [(i, (i + distance) % size) for i in range(si...  16.6 us
    pallas_call x1, Pallas kernels, run_layers(): pl.pallas_call(layers_kernel, out_shape=(kv_shape, kv_shape, kv_half, kv_...  11.2 us
    all_to_all x2, waiting for transfers between devices, exchanged(): return lax.all_to_all(block, axes, split_axis=0, concat_axis=0, tiled=True)  9.71 us
    unnamed x16, local copies, waits for them, and re-layouts  2.24 us
  transfers between devices with their start and end apart: 16, of which 10 were waited for; matrix products, arithmetic and copies ran while one was open for 2% of the time, Pallas kernels for 1%

profile of v2, /device:TPU:1, one launch (start us, length us, event | category | flops | bytes accessed | tf_op | source)
XLA Modules:
  0.0 109.4 jit_solution(15460086647258935085)
XLA Ops:
  0.6 0.7 copy-done
  1.4 0.8 copy-done.1
  2.1 0.9 spread.1
  3.0 13.1 %all-to-all-start = ((bf16[64,32,128]{2,1,0:T(8,128)(2,1)}), bf16[64,32,128]{2,1,0:T(8,128)(2,1)S(1)}, u32[]{:S(2)}, u32[]{:S(2)}) async-start(bf16[64,32,128]{2,1,0:T(8,128)(2,1)} %spread.1), calls=%async_computation | async-start | bytes 1048576 | tf_op jit(solution)/shard_map/all_to_all | solution.py:284
  16.3 3.0 %collective-permute-start.5 = (bf16[2,128,512]{2,1,0:T(8,128)(2,1)S(1)}, bf16[2,128,512]{2,1,0:T(8,128)(2,1)S(1)}, u32[]{:S(2)}, u32[]{:S(2)}) collective-permute-start(bf16[2,128,512]{2,1,0:T(8,128)(2,1)S(1)} %pad_maximum_fusion.4), channel_id=1, source_target_pairs={{0,128},{64,192},{128,0},{192,64},{1,129},{65,193},{129,1},{193,65... | collective-permute-start | bytes 786440 | tf_op jit(solution)/shard_map/ppermute | solution.py:280
  19.4 0.9 collective-permute-start.4
  20.2 0.7 copy-done.2
  20.9 0.6 dynamic_slice.45
  22.1 0.2 select_reduce_fusion
  22.3 0.7 fusion.2
  26.2 7.7 %all-to-all-done = bf16[64,32,128]{2,1,0:T(8,128)(2,1)S(1)} async-done(((bf16[64,32,128]{2,1,0:T(8,128)(2,1)}), bf16[64,32,128]{2,1,0:T(8,128)(2,1)S(1)}, u32[]{:S(2)}, u32[]{:S(2)}) %all-to-all-start) | async-done | bytes 524320 | tf_op jit(solution)/shard_map/all_to_all | solution.py:284
  34.0 1.4 %collective-permute-start.1 = (bf16[40,32,128]{2,1,0:T(8,128)(2,1)S(1)}, bf16[40,32,128]{2,1,0:T(8,128)(2,1)S(1)}, u32[]{:S(2)}, u32[]{:S(2)}) collective-permute-start(bf16[40,32,128]{2,1,0:T(8,128)(2,1)S(1)} %dynamic-slice_dynamic-update-slice_fusion.kv_own), channel_id=1, source_target_pairs={{0,64},{64,128},{128,192},{192,0},{1,65},{65,129},{129,193},{193,1... | collective-permute-start | bytes 983048 | tf_op jit(solution)/shard_map/ppermute | solution.py:280
  35.3 1.5 %collective-permute-start = (bf16[40,32,128]{2,1,0:T(8,128)(2,1)S(1)}, bf16[40,32,128]{2,1,0:T(8,128)(2,1)S(1)}, u32[]{:S(2)}, u32[]{:S(2)}) collective-permute-start(bf16[40,32,128]{2,1,0:T(8,128)(2,1)S(1)} %dynamic-slice_dynamic-update-slice_fusion.kv_own), channel_id=1, source_target_pairs={{0,192},{64,0},{128,64},{192,128},{1,193},{65,1},{129,65},{193,129... | collective-permute-start | bytes 983048 | tf_op jit(solution)/shard_map/ppermute | solution.py:280
  37.7 6.5 %collective-permute-done.1.kv_prev = bf16[40,32,128]{2,1,0:T(8,128)(2,1)S(1)} collective-permute-done((bf16[40,32,128]{2,1,0:T(8,128)(2,1)S(1)}, bf16[40,32,128]{2,1,0:T(8,128)(2,1)S(1)}, u32[]{:S(2)}, u32[]{:S(2)}) %collective-permute-start.1) | collective-permute-done | bytes 327712 | tf_op jit(solution)/shard_map/ppermute | solution.py:280
  44.4 2.9 %collective-permute-start.3 = (bf16[20,32,128]{2,1,0:T(8,128)(2,1)S(1)}, bf16[20,32,128]{2,1,0:T(8,128)(2,1)S(1)}, u32[]{:S(2)}, u32[]{:S(2)}) collective-permute-start(bf16[20,32,128]{2,1,0:T(8,128)(2,1)S(1)} %slice.49), channel_id=1, source_target_pairs={{0,192},{64,0},{128,64},{192,128},{1,193},{65,1},{129,65},{193,129... | collective-permute-start | bytes 491528 | tf_op jit(solution)/shard_map/ppermute | solution.py:280
  47.5 2.4 %collective-permute-done.6.qc_prev = bf16[2,128,512]{2,1,0:T(8,128)(2,1)S(1)} collective-permute-done((bf16[2,128,512]{2,1,0:T(8,128)(2,1)S(1)}, bf16[2,128,512]{2,1,0:T(8,128)(2,1)S(1)}, u32[]{:S(2)}, u32[]{:S(2)}) %collective-permute-start.6) | collective-permute-done | bytes 262176 | tf_op jit(solution)/shard_map/ppermute | solution.py:280
  49.9 3.5 %collective-permute-done.2.kv_far_a = bf16[20,32,128]{2,1,0:T(8,128)(2,1)S(1)} collective-permute-done((bf16[20,32,128]{2,1,0:T(8,128)(2,1)S(1)}, bf16[20,32,128]{2,1,0:T(8,128)(2,1)S(1)}, u32[]{:S(2)}, u32[]{:S(2)}) %collective-permute-start.2) | collective-permute-done | bytes 163872 | tf_op jit(solution)/shard_map/ppermute | solution.py:280
  53.4 11.2 %layers.1 = (bf16[40,32,128]{2,1,0:T(8,128)(2,1)S(1)}, bf16[40,32,128]{2,1,0:T(8,128)(2,1)S(1)}, bf16[20,32,128]{2,1,0:T(8,128)(2,1)S(1)}, bf16[20,32,128]{2,1,0...) custom-call(f32[128,640]{1,0:T(8,128)S(1)} %fusion.1.bias_in, ...), custom_call_target="tpu_custom_call" | custom-call | tf_op jit(solution)/shard_map/layers/pallas_call | solution.py:160
  64.7 1.5 %collective-permute-start.12 = (bf16[20,32,128]{2,1,0:T(8,128)(2,1)S(1)}, bf16[20,32,128]{2,1,0:T(8,128)(2,1)S(1)}, u32[]{:S(2)}, u32[]{:S(2)}) collective-permute-start(bf16[20,32,128]{2,1,0:T(8,128)(2,1)S(1)} %get-tuple-element.27), channel_id=1, source_target_pairs={{0,192},{64,0},{128,64},{192,128},{1,193},{65,1},{129,65},{193,129... | collective-permute-start | bytes 491528 | tf_op jit(solution)/shard_map/ppermute | solution.py:280
  66.3 3.0 %collective-permute-done.12 = bf16[20,32,128]{2,1,0:T(8,128)(2,1)S(1)} collective-permute-done((bf16[20,32,128]{2,1,0:T(8,128)(2,1)S(1)}, bf16[20,32,128]{2,1,0:T(8,128)(2,1)S(1)}, u32[]{:S(2)}, u32[]{:S(2)}) %collective-permute-start.12) | collective-permute-done | bytes 163872 | tf_op jit(solution)/shard_map/ppermute | solution.py:280
  69.4 2.3 %collective-permute-start.13 = (bf16[40,32,128]{2,1,0:T(8,128)(2,1)S(1)}, bf16[40,32,128]{2,1,0:T(8,128)(2,1)S(1)}, u32[]{:S(2)}, u32[]{:S(2)}) collective-permute-start(bf16[40,32,128]{2,1,0:T(8,128)(2,1)S(1)} %pad_maximum_fusion.1), channel_id=1, source_target_pairs={{0,192},{64,0},{128,64},{192,128},{1,193},{65,1},{129,65},{193,129... | collective-permute-start | bytes 983048 | tf_op jit(solution)/shard_map/ppermute | solution.py:280
  71.9 4.7 %collective-permute-done.13.down_in = bf16[40,32,128]{2,1,0:T(8,128)(2,1)S(1)} collective-permute-done((bf16[40,32,128]{2,1,0:T(8,128)(2,1)S(1)}, bf16[40,32,128]{2,1,0:T(8,128)(2,1)S(1)}, u32[]{:S(2)}, u32[]{:S(2)}) %collective-permute-start.13) | collective-permute-done | bytes 327712 | tf_op jit(solution)/shard_map/ppermute | solution.py:280
  76.6 3.0 %collective-permute-done.11.up_in = bf16[40,32,128]{2,1,0:T(8,128)(2,1)S(1)} collective-permute-done((bf16[40,32,128]{2,1,0:T(8,128)(2,1)S(1)}, bf16[40,32,128]{2,1,0:T(8,128)(2,1)S(1)}, u32[]{:S(2)}, u32[]{:S(2)}) %collective-permute-start.11) | collective-permute-done | bytes 327712 | tf_op jit(solution)/shard_map/ppermute | solution.py:280
  79.5 1.9 %place.1 = bf16[64,32,128]{2,1,0:T(8,128)(2,1)} custom-call(s32[8]{0:T(128)S(1)} %copy-done.2, bf16[40,32,128]{2,1,0:T(8,128)(2,1)S(1)} %get-tuple-element.23.own_in, bf16[40,32,128]{2,1,0:T(8,128)(2,1)S(1)} %collective-permute-done.11.up_in, bf16[40,32,128]{2,1,0:T(8,128)(2,1)S(1)} %collective-permute-done.13.down_in), custom_call_target="tpu_custom_call" | custom-call | tf_op jit(solution)/shard_map/place/pallas_call | solution.py:210
  81.4 9.4 %all-to-all-start.1 = ((bf16[64,32,128]{2,1,0:T(8,128)(2,1)}), bf16[64,32,128]{2,1,0:T(8,128)(2,1)S(1)}, u32[]{:S(2)}, u32[]{:S(2)}) async-start(bf16[64,32,128]{2,1,0:T(8,128)(2,1)} %place.1), calls=%async_computation.1 | async-start | bytes 1048576 | tf_op jit(solution)/shard_map/all_to_all | solution.py:284
  90.9 0.9 collective-permute-start.8
  91.8 1.7 %collective-permute-start.9 = (bf16[2,128,512]{2,1,0:T(8,128)(2,1)S(1)}, bf16[2,128,512]{2,1,0:T(8,128)(2,1)S(1)}, u32[]{:S(2)}, u32[]{:S(2)}) collective-permute-start(bf16[2,128,512]{2,1,0:T(8,128)(2,1)S(1)} %get-tuple-element.20), channel_id=1, source_target_pairs={{0,192},{64,0},{128,64},{192,128},{1,193},{65,1},{129,65},{193,129... | collective-permute-start | bytes 786440 | tf_op jit(solution)/shard_map/ppermute | solution.py:280
  93.5 11.6 %collective-permute-done.7.prev = bf16[2,128,512]{2,1,0:T(8,128)(2,1)S(1)} collective-permute-done((bf16[2,128,512]{2,1,0:T(8,128)(2,1)S(1)}, bf16[2,128,512]{2,1,0:T(8,128)(2,1)S(1)}, u32[]{:S(2)}, u32[]{:S(2)}) %collective-permute-start.7) | collective-permute-done | bytes 262176 | tf_op jit(solution)/shard_map/ppermute | solution.py:280
  105.1 0.3 collective-permute-done.9.after
  105.5 1.0 assemble.1
  106.5 2.0 %all-to-all-done.1.got_in = bf16[64,32,128]{2,1,0:T(8,128)(2,1)S(1)} async-done(((bf16[64,32,128]{2,1,0:T(8,128)(2,1)}), bf16[64,32,128]{2,1,0:T(8,128)(2,1)S(1)}, u32[]{:S(2)}, u32[]{:S(2)}) %all-to-all-start.1) | async-done | bytes 524320 | tf_op jit(solution)/shard_map/all_to_all | solution.py:284
  108.5 0.7 total.1
  (43 shorter events, 1.2 us)
Async XLA Ops:
  0.6 0.8 copy-start
  1.4 0.8 copy-start.1
  3.0 13.1 %copy-start.3 = (bf16[1,128,2048]{2,1,0:T(8,128)(2,1)S(1)}, bf16[1,128,2048]{2,1,0:T(8,128)(2,1)}, u32[]{:S(2)}) copy-start(bf16[1,128,2048]{2,1,0:T(8,128)(2,1)} %param.11) | copy-start | bytes 1572868
  3.0 13.2 %copy-start.4 = (bf16[1,128,2048]{2,1,0:T(8,128)(2,1)S(1)}, bf16[1,128,2048]{2,1,0:T(8,128)(2,1)}, u32[]{:S(2)}) copy-start(bf16[1,128,2048]{2,1,0:T(8,128)(2,1)} %param.6) | copy-start | bytes 1572868
  3.0 30.8 %all-to-all-start = ((bf16[64,32,128]{2,1,0:T(8,128)(2,1)}), bf16[64,32,128]{2,1,0:T(8,128)(2,1)S(1)}, u32[]{:S(2)}, u32[]{:S(2)}) async-start(bf16[64,32,128]{2,1,0:T(8,128)(2,1)} %spread.1), calls=%async_computation | async-start | bytes 1048576 | tf_op jit(solution)/shard_map/all_to_all | solution.py:284
  16.3 31.2 %collective-permute-start.5 = (bf16[2,128,512]{2,1,0:T(8,128)(2,1)S(1)}, bf16[2,128,512]{2,1,0:T(8,128)(2,1)S(1)}, u32[]{:S(2)}, u32[]{:S(2)}) collective-permute-start(bf16[2,128,512]{2,1,0:T(8,128)(2,1)S(1)} %pad_maximum_fusion.4), channel_id=1, source_target_pairs={{0,128},{64,192},{128,0},{192,64},{1,129},{65,193},{129,1},{193,65... | collective-permute-start | bytes 786440 | tf_op jit(solution)/shard_map/ppermute | solution.py:280
  19.4 28.1 %collective-permute-start.4 = (bf16[2,128,512]{2,1,0:T(8,128)(2,1)S(1)}, bf16[2,128,512]{2,1,0:T(8,128)(2,1)S(1)}, u32[]{:S(2)}, u32[]{:S(2)}) collective-permute-start(bf16[2,128,512]{2,1,0:T(8,128)(2,1)S(1)} %pad_maximum_fusion.3), channel_id=1, source_target_pairs={{0,192},{64,0},{128,64},{192,128},{1,193},{65,1},{129,65},{193,129... | collective-permute-start | bytes 786440 | tf_op jit(solution)/shard_map/ppermute | solution.py:280
  20.2 0.7 copy-start.2
  34.0 10.3 %collective-permute-start.1 = (bf16[40,32,128]{2,1,0:T(8,128)(2,1)S(1)}, bf16[40,32,128]{2,1,0:T(8,128)(2,1)S(1)}, u32[]{:S(2)}, u32[]{:S(2)}) collective-permute-start(bf16[40,32,128]{2,1,0:T(8,128)(2,1)S(1)} %dynamic-slice_dynamic-update-slice_fusion.kv_own), channel_id=1, source_target_pairs={{0,64},{64,128},{128,192},{192,0},{1,65},{65,129},{129,193},{193,1... | collective-permute-start | bytes 983048 | tf_op jit(solution)/shard_map/ppermute | solution.py:280
  35.3 9.1 %collective-permute-start = (bf16[40,32,128]{2,1,0:T(8,128)(2,1)S(1)}, bf16[40,32,128]{2,1,0:T(8,128)(2,1)S(1)}, u32[]{:S(2)}, u32[]{:S(2)}) collective-permute-start(bf16[40,32,128]{2,1,0:T(8,128)(2,1)S(1)} %dynamic-slice_dynamic-update-slice_fusion.kv_own), channel_id=1, source_target_pairs={{0,192},{64,0},{128,64},{192,128},{1,193},{65,1},{129,65},{193,129... | collective-permute-start | bytes 983048 | tf_op jit(solution)/shard_map/ppermute | solution.py:280
  36.9 0.8 copy-start.5
  36.9 13.0 %collective-permute-start.6 = (bf16[2,128,512]{2,1,0:T(8,128)(2,1)S(1)}, bf16[2,128,512]{2,1,0:T(8,128)(2,1)S(1)}, u32[]{:S(2)}, u32[]{:S(2)}) collective-permute-start(bf16[2,128,512]{2,1,0:T(8,128)(2,1)S(1)} %pad_maximum_fusion.5), channel_id=1, source_target_pairs={{0,64},{64,128},{128,192},{192,0},{1,65},{65,129},{129,193},{193,1... | collective-permute-start | bytes 786440 | tf_op jit(solution)/shard_map/ppermute | solution.py:280
  44.3 9.1 %collective-permute-start.2 = (bf16[20,32,128]{2,1,0:T(8,128)(2,1)S(1)}, bf16[20,32,128]{2,1,0:T(8,128)(2,1)S(1)}, u32[]{:S(2)}, u32[]{:S(2)}) collective-permute-start(bf16[20,32,128]{2,1,0:T(8,128)(2,1)S(1)} %slice.48), channel_id=1, source_target_pairs={{0,64},{64,128},{128,192},{192,0},{1,65},{65,129},{129,193},{193,1... | collective-permute-start | bytes 491528 | tf_op jit(solution)/shard_map/ppermute | solution.py:280
  44.4 9.0 %collective-permute-start.3 = (bf16[20,32,128]{2,1,0:T(8,128)(2,1)S(1)}, bf16[20,32,128]{2,1,0:T(8,128)(2,1)S(1)}, u32[]{:S(2)}, u32[]{:S(2)}) collective-permute-start(bf16[20,32,128]{2,1,0:T(8,128)(2,1)S(1)} %slice.49), channel_id=1, source_target_pairs={{0,192},{64,0},{128,64},{192,128},{1,193},{65,1},{129,65},{193,129... | collective-permute-start | bytes 491528 | tf_op jit(solution)/shard_map/ppermute | solution.py:280
  64.7 4.6 %collective-permute-start.12 = (bf16[20,32,128]{2,1,0:T(8,128)(2,1)S(1)}, bf16[20,32,128]{2,1,0:T(8,128)(2,1)S(1)}, u32[]{:S(2)}, u32[]{:S(2)}) collective-permute-start(bf16[20,32,128]{2,1,0:T(8,128)(2,1)S(1)} %get-tuple-element.27), channel_id=1, source_target_pairs={{0,192},{64,0},{128,64},{192,128},{1,193},{65,1},{129,65},{193,129... | collective-permute-start | bytes 491528 | tf_op jit(solution)/shard_map/ppermute | solution.py:280
  66.2 5.5 %collective-permute-start.10 = (bf16[20,32,128]{2,1,0:T(8,128)(2,1)S(1)}, bf16[20,32,128]{2,1,0:T(8,128)(2,1)S(1)}, u32[]{:S(2)}, u32[]{:S(2)}) collective-permute-start(bf16[20,32,128]{2,1,0:T(8,128)(2,1)S(1)} %get-tuple-element.25), channel_id=1, source_target_pairs={{0,64},{64,128},{128,192},{192,0},{1,65},{65,129},{129,193},{193,1... | collective-permute-start | bytes 491528 | tf_op jit(solution)/shard_map/ppermute | solution.py:280
  69.4 7.2 %collective-permute-start.13 = (bf16[40,32,128]{2,1,0:T(8,128)(2,1)S(1)}, bf16[40,32,128]{2,1,0:T(8,128)(2,1)S(1)}, u32[]{:S(2)}, u32[]{:S(2)}) collective-permute-start(bf16[40,32,128]{2,1,0:T(8,128)(2,1)S(1)} %pad_maximum_fusion.1), channel_id=1, source_target_pairs={{0,192},{64,0},{128,64},{192,128},{1,193},{65,1},{129,65},{193,129... | collective-permute-start | bytes 983048 | tf_op jit(solution)/shard_map/ppermute | solution.py:280
  71.8 7.8 %collective-permute-start.11 = (bf16[40,32,128]{2,1,0:T(8,128)(2,1)S(1)}, bf16[40,32,128]{2,1,0:T(8,128)(2,1)S(1)}, u32[]{:S(2)}, u32[]{:S(2)}) collective-permute-start(bf16[40,32,128]{2,1,0:T(8,128)(2,1)S(1)} %pad_maximum_fusion), channel_id=1, source_target_pairs={{0,64},{64,128},{128,192},{192,0},{1,65},{65,129},{129,193},{193,1... | collective-permute-start | bytes 983048 | tf_op jit(solution)/shard_map/ppermute | solution.py:280
  81.4 27.1 %all-to-all-start.1 = ((bf16[64,32,128]{2,1,0:T(8,128)(2,1)}), bf16[64,32,128]{2,1,0:T(8,128)(2,1)S(1)}, u32[]{:S(2)}, u32[]{:S(2)}) async-start(bf16[64,32,128]{2,1,0:T(8,128)(2,1)} %place.1), calls=%async_computation.1 | async-start | bytes 1048576 | tf_op jit(solution)/shard_map/all_to_all | solution.py:284
  90.8 14.3 %collective-permute-start.7 = (bf16[2,128,512]{2,1,0:T(8,128)(2,1)S(1)}, bf16[2,128,512]{2,1,0:T(8,128)(2,1)S(1)}, u32[]{:S(2)}, u32[]{:S(2)}) collective-permute-start(bf16[2,128,512]{2,1,0:T(8,128)(2,1)S(1)} %get-tuple-element.18), channel_id=1, source_target_pairs={{0,64},{64,128},{128,192},{192,0},{1,65},{65,129},{129,193},{193,1... | collective-permute-start | bytes 786440 | tf_op jit(solution)/shard_map/ppermute | solution.py:280
  90.9 14.2 %collective-permute-start.8 = (bf16[2,128,512]{2,1,0:T(8,128)(2,1)S(1)}, bf16[2,128,512]{2,1,0:T(8,128)(2,1)S(1)}, u32[]{:S(2)}, u32[]{:S(2)}) collective-permute-start(bf16[2,128,512]{2,1,0:T(8,128)(2,1)S(1)} %get-tuple-element.19), channel_id=1, source_target_pairs={{0,128},{64,192},{128,0},{192,64},{1,129},{65,193},{129,1},{193,65... | collective-permute-start | bytes 786440 | tf_op jit(solution)/shard_map/ppermute | solution.py:280
  91.8 13.6 %collective-permute-start.9 = (bf16[2,128,512]{2,1,0:T(8,128)(2,1)S(1)}, bf16[2,128,512]{2,1,0:T(8,128)(2,1)S(1)}, u32[]{:S(2)}, u32[]{:S(2)}) collective-permute-start(bf16[2,128,512]{2,1,0:T(8,128)(2,1)S(1)} %get-tuple-element.20), channel_id=1, source_target_pairs={{0,192},{64,0},{128,64},{192,128},{1,193},{65,1},{129,65},{193,129... | collective-permute-start | bytes 786440 | tf_op jit(solution)/shard_map/ppermute | solution.py:280

commit v3 on v2

v3 whole, which is shorter than its diff:
```python
import math

import jax
import jax.numpy as jnp
from jax import lax
from jax.experimental import pallas as pl
from jax.experimental.pallas import tpu as pltpu
from jax.sharding import PartitionSpec as P

HEAD_DIM = 128
BLOCK = 128
REACH = 4
NEAR = REACH + 1
SPAN = NEAR * BLOCK
LAYERS = 4
TILE = 16
SUBS = BLOCK // TILE
SCALE = HEAD_DIM ** (-0.5)
EXP2_SCALE = SCALE * math.log2(math.e)

masked_score = -1e30
bf16 = jnp.bfloat16
f32 = jnp.float32
ANY = pl.BlockSpec(memory_space=pl.ANY)
VMEM = pl.BlockSpec(memory_space=pltpu.VMEM)
SMEM = pl.BlockSpec(memory_space=pltpu.SMEM)
PARAMS = pltpu.CompilerParams(vmem_limit_bytes=48 * 1024 * 1024)


def shape(*dims, dtype=bf16):
    return jax.ShapeDtypeStruct(dims, dtype)


def nt(a, b):
    return lax.dot_general(a, b, (((1,), (1,)), ((), ())), preferred_element_type=f32)


def nn(a, b):
    return lax.dot_general(a, b, (((1,), (0,)), ((), ())), preferred_element_type=f32)


def spread_kernel(key_in, value_in, sent, key, value, sems):
    ctx_count = sent.shape[0] // SUBS
    copies = [
        pltpu.make_async_copy(key_in, key, sems.at[0]),
        pltpu.make_async_copy(value_in, value, sems.at[1]),
    ]
    for copy in copies:
        copy.start()
    for copy in copies:
        copy.wait()
    for t in range(SUBS):
        rows = key if t % 2 == 0 else value
        for j in range(2):
            head = t // 2 * 2 + j
            block = rows[:, head * HEAD_DIM:(head + 1) * HEAD_DIM]
            for c in range(ctx_count):
                sent[c * SUBS + t, j * TILE:(j + 1) * TILE] = block


def spread(key, value, ctx_count):
    return pl.pallas_call(
        spread_kernel,
        out_shape=shape(ctx_count * SUBS, 2 * TILE, HEAD_DIM),
        in_specs=[ANY, ANY],
        out_specs=VMEM,
        scratch_shapes=[pltpu.VMEM(key.shape, bf16)] * 2 + [pltpu.SemaphoreType.DMA((2,))],
        compiler_params=PARAMS,
        name="spread",
    )(key, value)


def run_copies(pairs, sems):
    copies = [pltpu.make_async_copy(a, b, sems.at[i]) for i, (a, b) in enumerate(pairs)]
    for copy in copies:
        copy.start()
    for copy in copies:
        copy.wait()


def place_of():
    pipe = lax.axis_index("pipe")
    core = lax.rem(lax.axis_index("tp"), 2)
    return pipe, core, lax.rem(pipe, 2) * 2 + core


def layers_kernel(
    bias_in, a0, a1, a2, a3, b0, b1, b2, b3, q0, q1, q2, q3,
    keep, give, og0, og1, og2, og3,
    bias, kv, qc, og, dkv, expo, queries, scale_rows, gs_all, ds_all, sems, out_sems,
):
    layers, _, rows, width = qc.shape
    heads = width // HEAD_DIM
    pipe, core, group = place_of()

    def back(start, d):
        return lax.rem(start + layers - d, layers)

    run_copies(
        [(x, kv.at[core, back(pipe, d)]) for d, x in enumerate((a0, a1, a2, a3))]
        + [(x, kv.at[1 - core, back(pipe, d)]) for d, x in enumerate((b0, b1, b2, b3))]
        + [(x, qc.at[back(group, m)]) for m, x in enumerate((q0, q1, q2, q3))]
        + [(bias_in, bias)],
        sems,
    )

    def cols(h):
        return slice(h * HEAD_DIM, (h + 1) * HEAD_DIM)

    def span(h):
        return slice(h * rows, (h + 1) * rows)

    for l in range(layers):
        for h in range(heads):
            q = qc[l, 0, :, cols(h)]
            if l > 0:
                q = (q.astype(f32) + og[l - 1, 0, :, cols(h)].astype(f32)).astype(bf16)
            queries[l, span(h)] = q
            t = nt(q, kv[0, l]) * EXP2_SCALE + bias[...]
            e = jnp.exp2(t - jnp.max(t, axis=-1, keepdims=True))
            r = 1.0 / jnp.sum(e, axis=-1, keepdims=True)
            e = e.astype(bf16)
            expo[l, span(h)] = e
            scale_rows[l, span(h)] = jnp.broadcast_to(r, (rows, HEAD_DIM))
            og[l, 0, :, cols(h)] = (nn(e, kv[1, l]) * r).astype(bf16)

    for l in reversed(range(layers)):
        for h in range(heads):
            g = qc[l, 1, :, cols(h)]
            if l < layers - 1:
                g = (g.astype(f32) + og[l + 1, 1, :, cols(h)].astype(f32)).astype(bf16)
            gs = (g.astype(f32) * scale_rows[l, span(h)]).astype(bf16)
            gs_all[span(h)] = gs
            delta = jnp.sum(
                gs.astype(f32) * og[l, 0, :, cols(h)].astype(f32), axis=-1, keepdims=True
            )
            ds = (expo[l, span(h)].astype(f32) * (nt(gs, kv[1, l]) - delta)).astype(bf16)
            ds_all[span(h)] = ds
            og[l, 1, :, cols(h)] = (nn(ds, kv[0, l]) * SCALE).astype(bf16)
        gk = nn(queries[l].T, ds_all[...]) * SCALE
        gv = nn(gs_all[...].T, expo[l])
        dkv[0, l] = gk.T.astype(bf16)
        dkv[1, l] = gv.T.astype(bf16)

    run_copies(
        [(dkv.at[1 - core, lax.rem(pipe + d, layers)], give.at[d]) for d in range(layers)]
        + [(dkv.at[core, lax.rem(pipe + d, layers)], keep.at[d]) for d in range(layers)]
        + [(og.at[back(group, m)], x) for m, x in enumerate((og0, og1, og2, og3))],
        out_sems,
    )


def run_layers(bias, mine, theirs, qc_parts):
    _, rows, width = qc_parts[0].shape
    stacked = rows * width // HEAD_DIM
    kv_shape = shape(LAYERS, SPAN, HEAD_DIM)
    return pl.pallas_call(
        layers_kernel,
        out_shape=(kv_shape, kv_shape) + (shape(2, rows, width),) * LAYERS,
        in_specs=[ANY] * 13,
        out_specs=(ANY,) * 6,
        scratch_shapes=[
            pltpu.VMEM((rows, SPAN), f32),
            pltpu.VMEM((2, LAYERS, SPAN, HEAD_DIM), bf16),
            pltpu.VMEM((LAYERS, 2, rows, width), bf16),
            pltpu.VMEM((LAYERS, 2, rows, width), bf16),
            pltpu.VMEM((2, LAYERS, SPAN, HEAD_DIM), bf16),
            pltpu.VMEM((LAYERS, stacked, SPAN), bf16),
            pltpu.VMEM((LAYERS, stacked, HEAD_DIM), bf16),
            pltpu.VMEM((LAYERS, stacked, HEAD_DIM), f32),
            pltpu.VMEM((stacked, HEAD_DIM), bf16),
            pltpu.VMEM((stacked, SPAN), bf16),
            pltpu.SemaphoreType.DMA((13,)),
            pltpu.SemaphoreType.DMA((12,)),
        ],
        compiler_params=PARAMS,
        name="layers",
    )(bias, *mine, *theirs, *qc_parts)


def place_kernel(order, p0, p1, p2, p3, sent, parts, sems):
    pipe, _, _ = place_of()
    run_copies(
        [
            (x, parts.at[lax.rem(pipe + LAYERS - d, LAYERS)])
            for d, x in enumerate((p0, p1, p2, p3))
        ],
        sems,
    )
    first = order[lax.axis_index("ctx")] - REACH
    for c in range(sent.shape[0] // SUBS):
        j = order[c] - first
        near = (j >= 0) & (j <= REACH)
        at = pl.ds(pl.multiple_of(jnp.clip(j, 0, REACH) * BLOCK, BLOCK), BLOCK)

        @pl.when(near)
        def _():
            for head in range(2):
                total = parts[2 * head, at].astype(f32) + parts[2 * head + 1, at].astype(f32)
                sent[c * SUBS:(c + 1) * SUBS, head * TILE:(head + 1) * TILE] = total.astype(
                    bf16
                ).reshape(SUBS, TILE, HEAD_DIM)

        @pl.when(jnp.logical_not(near))
        def _():
            sent[c * SUBS:(c + 1) * SUBS] = jnp.zeros((SUBS, 2 * TILE, HEAD_DIM), bf16)


def place(order, parts):
    return pl.pallas_call(
        place_kernel,
        out_shape=shape(order.shape[0] * SUBS, 2 * TILE, HEAD_DIM),
        in_specs=[SMEM] + [ANY] * LAYERS,
        out_specs=VMEM,
        scratch_shapes=[
            pltpu.VMEM((LAYERS, SPAN, HEAD_DIM), bf16), pltpu.SemaphoreType.DMA((LAYERS,))
        ],
        compiler_params=PARAMS,
        name="place",
    )(order, *parts)


def total_kernel(got_in, grad_key, grad_value, got, sem):
    copy = pltpu.make_async_copy(got_in, got, sem)
    copy.start()
    copy.wait()
    for t in range(SUBS):
        total = got[t].astype(f32)
        for c in range(1, got.shape[0] // SUBS):
            total = total + got[c * SUBS + t].astype(f32)
        total = total.astype(bf16)
        whole = grad_key if t % 2 == 0 else grad_value
        for j in range(2):
            head = t // 2 * 2 + j
            whole[:, head * HEAD_DIM:(head + 1) * HEAD_DIM] = total[j * TILE:(j + 1) * TILE]


def total(got):
    return pl.pallas_call(
        total_kernel,
        out_shape=(shape(TILE, SUBS * HEAD_DIM),) * 2,
        in_specs=[ANY],
        out_specs=(VMEM, VMEM),
        scratch_shapes=[pltpu.VMEM(got.shape, bf16), pltpu.SemaphoreType.DMA],
        compiler_params=PARAMS,
        name="total",
    )(got)


def assemble_kernel(g0, g1, g2, g3, out, grad_query, sems):
    me = lax.axis_index("pipe")
    width = g0.shape[2]
    pairs = []
    for m, piece in enumerate((g0, g1, g2, g3)):
        column = pl.multiple_of(lax.rem(me + m, LAYERS) * width, width)
        for i, whole in enumerate((out, grad_query)):
            pairs.append((piece.at[i], whole.at[:, pl.ds(column, width)]))
    run_copies(pairs, sems)


def assemble(pieces):
    _, rows, width = pieces[0].shape
    return pl.pallas_call(
        assemble_kernel,
        out_shape=(shape(rows, LAYERS * width),) * 2,
        in_specs=[ANY] * 4,
        out_specs=(ANY, ANY),
        scratch_shapes=[pltpu.SemaphoreType.DMA((8,))],
        compiler_params=PARAMS,
        name="assemble",
    )(*pieces)


def moved(block, distance):
    size = lax.axis_size("pipe")
    return lax.ppermute(block, "pipe", [(i, (i + distance) % size) for i in range(size)])


def swapped(block):
    size = lax.axis_size("tp")
    return lax.ppermute(block, "tp", [(i, i ^ 1) for i in range(size)])


def group_pairs(m):
    tp_count = lax.axis_size("tp")
    pairs = []
    for l in range(LAYERS):
        for tp in range(tp_count):
            group = (l + m) % LAYERS
            pipe = 2 * (tp % 2) + group // 2
            pairs.append((l * tp_count + tp, pipe * tp_count + tp - tp % 2 + group % 2))
    return pairs


def exchanged(block, axes):
    return lax.all_to_all(block, axes, split_axis=0, concat_axis=0, tiled=True)


def cut(block, starts, sizes):
    return lax.dynamic_slice(block, starts, sizes, allow_negative_indices=False)


def shards(query_in, key_in, value_in, doc_ids, stretch_order, out_cot):
    ctx_count = lax.axis_size("ctx")
    layer = lax.axis_index("pipe")
    rows = query_in.shape[1]
    part = query_in.shape[2] // LAYERS

    got = exchanged(spread(key_in[0], value_in[0], ctx_count), ("ctx", "tp"))

    qc_parts = []
    for m in range(LAYERS):
        start = lax.rem(layer + m, LAYERS) * part
        piece = jnp.stack([cut(x[0], (0, start), (rows, part)) for x in (query_in, out_cot)])
        qc_parts.append(lax.ppermute(piece, ("pipe", "tp"), group_pairs(m)))

    position = stretch_order[lax.axis_index("ctx")]
    block_ids = jnp.arange(ctx_count, dtype=jnp.int32)
    wanted = jnp.maximum(position - REACH + jnp.arange(NEAR, dtype=jnp.int32), 0)
    holder = jnp.sum(
        jnp.where(stretch_order[None, :] == wanted[:, None], block_ids[None, :], 0), axis=1
    )

    def window(distance):
        head = lax.rem(layer + distance, LAYERS) // 2
        return jnp.concatenate(
            [
                cut(got, (holder[j] * SUBS, head * TILE, 0), (SUBS, TILE, HEAD_DIM))
                for j in range(NEAR)
            ]
        ).reshape(SPAN, HEAD_DIM)

    mine = [window(0)] + [moved(window(d), d) for d in (1, 3, 2)]
    mine = [mine[0], mine[1], mine[3], mine[2]]
    theirs = [swapped(x) for x in mine]

    offsets = jnp.arange(SPAN, dtype=jnp.int32)
    row_ids = jnp.arange(rows, dtype=jnp.int32)
    documents = jnp.concatenate([jnp.full((REACH * BLOCK,), -1, jnp.int32), doc_ids])
    near_documents = cut(documents, (position * BLOCK,), (SPAN,))
    own_documents = near_documents[REACH * BLOCK:]
    allowed = (offsets[None, :] <= row_ids[:, None] + REACH * BLOCK) & (
        near_documents[None, :] == own_documents[:, None]
    )
    bias = jnp.where(allowed, 0.0, masked_score).astype(f32)

    keep, give, *groups = run_layers(bias, mine, theirs, qc_parts)
    received = swapped(give)
    sums = [
        (keep[d].astype(f32) + received[d].astype(f32)).astype(bf16) for d in range(LAYERS)
    ]
    parts = [sums[0]] + [moved(sums[d], d) for d in (1, 3, 2)]
    parts = [parts[0], parts[1], parts[3], parts[2]]
    grad_key, grad_value = total(exchanged(place(stretch_order, parts), ("ctx", "tp")))
    pieces = [
        lax.ppermute(x, ("pipe", "tp"), [(b, a) for a, b in group_pairs(m)])
        for m, x in enumerate(groups)
    ]
    out, grad_query = assemble(pieces)
    return (out[None], grad_query[None], grad_key[None], grad_value[None])


def solution(mesh):
    return jax.shard_map(
        shards,
        mesh=mesh,
        in_specs=(
            P("pipe", "ctx", "tp"),
            P("pipe", ("ctx", "tp"), None),
            P("pipe", ("ctx", "tp"), None),
            P(),
            P(),
            P("pipe", "ctx", "tp"),
        ),
        out_specs=(
            P("pipe", "ctx", "tp"),
            P("pipe", "ctx", "tp"),
            P("pipe", ("ctx", "tp"), None),
            P("pipe", ("ctx", "tp"), None),
        ),
        check_vma=False,
    )
```

time: 110 us -> 108 us (0.982)
  waiting for transfers between devices: 44.7 us -> 24.6 us
  starting transfers between devices: 39.1 us -> 53.8 us
  Pallas kernels: 15.7 us -> 18.6 us
    ppermute x0 -> x13, starting transfers between devices: none -> 26.9 us  [the longest x4 12.1 us: shards(): qc_parts.append(lax.ppermute(piece, ('pipe', 'tp'), group_pairs(m)))]
    ppermute x14 -> x6, waiting for transfers between devices: 35 us -> 11.6 us  [moved(): lax.ppermute(block, 'pipe', [(i, (i + distance) % size) for i in range(si...]
    ppermute x0 -> x13, waiting for transfers between devices: none -> 10.5 us  [the longest x4 7.89 us: shards(): lax.ppermute(x, ('pipe', 'tp'), [(b, a) for a, b in group_pairs(m)])]
    ppermute x14 -> x6, starting transfers between devices: 16.6 us -> 6.65 us  [moved(): lax.ppermute(block, 'pipe', [(i, (i + distance) % size) for i in range(si...]
    all_to_all x2, waiting for transfers between devices: 9.71 us -> 2.52 us  [exchanged(): return lax.all_to_all(block, axes, split_axis=0, concat_axis=0, tiled=True)]
    pallas_call x1, Pallas kernels: 11.2 us -> 13.5 us  [run_layers(): pl.pallas_call(layers_kernel, out_shape=(kv_shape, kv_shape) + (shape(2,...]
    all_to_all x2, starting transfers between devices: 22.5 us -> 20.3 us  [exchanged(): return lax.all_to_all(block, axes, split_axis=0, concat_axis=0, tiled=True)]
  transfers between devices with their start and end apart: 16 -> 21, of which waited for: 10 -> 11; matrix products, arithmetic and copies ran while one was open for 2% -> 2% of each run, Pallas kernels for 1% -> 1%
where the time goes in v3:
time: 108 us; the launch traced here: 107 us
  starting transfers between devices  53.8 us (50%)
  waiting for transfers between devices  24.6 us (23%)
  Pallas kernels  18.6 us (17%)
  between operations  5.75 us (5%)
  local copies, waits for them, and re-layouts  3.78 us (4%)
    all_to_all x2, starting transfers between devices, exchanged(): return lax.all_to_all(block, axes, split_axis=0, concat_axis=0, tiled=True)  20.3 us
    pallas_call x1, Pallas kernels, run_layers(): pl.pallas_call(layers_kernel, out_shape=(kv_shape, kv_shape) + (shape(2,...  13.5 us
    ppermute x4, starting transfers between devices, shards(): qc_parts.append(lax.ppermute(piece, ('pipe', 'tp'), group_pairs(m)))  12.1 us
    ppermute x6, waiting for transfers between devices, moved(): lax.ppermute(block, 'pipe', [(i, (i + distance) % size) for i in range(si...  11.6 us
    ppermute x4, starting transfers between devices, shards(): lax.ppermute(x, ('pipe', 'tp'), [(b, a) for a, b in group_pairs(m)])  9.8 us
    ppermute x4, waiting for transfers between devices, shards(): lax.ppermute(x, ('pipe', 'tp'), [(b, a) for a, b in group_pairs(m)])  7.89 us
    ppermute x6, starting transfers between devices, moved(): lax.ppermute(block, 'pipe', [(i, (i + distance) % size) for i in range(si...  6.65 us
    ppermute x5, starting transfers between devices, swapped(): return lax.ppermute(block, 'tp', [(i, i ^ 1) for i in range(size)])  5.05 us
  transfers between devices with their start and end apart: 21, of which 11 were waited for; matrix products, arithmetic and copies ran while one was open for 2% of the time, Pallas kernels for 1%

profile of v3, /device:TPU:1, one launch (start us, length us, event | category | flops | bytes accessed | tf_op | source)
XLA Modules:
  0.0 107.1 jit_solution(11626503941711370919)
XLA Ops:
  1.4 0.8 copy-done.1
  2.1 0.9 spread.1
  3.1 13.1 %all-to-all-start = ((bf16[64,32,128]{2,1,0:T(8,128)(2,1)}), bf16[64,32,128]{2,1,0:T(8,128)(2,1)S(1)}, u32[]{:S(2)}, u32[]{:S(2)}) async-start(bf16[64,32,128]{2,1,0:T(8,128)(2,1)} %spread.1), calls=%async_computation | async-start | bytes 1048576 | tf_op jit(solution)/shard_map/all_to_all | solution.py:296
  16.4 3.2 %collective-permute-start.9 = (bf16[2,128,512]{2,1,0:T(8,128)(2,1)S(1)}, bf16[2,128,512]{2,1,0:T(8,128)(2,1)S(1)}, u32[]{:S(2)}, u32[]{:S(2)}) collective-permute-start(bf16[2,128,512]{2,1,0:T(8,128)(2,1)S(1)} %pad_maximum_fusion.2), channel_id=1, source_target_pairs={{0,64},{1,192},{2,66},{3,194},{4,68},{5,196},{6,70},{7,198},{64,65... | collective-permute-start | bytes 786440 | tf_op jit(solution)/shard_map/ppermute | solution.py:315
  19.6 2.4 %collective-permute-start.7 = (bf16[2,128,512]{2,1,0:T(8,128)(2,1)S(1)}, bf16[2,128,512]{2,1,0:T(8,128)(2,1)S(1)}, u32[]{:S(2)}, u32[]{:S(2)}) collective-permute-start(bf16[2,128,512]{2,1,0:T(8,128)(2,1)S(1)} %pad_maximum_fusion), channel_id=1, source_target_pairs={{0,0},{1,128},{2,2},{3,130},{4,4},{5,132},{6,6},{7,134},{64,1},{65... | collective-permute-start | bytes 786440 | tf_op jit(solution)/shard_map/ppermute | solution.py:315
  22.1 2.6 %collective-permute-start.8 = (bf16[2,128,512]{2,1,0:T(8,128)(2,1)S(1)}, bf16[2,128,512]{2,1,0:T(8,128)(2,1)S(1)}, u32[]{:S(2)}, u32[]{:S(2)}) collective-permute-start(bf16[2,128,512]{2,1,0:T(8,128)(2,1)S(1)} %pad_maximum_fusion.1), channel_id=1, source_target_pairs={{0,1},{1,129},{2,3},{3,131},{4,5},{5,133},{6,7},{7,135},{64,64},{6... | collective-permute-start | bytes 786440 | tf_op jit(solution)/shard_map/ppermute | solution.py:315
  31.5 2.5 %all-to-all-done = bf16[64,32,128]{2,1,0:T(8,128)(2,1)S(1)} async-done(((bf16[64,32,128]{2,1,0:T(8,128)(2,1)}), bf16[64,32,128]{2,1,0:T(8,128)(2,1)S(1)}, u32[]{:S(2)}, u32[]{:S(2)}) %all-to-all-start) | async-done | bytes 524320 | tf_op jit(solution)/shard_map/all_to_all | solution.py:296
  34.2 3.0 %collective-permute-start.1 = (bf16[640,128]{1,0:T(8,128)(2,1)S(1)}, bf16[640,128]{1,0:T(8,128)(2,1)S(1)}, u32[]{:S(2)}, u32[]{:S(2)}) collective-permute-start(bf16[640,128]{1,0:T(8,128)(2,1)S(1)} %bitcast.30), channel_id=1, source_target_pairs={{0,128},{64,192},{128,0},{192,64},{1,129},{65,193},{129,1},{193,65... | collective-permute-start | bytes 491528 | tf_op jit(solution)/shard_map/ppermute | solution.py:276
  37.2 0.8 collective-permute-start.2
  38.7 3.9 %collective-permute-start.10 = (bf16[2,128,512]{2,1,0:T(8,128)(2,1)S(1)}, bf16[2,128,512]{2,1,0:T(8,128)(2,1)S(1)}, u32[]{:S(2)}, u32[]{:S(2)}) collective-permute-start(bf16[2,128,512]{2,1,0:T(8,128)(2,1)S(1)} %pad_maximum_fusion.3), channel_id=1, source_target_pairs={{0,65},{1,193},{2,67},{3,195},{4,69},{5,197},{6,71},{7,199},{64,0}... | collective-permute-start | bytes 786440 | tf_op jit(solution)/shard_map/ppermute | solution.py:315
  43.2 1.8 %collective-permute-done.2.a3 = bf16[640,128]{1,0:T(8,128)(2,1)S(1)} collective-permute-done((bf16[640,128]{1,0:T(8,128)(2,1)S(1)}, bf16[640,128]{1,0:T(8,128)(2,1)S(1)}, u32[]{:S(2)}, u32[]{:S(2)}) %collective-permute-start.2) | collective-permute-done | bytes 163872 | tf_op jit(solution)/shard_map/ppermute | solution.py:276
  45.0 1.2 %collective-permute-start.6 = (bf16[640,128]{1,0:T(8,128)(2,1)S(1)}, bf16[640,128]{1,0:T(8,128)(2,1)S(1)}, u32[]{:S(2)}, u32[]{:S(2)}) collective-permute-start(bf16[640,128]{1,0:T(8,128)(2,1)S(1)} %collective-permute-done.2.a3), channel_id=1, source_target_pairs={{0,1},{1,0},{2,3},{3,2},{4,5},{5,4},{6,7},{7,6},{8,9},{9,8},{10,11... | collective-permute-start | bytes 491528 | tf_op jit(solution)/shard_map/ppermute | solution.py:281
  46.3 2.8 %collective-permute-start.4 = (bf16[640,128]{1,0:T(8,128)(2,1)S(1)}, bf16[640,128]{1,0:T(8,128)(2,1)S(1)}, u32[]{:S(2)}, u32[]{:S(2)}) collective-permute-start(bf16[640,128]{1,0:T(8,128)(2,1)S(1)} %collective-permute-done.a1), channel_id=1, source_target_pairs={{0,1},{1,0},{2,3},{3,2},{4,5},{5,4},{6,7},{7,6},{8,9},{9,8},{10,11... | collective-permute-start | bytes 491528 | tf_op jit(solution)/shard_map/ppermute | solution.py:281
  49.2 0.9 collective-permute-done.4.b1
  50.1 13.5 %layers.1 = (bf16[4,640,128]{2,1,0:T(8,128)(2,1)S(1)}, bf16[4,640,128]{2,1,0:T(8,128)(2,1)S(1)}, bf16[2,128,512]{2,1,0:T(8,128)(2,1)S(1)}, bf16[2,128,512]{2,1,0...) custom-call(f32[128,640]{1,0:T(8,128)S(1)} %fusion.1.bias_in, ...), custom_call_target="tpu_custom_call" | custom-call | tf_op jit(solution)/shard_map/layers/pallas_call | solution.py:157
  64.0 1.7 %collective-permute-done.15 = bf16[4,640,128]{2,1,0:T(8,128)(2,1)S(1)} collective-permute-done((bf16[4,640,128]{2,1,0:T(8,128)(2,1)S(1)}, bf16[4,640,128]{2,1,0:T(8,128)(2,1)S(1)}, u32[]{:S(2)}, u32[]{:S(2)}) %collective-permute-start.15) | collective-permute-done | bytes 655392 | tf_op jit(solution)/shard_map/ppermute | solution.py:281
  65.9 0.8 collective-permute-start.18
  66.8 0.8 collective-permute-start.17
  68.1 3.3 %collective-permute-done.18.p3 = bf16[640,128]{1,0:T(8,128)(2,1)S(1)} collective-permute-done((bf16[640,128]{1,0:T(8,128)(2,1)S(1)}, bf16[640,128]{1,0:T(8,128)(2,1)S(1)}, u32[]{:S(2)}, u32[]{:S(2)}) %collective-permute-start.18) | collective-permute-done | bytes 163872 | tf_op jit(solution)/shard_map/ppermute | solution.py:276
  71.4 2.2 %collective-permute-done.17.p2 = bf16[640,128]{1,0:T(8,128)(2,1)S(1)} collective-permute-done((bf16[640,128]{1,0:T(8,128)(2,1)S(1)}, bf16[640,128]{1,0:T(8,128)(2,1)S(1)}, u32[]{:S(2)}, u32[]{:S(2)}) %collective-permute-start.17) | collective-permute-done | bytes 163872 | tf_op jit(solution)/shard_map/ppermute | solution.py:276
  73.7 4.2 %collective-permute-done.16.p1 = bf16[640,128]{1,0:T(8,128)(2,1)S(1)} collective-permute-done((bf16[640,128]{1,0:T(8,128)(2,1)S(1)}, bf16[640,128]{1,0:T(8,128)(2,1)S(1)}, u32[]{:S(2)}, u32[]{:S(2)}) %collective-permute-start.16) | collective-permute-done | bytes 163872 | tf_op jit(solution)/shard_map/ppermute | solution.py:276
  77.9 2.4 %place.1 = bf16[64,32,128]{2,1,0:T(8,128)(2,1)} custom-call(s32[8]{0:T(128)S(1)} %copy-done.2, bf16[640,128]{1,0:T(8,128)(2,1)S(1)} %get-tuple-element.27.p0, bf16[640,128]{1,0:T(8,128)(2,1)S(1)} %collective-permute-done.16.p1, bf16[640,128]{1,0:T(8,128)(2,1)S(1)} %collective-permute-done.17.p2, bf16[640,128]{1,0:T(8,128)(2,1)S(1)} %collective-permute-done.18.p3), custom_call_target="tpu_custom_call" | custom-call | tf_op jit(solution)/shard_map/place/pallas_call | solution.py:210
  80.3 7.1 %all-to-all-start.1 = ((bf16[64,32,128]{2,1,0:T(8,128)(2,1)}), bf16[64,32,128]{2,1,0:T(8,128)(2,1)S(1)}, u32[]{:S(2)}, u32[]{:S(2)}) async-start(bf16[64,32,128]{2,1,0:T(8,128)(2,1)} %place.1), calls=%async_computation.1 | async-start | bytes 1048576 | tf_op jit(solution)/shard_map/all_to_all | solution.py:296
  87.5 1.9 %collective-permute-start.11 = (bf16[2,128,512]{2,1,0:T(8,128)(2,1)S(1)}, bf16[2,128,512]{2,1,0:T(8,128)(2,1)S(1)}, u32[]{:S(2)}, u32[]{:S(2)}) collective-permute-start(bf16[2,128,512]{2,1,0:T(8,128)(2,1)S(1)} %get-tuple-element.14), channel_id=1, source_target_pairs={{0,0},{128,1},{2,2},{130,3},{4,4},{132,5},{6,6},{134,7},{1,64},{12... | collective-permute-start | bytes 786440 | tf_op jit(solution)/shard_map/ppermute | solution.py:356
  89.4 1.9 %collective-permute-start.12 = (bf16[2,128,512]{2,1,0:T(8,128)(2,1)S(1)}, bf16[2,128,512]{2,1,0:T(8,128)(2,1)S(1)}, u32[]{:S(2)}, u32[]{:S(2)}) collective-permute-start(bf16[2,128,512]{2,1,0:T(8,128)(2,1)S(1)} %get-tuple-element.15), channel_id=1, source_target_pairs={{1,0},{129,1},{3,2},{131,3},{5,4},{133,5},{7,6},{135,7},{64,64},{1... | collective-permute-start | bytes 786440 | tf_op jit(solution)/shard_map/ppermute | solution.py:356
  91.4 4.1 %collective-permute-start.13 = (bf16[2,128,512]{2,1,0:T(8,128)(2,1)S(1)}, bf16[2,128,512]{2,1,0:T(8,128)(2,1)S(1)}, u32[]{:S(2)}, u32[]{:S(2)}) collective-permute-start(bf16[2,128,512]{2,1,0:T(8,128)(2,1)S(1)} %get-tuple-element.16), channel_id=1, source_target_pairs={{64,0},{192,1},{66,2},{194,3},{68,4},{196,5},{70,6},{198,7},{65,64... | collective-permute-start | bytes 786440 | tf_op jit(solution)/shard_map/ppermute | solution.py:356
  95.4 1.9 %collective-permute-start.14 = (bf16[2,128,512]{2,1,0:T(8,128)(2,1)S(1)}, bf16[2,128,512]{2,1,0:T(8,128)(2,1)S(1)}, u32[]{:S(2)}, u32[]{:S(2)}) collective-permute-start(bf16[2,128,512]{2,1,0:T(8,128)(2,1)S(1)} %get-tuple-element.17), channel_id=1, source_target_pairs={{65,0},{193,1},{67,2},{195,3},{69,4},{197,5},{71,6},{199,7},{0,64}... | collective-permute-start | bytes 786440 | tf_op jit(solution)/shard_map/ppermute | solution.py:356
  97.3 1.1 collective-permute-done.11.g0
  98.4 2.8 %collective-permute-done.12.g1 = bf16[2,128,512]{2,1,0:T(8,128)(2,1)S(1)} collective-permute-done((bf16[2,128,512]{2,1,0:T(8,128)(2,1)S(1)}, bf16[2,128,512]{2,1,0:T(8,128)(2,1)S(1)}, u32[]{:S(2)}, u32[]{:S(2)}) %collective-permute-start.12) | collective-permute-done | bytes 262176 | tf_op jit(solution)/shard_map/ppermute | solution.py:356
  101.2 2.7 %collective-permute-done.13.g2 = bf16[2,128,512]{2,1,0:T(8,128)(2,1)S(1)} collective-permute-done((bf16[2,128,512]{2,1,0:T(8,128)(2,1)S(1)}, bf16[2,128,512]{2,1,0:T(8,128)(2,1)S(1)}, u32[]{:S(2)}, u32[]{:S(2)}) %collective-permute-start.13) | collective-permute-done | bytes 262176 | tf_op jit(solution)/shard_map/ppermute | solution.py:356
  103.9 1.3 %collective-permute-done.14.g3 = bf16[2,128,512]{2,1,0:T(8,128)(2,1)S(1)} collective-permute-done((bf16[2,128,512]{2,1,0:T(8,128)(2,1)S(1)}, bf16[2,128,512]{2,1,0:T(8,128)(2,1)S(1)}, u32[]{:S(2)}, u32[]{:S(2)}) %collective-permute-start.14) | collective-permute-done | bytes 262176 | tf_op jit(solution)/shard_map/ppermute | solution.py:356
  105.2 1.0 assemble.1
  (46 shorter events, 6.7 us)
Async XLA Ops:
  0.6 0.8 copy-start
  1.4 0.8 copy-start.1
  3.1 13.2 %copy-start.3 = (bf16[1,128,2048]{2,1,0:T(8,128)(2,1)S(1)}, bf16[1,128,2048]{2,1,0:T(8,128)(2,1)}, u32[]{:S(2)}) copy-start(bf16[1,128,2048]{2,1,0:T(8,128)(2,1)} %param.11) | copy-start | bytes 1572868
  3.1 13.2 %copy-start.4 = (bf16[1,128,2048]{2,1,0:T(8,128)(2,1)S(1)}, bf16[1,128,2048]{2,1,0:T(8,128)(2,1)}, u32[]{:S(2)}) copy-start(bf16[1,128,2048]{2,1,0:T(8,128)(2,1)} %param.6) | copy-start | bytes 1572868
  3.1 30.9 %all-to-all-start = ((bf16[64,32,128]{2,1,0:T(8,128)(2,1)}), bf16[64,32,128]{2,1,0:T(8,128)(2,1)S(1)}, u32[]{:S(2)}, u32[]{:S(2)}) async-start(bf16[64,32,128]{2,1,0:T(8,128)(2,1)} %spread.1), calls=%async_computation | async-start | bytes 1048576 | tf_op jit(solution)/shard_map/all_to_all | solution.py:296
  16.4 21.5 %collective-permute-start.9 = (bf16[2,128,512]{2,1,0:T(8,128)(2,1)S(1)}, bf16[2,128,512]{2,1,0:T(8,128)(2,1)S(1)}, u32[]{:S(2)}, u32[]{:S(2)}) collective-permute-start(bf16[2,128,512]{2,1,0:T(8,128)(2,1)S(1)} %pad_maximum_fusion.2), channel_id=1, source_target_pairs={{0,64},{1,192},{2,66},{3,194},{4,68},{5,196},{6,70},{7,198},{64,65... | collective-permute-start | bytes 786440 | tf_op jit(solution)/shard_map/ppermute | solution.py:315
  19.6 19.1 %collective-permute-start.7 = (bf16[2,128,512]{2,1,0:T(8,128)(2,1)S(1)}, bf16[2,128,512]{2,1,0:T(8,128)(2,1)S(1)}, u32[]{:S(2)}, u32[]{:S(2)}) collective-permute-start(bf16[2,128,512]{2,1,0:T(8,128)(2,1)S(1)} %pad_maximum_fusion), channel_id=1, source_target_pairs={{0,0},{1,128},{2,2},{3,130},{4,4},{5,132},{6,6},{7,134},{64,1},{65... | collective-permute-start | bytes 786440 | tf_op jit(solution)/shard_map/ppermute | solution.py:315
  22.1 20.5 %collective-permute-start.8 = (bf16[2,128,512]{2,1,0:T(8,128)(2,1)S(1)}, bf16[2,128,512]{2,1,0:T(8,128)(2,1)S(1)}, u32[]{:S(2)}, u32[]{:S(2)}) collective-permute-start(bf16[2,128,512]{2,1,0:T(8,128)(2,1)S(1)} %pad_maximum_fusion.1), channel_id=1, source_target_pairs={{0,1},{1,129},{2,3},{3,131},{4,5},{5,133},{6,7},{7,135},{64,64},{6... | collective-permute-start | bytes 786440 | tf_op jit(solution)/shard_map/ppermute | solution.py:315
  24.8 0.7 copy-start.2
  34.2 8.6 %collective-permute-start.1 = (bf16[640,128]{1,0:T(8,128)(2,1)S(1)}, bf16[640,128]{1,0:T(8,128)(2,1)S(1)}, u32[]{:S(2)}, u32[]{:S(2)}) collective-permute-start(bf16[640,128]{1,0:T(8,128)(2,1)S(1)} %bitcast.30), channel_id=1, source_target_pairs={{0,128},{64,192},{128,0},{192,64},{1,129},{65,193},{129,1},{193,65... | collective-permute-start | bytes 491528 | tf_op jit(solution)/shard_map/ppermute | solution.py:276
  37.2 1.5 %copy-start.5 = (s32[1024]{0:T(1024)S(1)}, s32[1024]{0:T(1024)}, u32[]{:S(2)}) copy-start(s32[1024]{0:T(1024)} %param.9) | copy-start | bytes 12292
  37.2 7.9 %collective-permute-start.2 = (bf16[640,128]{1,0:T(8,128)(2,1)S(1)}, bf16[640,128]{1,0:T(8,128)(2,1)S(1)}, u32[]{:S(2)}, u32[]{:S(2)}) collective-permute-start(bf16[640,128]{1,0:T(8,128)(2,1)S(1)} %bitcast.29), channel_id=1, source_target_pairs={{0,192},{64,0},{128,64},{192,128},{1,193},{65,1},{129,65},{193,129... | collective-permute-start | bytes 491528 | tf_op jit(solution)/shard_map/ppermute | solution.py:276
  37.9 8.3 %collective-permute-start = (bf16[640,128]{1,0:T(8,128)(2,1)S(1)}, bf16[640,128]{1,0:T(8,128)(2,1)S(1)}, u32[]{:S(2)}, u32[]{:S(2)}) collective-permute-start(bf16[640,128]{1,0:T(8,128)(2,1)S(1)} %bitcast.31), channel_id=1, source_target_pairs={{0,64},{64,128},{128,192},{192,0},{1,65},{65,129},{129,193},{193,1... | collective-permute-start | bytes 491528 | tf_op jit(solution)/shard_map/ppermute | solution.py:276
  38.7 10.5 %collective-permute-start.10 = (bf16[2,128,512]{2,1,0:T(8,128)(2,1)S(1)}, bf16[2,128,512]{2,1,0:T(8,128)(2,1)S(1)}, u32[]{:S(2)}, u32[]{:S(2)}) collective-permute-start(bf16[2,128,512]{2,1,0:T(8,128)(2,1)S(1)} %pad_maximum_fusion.3), channel_id=1, source_target_pairs={{0,65},{1,193},{2,67},{3,195},{4,69},{5,197},{6,71},{7,199},{64,0}... | collective-permute-start | bytes 786440 | tf_op jit(solution)/shard_map/ppermute | solution.py:315
  42.6 6.5 %collective-permute-start.3 = (bf16[640,128]{1,0:T(8,128)(2,1)S(1)}, bf16[640,128]{1,0:T(8,128)(2,1)S(1)}, u32[]{:S(2)}, u32[]{:S(2)}) collective-permute-start(bf16[640,128]{1,0:T(8,128)(2,1)S(1)} %bitcast.25), channel_id=1, source_target_pairs={{0,1},{1,0},{2,3},{3,2},{4,5},{5,4},{6,7},{7,6},{8,9},{9,8},{10,11... | collective-permute-start | bytes 491528 | tf_op jit(solution)/shard_map/ppermute | solution.py:281
  42.8 6.4 %collective-permute-start.5 = (bf16[640,128]{1,0:T(8,128)(2,1)S(1)}, bf16[640,128]{1,0:T(8,128)(2,1)S(1)}, u32[]{:S(2)}, u32[]{:S(2)}) collective-permute-start(bf16[640,128]{1,0:T(8,128)(2,1)S(1)} %collective-permute-done.1.a2), channel_id=1, source_target_pairs={{0,1},{1,0},{2,3},{3,2},{4,5},{5,4},{6,7},{7,6},{8,9},{9,8},{10,11... | collective-permute-start | bytes 491528 | tf_op jit(solution)/shard_map/ppermute | solution.py:281
  45.0 4.2 %collective-permute-start.6 = (bf16[640,128]{1,0:T(8,128)(2,1)S(1)}, bf16[640,128]{1,0:T(8,128)(2,1)S(1)}, u32[]{:S(2)}, u32[]{:S(2)}) collective-permute-start(bf16[640,128]{1,0:T(8,128)(2,1)S(1)} %collective-permute-done.2.a3), channel_id=1, source_target_pairs={{0,1},{1,0},{2,3},{3,2},{4,5},{5,4},{6,7},{7,6},{8,9},{9,8},{10,11... | collective-permute-start | bytes 491528 | tf_op jit(solution)/shard_map/ppermute | solution.py:281
  46.3 3.8 %collective-permute-start.4 = (bf16[640,128]{1,0:T(8,128)(2,1)S(1)}, bf16[640,128]{1,0:T(8,128)(2,1)S(1)}, u32[]{:S(2)}, u32[]{:S(2)}) collective-permute-start(bf16[640,128]{1,0:T(8,128)(2,1)S(1)} %collective-permute-done.a1), channel_id=1, source_target_pairs={{0,1},{1,0},{2,3},{3,2},{4,5},{5,4},{6,7},{7,6},{8,9},{9,8},{10,11... | collective-permute-start | bytes 491528 | tf_op jit(solution)/shard_map/ppermute | solution.py:281
  63.6 2.2 %collective-permute-start.15 = (bf16[4,640,128]{2,1,0:T(8,128)(2,1)S(1)}, bf16[4,640,128]{2,1,0:T(8,128)(2,1)S(1)}, u32[]{:S(2)}, u32[]{:S(2)}) collective-permute-start(bf16[4,640,128]{2,1,0:T(8,128)(2,1)S(1)} %get-tuple-element.21), channel_id=1, source_target_pairs={{0,1},{1,0},{2,3},{3,2},{4,5},{5,4},{6,7},{7,6},{8,9},{9,8},{10,11... | collective-permute-start | bytes 1966088 | tf_op jit(solution)/shard_map/ppermute | solution.py:281
  65.9 5.5 %collective-permute-start.18 = (bf16[640,128]{1,0:T(8,128)(2,1)S(1)}, bf16[640,128]{1,0:T(8,128)(2,1)S(1)}, u32[]{:S(2)}, u32[]{:S(2)}) collective-permute-start(bf16[640,128]{1,0:T(8,128)(2,1)S(1)} %get-tuple-element.24), channel_id=1, source_target_pairs={{0,192},{64,0},{128,64},{192,128},{1,193},{65,1},{129,65},{193,129... | collective-permute-start | bytes 491528 | tf_op jit(solution)/shard_map/ppermute | solution.py:276
  66.8 6.9 %collective-permute-start.17 = (bf16[640,128]{1,0:T(8,128)(2,1)S(1)}, bf16[640,128]{1,0:T(8,128)(2,1)S(1)}, u32[]{:S(2)}, u32[]{:S(2)}) collective-permute-start(bf16[640,128]{1,0:T(8,128)(2,1)S(1)} %get-tuple-element.25), channel_id=1, source_target_pairs={{0,128},{64,192},{128,0},{192,64},{1,129},{65,193},{129,1},{193,65... | collective-permute-start | bytes 491528 | tf_op jit(solution)/shard_map/ppermute | solution.py:276
  67.6 10.3 %collective-permute-start.16 = (bf16[640,128]{1,0:T(8,128)(2,1)S(1)}, bf16[640,128]{1,0:T(8,128)(2,1)S(1)}, u32[]{:S(2)}, u32[]{:S(2)}) collective-permute-start(bf16[640,128]{1,0:T(8,128)(2,1)S(1)} %get-tuple-element.26), channel_id=1, source_target_pairs={{0,64},{64,128},{128,192},{192,0},{1,65},{65,129},{129,193},{193,1... | collective-permute-start | bytes 491528 | tf_op jit(solution)/shard_map/ppermute | solution.py:276
  80.3 25.9 %all-to-all-start.1 = ((bf16[64,32,128]{2,1,0:T(8,128)(2,1)}), bf16[64,32,128]{2,1,0:T(8,128)(2,1)S(1)}, u32[]{:S(2)}, u32[]{:S(2)}) async-start(bf16[64,32,128]{2,1,0:T(8,128)(2,1)} %place.1), calls=%async_computation.1 | async-start | bytes 1048576 | tf_op jit(solution)/shard_map/all_to_all | solution.py:296
  87.5 10.9 %collective-permute-start.11 = (bf16[2,128,512]{2,1,0:T(8,128)(2,1)S(1)}, bf16[2,128,512]{2,1,0:T(8,128)(2,1)S(1)}, u32[]{:S(2)}, u32[]{:S(2)}) collective-permute-start(bf16[2,128,512]{2,1,0:T(8,128)(2,1)S(1)} %get-tuple-element.14), channel_id=1, source_target_pairs={{0,0},{128,1},{2,2},{130,3},{4,4},{132,5},{6,6},{134,7},{1,64},{12... | collective-permute-start | bytes 786440 | tf_op jit(solution)/shard_map/ppermute | solution.py:356
  89.4 11.8 %collective-permute-start.12 = (bf16[2,128,512]{2,1,0:T(8,128)(2,1)S(1)}, bf16[2,128,512]{2,1,0:T(8,128)(2,1)S(1)}, u32[]{:S(2)}, u32[]{:S(2)}) collective-permute-start(bf16[2,128,512]{2,1,0:T(8,128)(2,1)S(1)} %get-tuple-element.15), channel_id=1, source_target_pairs={{1,0},{129,1},{3,2},{131,3},{5,4},{133,5},{7,6},{135,7},{64,64},{1... | collective-permute-start | bytes 786440 | tf_op jit(solution)/shard_map/ppermute | solution.py:356
  91.4 12.6 %collective-permute-start.13 = (bf16[2,128,512]{2,1,0:T(8,128)(2,1)S(1)}, bf16[2,128,512]{2,1,0:T(8,128)(2,1)S(1)}, u32[]{:S(2)}, u32[]{:S(2)}) collective-permute-start(bf16[2,128,512]{2,1,0:T(8,128)(2,1)S(1)} %get-tuple-element.16), channel_id=1, source_target_pairs={{64,0},{192,1},{66,2},{194,3},{68,4},{196,5},{70,6},{198,7},{65,64... | collective-permute-start | bytes 786440 | tf_op jit(solution)/shard_map/ppermute | solution.py:356
  95.4 9.8 %collective-permute-start.14 = (bf16[2,128,512]{2,1,0:T(8,128)(2,1)S(1)}, bf16[2,128,512]{2,1,0:T(8,128)(2,1)S(1)}, u32[]{:S(2)}, u32[]{:S(2)}) collective-permute-start(bf16[2,128,512]{2,1,0:T(8,128)(2,1)S(1)} %get-tuple-element.17), channel_id=1, source_target_pairs={{65,0},{193,1},{67,2},{195,3},{69,4},{197,5},{71,6},{199,7},{0,64}... | collective-permute-start | bytes 786440 | tf_op jit(solution)/shard_map/ppermute | solution.py:356

commit v4 on v3

v4 whole, which is shorter than its diff:
```python
import math

import jax
import jax.numpy as jnp
from jax import lax
from jax.experimental import pallas as pl
from jax.experimental.pallas import tpu as pltpu
from jax.sharding import PartitionSpec as P

HEAD_DIM = 128
BLOCK = 128
REACH = 4
NEAR = REACH + 1
SPAN = NEAR * BLOCK
LAYERS = 4
TILE = 16
CORES = 2
TILES = BLOCK // TILE // CORES
SCALE = HEAD_DIM ** (-0.5)
EXP2_SCALE = SCALE * math.log2(math.e)

masked_score = -1e30
bf16 = jnp.bfloat16
f32 = jnp.float32
ANY = pl.BlockSpec(memory_space=pl.ANY)
HBM = pl.BlockSpec(memory_space=pltpu.HBM)
VMEM = pl.BlockSpec(memory_space=pltpu.VMEM)
SMEM = pl.BlockSpec(memory_space=pltpu.SMEM)
PARAMS = pltpu.CompilerParams(vmem_limit_bytes=48 * 1024 * 1024)


def shape(*dims, dtype=bf16):
    return jax.ShapeDtypeStruct(dims, dtype)


def nt(a, b):
    return lax.dot_general(a, b, (((1,), (1,)), ((), ())), preferred_element_type=f32)


def nn(a, b):
    return lax.dot_general(a, b, (((1,), (0,)), ((), ())), preferred_element_type=f32)


def run_copies(pairs, sems, meanwhile=None):
    copies = [pltpu.make_async_copy(a, b, sems.at[i]) for i, (a, b) in enumerate(pairs)]
    for copy in copies:
        copy.start()
    if meanwhile is not None:
        meanwhile()
    for copy in copies:
        copy.wait()


def place_of():
    pipe = lax.axis_index("pipe")
    core = lax.rem(lax.axis_index("tp"), CORES)
    return pipe, core, lax.rem(pipe, 2) * CORES + core


def spread_kernel(key_in, value_in, sent, key, value, sems):
    ctx_count = sent.shape[0] // TILES
    run_copies([(key_in, key), (value_in, value)], sems)
    for x in range(TILES):
        for kind, rows in enumerate((key, value)):
            for j in range(2):
                head = 2 * x + j
                block = rows[:, head * HEAD_DIM:(head + 1) * HEAD_DIM]
                for c in range(ctx_count):
                    sent[c * TILES + x, kind, j] = block


def spread(key, value, ctx_count):
    return pl.pallas_call(
        spread_kernel,
        out_shape=shape(ctx_count * TILES, 2, 2, TILE, HEAD_DIM),
        in_specs=[HBM, HBM],
        out_specs=VMEM,
        scratch_shapes=[pltpu.VMEM(key.shape, bf16)] * 2 + [pltpu.SemaphoreType.DMA((2,))],
        compiler_params=PARAMS,
        name="spread",
    )(key, value)


def pieces_kernel(query, cot, p0, p1, p2, p3, sems):
    me = lax.axis_index("pipe")
    width = p0.shape[2]
    pairs = []
    for m, piece in enumerate((p0, p1, p2, p3)):
        column = pl.multiple_of(lax.rem(me + m, LAYERS) * width, width)
        for i, whole in enumerate((query, cot)):
            pairs.append((whole.at[:, pl.ds(column, width)], piece.at[i]))
    run_copies(pairs, sems)


def pieces_of(query, cot):
    rows, width = query.shape
    return pl.pallas_call(
        pieces_kernel,
        out_shape=(shape(2, rows, width // LAYERS),) * LAYERS,
        in_specs=[HBM, HBM],
        out_specs=(ANY,) * LAYERS,
        scratch_shapes=[pltpu.SemaphoreType.DMA((2 * LAYERS,))],
        compiler_params=PARAMS,
        name="pieces",
    )(query, cot)


def layers_kernel(
    bias_in, a0, a1, a2, a3, b0, b1, b2, b3, q0, q1, q2, q3,
    keep, give, og0, og1, og2, og3,
    bias, kv, qc, og, dkv, expo, queries, scale_rows, gs_all, ds_all, sems, out_sems,
):
    layers, _, rows, width = qc.shape
    heads = width // HEAD_DIM
    pipe, core, group = place_of()

    def back(start, d):
        return lax.rem(start + layers - d, layers)

    pairs = []
    for k in range(2):
        for d, x in enumerate((a0, a1, a2, a3)):
            pairs.append((x.at[:, k], kv.at[k, back(pipe, d), :, core]))
        for d, x in enumerate((b0, b1, b2, b3)):
            pairs.append((x.at[:, k], kv.at[k, back(pipe, d), :, 1 - core]))
    for m, x in enumerate((q0, q1, q2, q3)):
        pairs.append((x, qc.at[back(group, m)]))
    pairs.append((bias_in, bias))
    run_copies(pairs, sems)

    def cols(h):
        return slice(h * HEAD_DIM, (h + 1) * HEAD_DIM)

    def span(h):
        return slice(h * rows, (h + 1) * rows)

    def keys(l):
        return kv[0, l].reshape(SPAN, HEAD_DIM)

    def values(l):
        return kv[1, l].reshape(SPAN, HEAD_DIM)

    ones = jnp.ones((SPAN, HEAD_DIM), bf16)
    for l in range(layers):
        for h in range(heads):
            q = qc[l, 0, :, cols(h)]
            if l > 0:
                q = (q.astype(f32) + og[l - 1, 0, :, cols(h)].astype(f32)).astype(bf16)
            queries[l, span(h)] = q
            t = nt(q, keys(l)) * EXP2_SCALE + bias[...]
            e = jnp.exp2(t - jnp.max(t, axis=-1, keepdims=True)).astype(bf16)
            expo[l, span(h)] = e
            mixed = nn(e, jnp.concatenate([values(l), ones], axis=1))
            r = 1.0 / mixed[:, HEAD_DIM:]
            scale_rows[l, span(h)] = r
            og[l, 0, :, cols(h)] = (mixed[:, :HEAD_DIM] * r).astype(bf16)

    def probs_grad(l, h):
        g = qc[l, 1, :, cols(h)]
        if l < layers - 1:
            g = (g.astype(f32) + og[l + 1, 1, :, cols(h)].astype(f32)).astype(bf16)
        gs = (g.astype(f32) * scale_rows[l, span(h)]).astype(bf16)
        gs_all[l, span(h)] = gs
        delta = jnp.sum(gs.astype(f32) * og[l, 0, :, cols(h)].astype(f32), axis=-1, keepdims=True)
        return nt(gs, values(l)), delta

    def scores_grad(l, h, dp, delta):
        ds = (expo[l, span(h)].astype(f32) * (dp - delta)).astype(bf16)
        ds_all[l, span(h)] = ds
        return ds

    def query_grad(l, h, ds):
        og[l, 1, :, cols(h)] = (nn(ds, keys(l)) * SCALE).astype(bf16)
        if h == heads - 1:
            gk = nn(queries[l].T, ds_all[l]) * SCALE
            gv = nn(gs_all[l].T, expo[l])
            dkv[0, l] = gk.T.astype(bf16).reshape(NEAR * TILES, CORES, TILE, HEAD_DIM)
            dkv[1, l] = gv.T.astype(bf16).reshape(NEAR * TILES, CORES, TILE, HEAD_DIM)

    steps = [(l, h) for l in reversed(range(layers)) for h in range(heads)]
    first, second = {}, {}
    for i in range(len(steps) + 2):
        if i < len(steps):
            first[i] = probs_grad(*steps[i])
        if 1 <= i <= len(steps):
            second[i - 1] = scores_grad(*steps[i - 1], *first.pop(i - 1))
        if i >= 2:
            query_grad(*steps[i - 2], second.pop(i - 2))

    pairs = []
    for d in range(layers):
        l = lax.rem(pipe + d, layers)
        for k in range(2):
            pairs.append((dkv.at[k, l, :, 1 - core], give.at[d, k]))
            pairs.append((dkv.at[k, l, :, core], keep.at[d, k]))
    for m, x in enumerate((og0, og1, og2, og3)):
        pairs.append((og.at[back(group, m)], x))
    run_copies(pairs, out_sems)


def run_layers(bias, mine, theirs, qc_parts):
    _, rows, width = qc_parts[0].shape
    stacked = rows * width // HEAD_DIM
    kv_shape = shape(LAYERS, 2, NEAR * TILES, TILE, HEAD_DIM)
    return pl.pallas_call(
        layers_kernel,
        out_shape=(kv_shape, kv_shape) + (shape(2, rows, width),) * LAYERS,
        in_specs=[ANY] * 13,
        out_specs=(ANY,) * 6,
        scratch_shapes=[
            pltpu.VMEM((rows, SPAN), f32),
            pltpu.VMEM((2, LAYERS, NEAR * TILES, CORES, TILE, HEAD_DIM), bf16),
            pltpu.VMEM((LAYERS, 2, rows, width), bf16),
            pltpu.VMEM((LAYERS, 2, rows, width), bf16),
            pltpu.VMEM((2, LAYERS, NEAR * TILES, CORES, TILE, HEAD_DIM), bf16),
            pltpu.VMEM((LAYERS, stacked, SPAN), bf16),
            pltpu.VMEM((LAYERS, stacked, HEAD_DIM), bf16),
            pltpu.VMEM((LAYERS, stacked, HEAD_DIM), f32),
            pltpu.VMEM((LAYERS, stacked, HEAD_DIM), bf16),
            pltpu.VMEM((LAYERS, stacked, SPAN), bf16),
            pltpu.SemaphoreType.DMA((21,)),
            pltpu.SemaphoreType.DMA((20,)),
        ],
        compiler_params=PARAMS,
        name="layers",
    )(bias, *mine, *theirs, *qc_parts)


def place_kernel(order, p0, p1, p2, p3, sent, parts, sems):
    pipe, _, _ = place_of()

    def clear():
        sent[...] = jnp.zeros(sent.shape, bf16)

    run_copies(
        [
            (x, parts.at[lax.rem(pipe + LAYERS - d, LAYERS)])
            for d, x in enumerate((p0, p1, p2, p3))
        ],
        sems,
        clear,
    )
    first = order[lax.axis_index("ctx")] - REACH
    for c in range(sent.shape[0] // TILES):
        j = order[c] - first

        @pl.when((j >= 0) & (j <= REACH))
        def _():
            at = pl.ds(j * TILES, TILES)
            for head in range(2):
                total = parts[2 * head, :, at].astype(f32) + parts[2 * head + 1, :, at].astype(f32)
                total = total.astype(bf16)
                for k in range(2):
                    sent[c * TILES:(c + 1) * TILES, k, head] = total[k]


def place(order, parts):
    return pl.pallas_call(
        place_kernel,
        out_shape=shape(order.shape[0] * TILES, 2, 2, TILE, HEAD_DIM),
        in_specs=[SMEM] + [ANY] * LAYERS,
        out_specs=VMEM,
        scratch_shapes=[
            pltpu.VMEM((LAYERS,) + parts[0].shape, bf16), pltpu.SemaphoreType.DMA((LAYERS,))
        ],
        compiler_params=PARAMS,
        name="place",
    )(order, *parts)


def total_kernel(got_in, grad_key, grad_value, got, sem):
    copy = pltpu.make_async_copy(got_in, got, sem)
    copy.start()
    copy.wait()
    for x in range(TILES):
        total = got[x].astype(f32)
        for c in range(1, got.shape[0] // TILES):
            total = total + got[c * TILES + x].astype(f32)
        total = total.astype(bf16)
        for kind, whole in enumerate((grad_key, grad_value)):
            for j in range(2):
                head = 2 * x + j
                whole[:, head * HEAD_DIM:(head + 1) * HEAD_DIM] = total[kind, j]


def total(got):
    return pl.pallas_call(
        total_kernel,
        out_shape=(shape(TILE, TILES * 2 * HEAD_DIM),) * 2,
        in_specs=[ANY],
        out_specs=(VMEM, VMEM),
        scratch_shapes=[pltpu.VMEM(got.shape, bf16), pltpu.SemaphoreType.DMA],
        compiler_params=PARAMS,
        name="total",
    )(got)


def assemble_kernel(g0, g1, g2, g3, out, grad_query, sems):
    me = lax.axis_index("pipe")
    width = g0.shape[2]
    pairs = []
    for m, piece in enumerate((g0, g1, g2, g3)):
        column = pl.multiple_of(lax.rem(me + m, LAYERS) * width, width)
        for i, whole in enumerate((out, grad_query)):
            pairs.append((piece.at[i], whole.at[:, pl.ds(column, width)]))
    run_copies(pairs, sems)


def assemble(pieces):
    _, rows, width = pieces[0].shape
    return pl.pallas_call(
        assemble_kernel,
        out_shape=(shape(rows, LAYERS * width),) * 2,
        in_specs=[ANY] * 4,
        out_specs=(ANY, ANY),
        scratch_shapes=[pltpu.SemaphoreType.DMA((8,))],
        compiler_params=PARAMS,
        name="assemble",
    )(*pieces)


def moved(block, distance):
    size = lax.axis_size("pipe")
    return lax.ppermute(block, "pipe", [(i, (i + distance) % size) for i in range(size)])


def swapped(block):
    size = lax.axis_size("tp")
    return lax.ppermute(block, "tp", [(i, i ^ 1) for i in range(size)])


def group_pairs(m):
    tp_count = lax.axis_size("tp")
    pairs = []
    for l in range(LAYERS):
        for tp in range(tp_count):
            group = (l + m) % LAYERS
            pipe = 2 * (tp % 2) + group // 2
            pairs.append((l * tp_count + tp, pipe * tp_count + tp - tp % 2 + group % 2))
    return pairs


def exchanged(block):
    ctx_count, tp_count = lax.axis_size("ctx"), lax.axis_size("tp")
    groups = [
        [c * tp_count + tp for c in range(ctx_count) for tp in range(core, tp_count, CORES)]
        for core in range(CORES)
    ]
    flat = block.reshape(block.shape[0], -1, HEAD_DIM)
    got = lax.all_to_all(
        flat, ("ctx", "tp"), split_axis=0, concat_axis=0, axis_index_groups=groups, tiled=True
    )
    return got.reshape(block.shape)


def cut(block, starts, sizes):
    return lax.dynamic_slice(block, starts, sizes, allow_negative_indices=False)


def shards(query_in, key_in, value_in, doc_ids, stretch_order, out_cot):
    ctx_count = lax.axis_size("ctx")
    layer = lax.axis_index("pipe")
    rows = query_in.shape[1]

    got = exchanged(spread(key_in[0], value_in[0], ctx_count))
    qc_parts = [
        lax.ppermute(piece, ("pipe", "tp"), group_pairs(m))
        for m, piece in enumerate(pieces_of(query_in[0], out_cot[0]))
    ]

    position = stretch_order[lax.axis_index("ctx")]
    block_ids = jnp.arange(ctx_count, dtype=jnp.int32)
    wanted = jnp.maximum(position - REACH + jnp.arange(NEAR, dtype=jnp.int32), 0)
    holder = jnp.sum(
        jnp.where(stretch_order[None, :] == wanted[:, None], block_ids[None, :], 0), axis=1
    )

    def window(distance):
        head = lax.rem(layer + distance, LAYERS) // 2
        return jnp.concatenate(
            [
                cut(got, (holder[j] * TILES, 0, head, 0, 0), (TILES, 2, 1, TILE, HEAD_DIM))
                for j in range(NEAR)
            ]
        ).reshape(NEAR * TILES, 2, TILE, HEAD_DIM)

    mine = [window(0)] + [moved(window(d), d) for d in (1, 3, 2)]
    mine = [mine[0], mine[1], mine[3], mine[2]]
    theirs = [swapped(x) for x in mine]

    offsets = jnp.arange(SPAN, dtype=jnp.int32)
    row_ids = jnp.arange(rows, dtype=jnp.int32)
    documents = jnp.concatenate([jnp.full((REACH * BLOCK,), -1, jnp.int32), doc_ids])
    near_documents = cut(documents, (position * BLOCK,), (SPAN,))
    own_documents = near_documents[REACH * BLOCK:]
    allowed = (offsets[None, :] <= row_ids[:, None] + REACH * BLOCK) & (
        near_documents[None, :] == own_documents[:, None]
    )
    bias = jnp.where(allowed, 0.0, masked_score).astype(f32)

    keep, give, *groups = run_layers(bias, mine, theirs, qc_parts)
    received = swapped(give)
    sums = [
        (keep[d].astype(f32) + received[d].astype(f32)).astype(bf16) for d in range(LAYERS)
    ]
    parts = [sums[0]] + [moved(sums[d], d) for d in (1, 3, 2)]
    parts = [parts[0], parts[1], parts[3], parts[2]]
    grad_key, grad_value = total(exchanged(place(stretch_order, parts)))
    out, grad_query = assemble(
        [
            lax.ppermute(x, ("pipe", "tp"), [(b, a) for a, b in group_pairs(m)])
            for m, x in enumerate(groups)
        ]
    )
    return (out[None], grad_query[None], grad_key[None], grad_value[None])


def solution(mesh):
    return jax.shard_map(
        shards,
        mesh=mesh,
        in_specs=(
            P("pipe", "ctx", "tp"),
            P("pipe", ("ctx", "tp"), None),
            P("pipe", ("ctx", "tp"), None),
            P(),
            P(),
            P("pipe", "ctx", "tp"),
        ),
        out_specs=(
            P("pipe", "ctx", "tp"),
            P("pipe", "ctx", "tp"),
            P("pipe", ("ctx", "tp"), None),
            P("pipe", ("ctx", "tp"), None),
        ),
        check_vma=False,
    )
```

time: 108 us -> 98.5 us (0.912)
  Pallas kernels: 18.6 us -> 11.9 us
  waiting for transfers between devices: 24.6 us -> 19.4 us
  starting transfers between devices: 53.8 us -> 56.7 us
    pallas_call x1, Pallas kernels: 13.5 us -> 6.48 us  [run_layers(): pl.pallas_call(layers_kernel, out_shape=(kv_shape, kv_shape) + (shape(2,...]
    ppermute x5, starting transfers between devices: 5.05 us -> 8.04 us  [swapped(): return lax.ppermute(block, 'tp', [(i, i ^ 1) for i in range(size)])]
    all_to_all x2, starting transfers between devices: 20.3 us -> 17.5 us  [exchanged(): lax.all_to_all(flat, ('ctx', 'tp'), split_axis=0, concat_axis=0, axis_ind...]
    ppermute x6, waiting for transfers between devices: 11.6 us -> 9.08 us  [moved(): lax.ppermute(block, 'pipe', [(i, (i + distance) % size) for i in range(si...]
    ppermute x4, starting transfers between devices: 9.8 us -> 11.8 us  [shards(): lax.ppermute(x, ('pipe', 'tp'), [(b, a) for a, b in group_pairs(m)])]
    all_to_all x2, waiting for transfers between devices: 2.52 us -> 0.57 us  [exchanged(): lax.all_to_all(flat, ('ctx', 'tp'), split_axis=0, concat_axis=0, axis_ind...]
    pallas_call x3 -> x4, Pallas kernels: 4.11 us -> 4.38 us  [the longest x1 2.45 us: place(): pl.pallas_call(place_kernel, out_shape=shape(order.shape[0] * TILES, 2, 2...]
  transfers between devices with their start and end apart: 21 -> 21, of which waited for: 11 -> 9; matrix products, arithmetic and copies ran while one was open for 2% -> 2% of each run, Pallas kernels for 1% -> 1%
where the time goes in v4:
time: 98.5 us; the launch traced here: 97.9 us
  starting transfers between devices  56.7 us (58%)
  waiting for transfers between devices  19.4 us (20%)
  Pallas kernels  11.9 us (12%)
  between operations  5.72 us (6%)
  local copies, waits for them, and re-layouts  3.65 us (4%)
    all_to_all x2, starting transfers between devices, exchanged(): lax.all_to_all(flat, ('ctx', 'tp'), split_axis=0, concat_axis=0, axis_ind...  17.5 us
    ppermute x4, starting transfers between devices, shards(): lax.ppermute(piece, ('pipe', 'tp'), group_pairs(m))  12.5 us
    ppermute x4, starting transfers between devices, shards(): lax.ppermute(x, ('pipe', 'tp'), [(b, a) for a, b in group_pairs(m)])  11.8 us
    ppermute x6, waiting for transfers between devices, moved(): lax.ppermute(block, 'pipe', [(i, (i + distance) % size) for i in range(si...  9.08 us
    ppermute x5, starting transfers between devices, swapped(): return lax.ppermute(block, 'tp', [(i, i ^ 1) for i in range(size)])  8.04 us
    ppermute x4, waiting for transfers between devices, shards(): lax.ppermute(x, ('pipe', 'tp'), [(b, a) for a, b in group_pairs(m)])  7.19 us
    ppermute x6, starting transfers between devices, moved(): lax.ppermute(block, 'pipe', [(i, (i + distance) % size) for i in range(si...  6.87 us
    pallas_call x1, Pallas kernels, run_layers(): pl.pallas_call(layers_kernel, out_shape=(kv_shape, kv_shape) + (shape(2,...  6.48 us
  transfers between devices with their start and end apart: 21, of which 9 were waited for; matrix products, arithmetic and copies ran while one was open for 2% of the time, Pallas kernels for 1%

profile of v4, /device:TPU:1, one launch (start us, length us, event | category | flops | bytes accessed | tf_op | source)
XLA Modules:
  0.0 97.9 jit_solution(2627414007570483828)
XLA Ops:
  0.6 0.7 copy-done.2
  1.4 0.8 copy-done.3
  2.1 0.9 spread.1
  3.1 12.0 %all-to-all-start = ((bf16[32,64,128]{2,1,0:T(8,128)(2,1)}), bf16[32,64,128]{2,1,0:T(8,128)(2,1)S(1)}, u32[]{:S(2)}, u32[]{:S(2)}) async-start(bf16[32,64,128]{2,1,0:T(8,128)(2,1)} %bitcast.3), calls=%async_computation | async-start | bytes 1048576 | tf_op jit(solution)/shard_map/all_to_all | solution.py:350
  15.4 5.7 %collective-permute-start.7 = (bf16[2,128,512]{2,1,0:T(8,128)(2,1)S(1)}, bf16[2,128,512]{2,1,0:T(8,128)(2,1)S(1)}, u32[]{:S(2)}, u32[]{:S(2)}) collective-permute-start(bf16[2,128,512]{2,1,0:T(8,128)(2,1)S(1)} %get-tuple-element.18), channel_id=1, source_target_pairs={{0,0},{1,128},{2,2},{3,130},{4,4},{5,132},{6,6},{7,134},{64,1},{65... | collective-permute-start | bytes 786440 | tf_op jit(solution)/shard_map/ppermute | solution.py:367
  21.1 2.9 %collective-permute-start.8 = (bf16[2,128,512]{2,1,0:T(8,128)(2,1)S(1)}, bf16[2,128,512]{2,1,0:T(8,128)(2,1)S(1)}, u32[]{:S(2)}, u32[]{:S(2)}) collective-permute-start(bf16[2,128,512]{2,1,0:T(8,128)(2,1)S(1)} %get-tuple-element.19), channel_id=1, source_target_pairs={{0,1},{1,129},{2,3},{3,131},{4,5},{5,133},{6,7},{7,135},{64,64},{6... | collective-permute-start | bytes 786440 | tf_op jit(solution)/shard_map/ppermute | solution.py:367
  26.9 0.7 fusion.6
  31.6 3.0 %collective-permute-start.1 = (bf16[20,2,16,128]{3,2,1,0:T(8,128)(2,1)S(1)}, bf16[20,2,16,128]{3,2,1,0:T(8,128)(2,1)S(1)}, u32[]{:S(2)}, u32[]{:S(2)}) collective-permute-start(bf16[20,2,16,128]{3,2,1,0:T(8,128)(2,1)S(1)} %bitcast.84), channel_id=1, source_target_pairs={{0,128},{64,192},{128,0},{192,64},{1,129},{65,193},{129,1},{193,65... | collective-permute-start | bytes 491528 | tf_op jit(solution)/shard_map/ppermute | solution.py:324
  34.6 0.8 collective-permute-start.2
  35.4 0.7 collective-permute-start
  36.1 3.9 %collective-permute-start.10 = (bf16[2,128,512]{2,1,0:T(8,128)(2,1)S(1)}, bf16[2,128,512]{2,1,0:T(8,128)(2,1)S(1)}, u32[]{:S(2)}, u32[]{:S(2)}) collective-permute-start(bf16[2,128,512]{2,1,0:T(8,128)(2,1)S(1)} %get-tuple-element.21), channel_id=1, source_target_pairs={{0,65},{1,193},{2,67},{3,195},{4,69},{5,197},{6,71},{7,199},{64,0}... | collective-permute-start | bytes 786440 | tf_op jit(solution)/shard_map/ppermute | solution.py:367
  40.1 1.3 %collective-permute-start.3 = (bf16[20,2,16,128]{3,2,1,0:T(8,128)(2,1)S(1)}, bf16[20,2,16,128]{3,2,1,0:T(8,128)(2,1)S(1)}, u32[]{:S(2)}, u32[]{:S(2)}) collective-permute-start(bf16[20,2,16,128]{3,2,1,0:T(8,128)(2,1)S(1)} %bitcast.74), channel_id=1, source_target_pairs={{0,1},{1,0},{2,3},{3,2},{4,5},{5,4},{6,7},{7,6},{8,9},{9,8},{10,11... | collective-permute-start | bytes 491528 | tf_op jit(solution)/shard_map/ppermute | solution.py:329
  42.0 2.2 %collective-permute-start.6 = (bf16[20,2,16,128]{3,2,1,0:T(8,128)(2,1)S(1)}, bf16[20,2,16,128]{3,2,1,0:T(8,128)(2,1)S(1)}, u32[]{:S(2)}, u32[]{:S(2)}) collective-permute-start(bf16[20,2,16,128]{3,2,1,0:T(8,128)(2,1)S(1)} %collective-permute-done.2.a3), channel_id=1, source_target_pairs={{0,1},{1,0},{2,3},{3,2},{4,5},{5,4},{6,7},{7,6},{8,9},{9,8},{10,11... | collective-permute-start | bytes 491528 | tf_op jit(solution)/shard_map/ppermute | solution.py:329
  44.3 3.4 %collective-permute-start.4 = (bf16[20,2,16,128]{3,2,1,0:T(8,128)(2,1)S(1)}, bf16[20,2,16,128]{3,2,1,0:T(8,128)(2,1)S(1)}, u32[]{:S(2)}, u32[]{:S(2)}) collective-permute-start(bf16[20,2,16,128]{3,2,1,0:T(8,128)(2,1)S(1)} %collective-permute-done.a1), channel_id=1, source_target_pairs={{0,1},{1,0},{2,3},{3,2},{4,5},{5,4},{6,7},{7,6},{8,9},{9,8},{10,11... | collective-permute-start | bytes 491528 | tf_op jit(solution)/shard_map/ppermute | solution.py:329
  47.8 0.9 collective-permute-done.4.b1
  48.7 6.5 %layers.1 = (bf16[4,2,20,16,128]{4,3,2,1,0:T(8,128)(2,1)S(1)}, bf16[4,2,20,16,128]{4,3,2,1,0:T(8,128)(2,1)S(1)}, bf16[2,128,512]{2,1,0:T(8,128)(2,1)S(1)}, bf16[...) custom-call(f32[128,640]{1,0:T(8,128)S(1)} %fusion.1.bias_in, ...), custom_call_target="tpu_custom_call" | custom-call | tf_op jit(solution)/shard_map/layers/pallas_call | solution.py:205
  55.6 1.7 %collective-permute-done.15 = bf16[4,2,20,16,128]{4,3,2,1,0:T(8,128)(2,1)S(1)} collective-permute-done((bf16[4,2,20,16,128]{4,3,2,1,0:T(8,128)(2,1)S(1)}, bf16[4,2,20,16,128]{4,3,2,1,0:T(8,128)(2,1)S(1)}, u32[]{:S(2)}, u32[]{:S(2)}) %collective-permute-start.15) | collective-permute-done | bytes 655392 | tf_op jit(solution)/shard_map/ppermute | solution.py:329
  58.0 1.9 %collective-permute-start.17 = (bf16[2,20,16,128]{3,2,1,0:T(8,128)(2,1)S(1)}, bf16[2,20,16,128]{3,2,1,0:T(8,128)(2,1)S(1)}, u32[]{:S(2)}, u32[]{:S(2)}) collective-permute-start(bf16[2,20,16,128]{3,2,1,0:T(8,128)(2,1)S(1)} %get-tuple-element.33), channel_id=1, source_target_pairs={{0,128},{64,192},{128,0},{192,64},{1,129},{65,193},{129,1},{193,65... | collective-permute-start | bytes 491528 | tf_op jit(solution)/shard_map/ppermute | solution.py:324
  60.0 3.1 %collective-permute-done.18.p3 = bf16[2,20,16,128]{3,2,1,0:T(8,128)(2,1)S(1)} collective-permute-done((bf16[2,20,16,128]{3,2,1,0:T(8,128)(2,1)S(1)}, bf16[2,20,16,128]{3,2,1,0:T(8,128)(2,1)S(1)}, u32[]{:S(2)}, u32[]{:S(2)}) %collective-permute-start.18) | collective-permute-done | bytes 163872 | tf_op jit(solution)/shard_map/ppermute | solution.py:324
  63.0 1.7 %collective-permute-done.17.p2 = bf16[2,20,16,128]{3,2,1,0:T(8,128)(2,1)S(1)} collective-permute-done((bf16[2,20,16,128]{3,2,1,0:T(8,128)(2,1)S(1)}, bf16[2,20,16,128]{3,2,1,0:T(8,128)(2,1)S(1)}, u32[]{:S(2)}, u32[]{:S(2)}) %collective-permute-start.17) | collective-permute-done | bytes 163872 | tf_op jit(solution)/shard_map/ppermute | solution.py:324
  64.8 4.2 %collective-permute-done.16.p1 = bf16[2,20,16,128]{3,2,1,0:T(8,128)(2,1)S(1)} collective-permute-done((bf16[2,20,16,128]{3,2,1,0:T(8,128)(2,1)S(1)}, bf16[2,20,16,128]{3,2,1,0:T(8,128)(2,1)S(1)}, u32[]{:S(2)}, u32[]{:S(2)}) %collective-permute-start.16) | collective-permute-done | bytes 163872 | tf_op jit(solution)/shard_map/ppermute | solution.py:324
  69.0 2.4 %place.1 = bf16[32,2,2,16,128]{4,3,2,1,0:T(8,128)(2,1)} custom-call(s32[8]{0:T(128)S(1)} %copy-done.4, bf16[2,20,16,128]{3,2,1,0:T(8,128)(2,1)S(1)} %get-tuple-element.35.p0, bf16[2,20,16,128]{3,2,1,0:T(8,128)(2,1)S(1)} %collective-permute-done.16.p1, bf16[2,20,16,128]{3,2,1,0:T(8,128)(2,1)S(1)} %collective-permute-done.17.p2, ...), custom_call_target="tpu_custom_call" | custom-call | tf_op jit(solution)/shard_map/place/pallas_call | solution.py:258
  71.5 5.5 %all-to-all-start.1 = ((bf16[32,64,128]{2,1,0:T(8,128)(2,1)}), bf16[32,64,128]{2,1,0:T(8,128)(2,1)S(1)}, u32[]{:S(2)}, u32[]{:S(2)}) async-start(bf16[32,64,128]{2,1,0:T(8,128)(2,1)} %bitcast.23), calls=%async_computation.1 | async-start | bytes 1048576 | tf_op jit(solution)/shard_map/all_to_all | solution.py:350
  76.9 4.5 %collective-permute-start.11 = (bf16[2,128,512]{2,1,0:T(8,128)(2,1)S(1)}, bf16[2,128,512]{2,1,0:T(8,128)(2,1)S(1)}, u32[]{:S(2)}, u32[]{:S(2)}) collective-permute-start(bf16[2,128,512]{2,1,0:T(8,128)(2,1)S(1)} %get-tuple-element.22), channel_id=1, source_target_pairs={{0,0},{128,1},{2,2},{130,3},{4,4},{132,5},{6,6},{134,7},{1,64},{12... | collective-permute-start | bytes 786440 | tf_op jit(solution)/shard_map/ppermute | solution.py:411
  81.5 1.9 %collective-permute-start.12 = (bf16[2,128,512]{2,1,0:T(8,128)(2,1)S(1)}, bf16[2,128,512]{2,1,0:T(8,128)(2,1)S(1)}, u32[]{:S(2)}, u32[]{:S(2)}) collective-permute-start(bf16[2,128,512]{2,1,0:T(8,128)(2,1)S(1)} %get-tuple-element.23), channel_id=1, source_target_pairs={{1,0},{129,1},{3,2},{131,3},{5,4},{133,5},{7,6},{135,7},{64,64},{1... | collective-permute-start | bytes 786440 | tf_op jit(solution)/shard_map/ppermute | solution.py:411
  83.4 2.4 %collective-permute-start.13 = (bf16[2,128,512]{2,1,0:T(8,128)(2,1)S(1)}, bf16[2,128,512]{2,1,0:T(8,128)(2,1)S(1)}, u32[]{:S(2)}, u32[]{:S(2)}) collective-permute-start(bf16[2,128,512]{2,1,0:T(8,128)(2,1)S(1)} %get-tuple-element.24), channel_id=1, source_target_pairs={{64,0},{192,1},{66,2},{194,3},{68,4},{196,5},{70,6},{198,7},{65,64... | collective-permute-start | bytes 786440 | tf_op jit(solution)/shard_map/ppermute | solution.py:411
  85.8 2.9 %collective-permute-start.14 = (bf16[2,128,512]{2,1,0:T(8,128)(2,1)S(1)}, bf16[2,128,512]{2,1,0:T(8,128)(2,1)S(1)}, u32[]{:S(2)}, u32[]{:S(2)}) collective-permute-start(bf16[2,128,512]{2,1,0:T(8,128)(2,1)S(1)} %get-tuple-element.25), channel_id=1, source_target_pairs={{65,0},{193,1},{67,2},{195,3},{69,4},{197,5},{71,6},{199,7},{0,64}... | collective-permute-start | bytes 786440 | tf_op jit(solution)/shard_map/ppermute | solution.py:411
  88.8 3.3 %collective-permute-done.12.g1 = bf16[2,128,512]{2,1,0:T(8,128)(2,1)S(1)} collective-permute-done((bf16[2,128,512]{2,1,0:T(8,128)(2,1)S(1)}, bf16[2,128,512]{2,1,0:T(8,128)(2,1)S(1)}, u32[]{:S(2)}, u32[]{:S(2)}) %collective-permute-start.12) | collective-permute-done | bytes 262176 | tf_op jit(solution)/shard_map/ppermute | solution.py:411
  92.1 2.5 %collective-permute-done.13.g2 = bf16[2,128,512]{2,1,0:T(8,128)(2,1)S(1)} collective-permute-done((bf16[2,128,512]{2,1,0:T(8,128)(2,1)S(1)}, bf16[2,128,512]{2,1,0:T(8,128)(2,1)S(1)}, u32[]{:S(2)}, u32[]{:S(2)}) %collective-permute-start.13) | collective-permute-done | bytes 262176 | tf_op jit(solution)/shard_map/ppermute | solution.py:411
  94.6 1.3 %collective-permute-done.14.g3 = bf16[2,128,512]{2,1,0:T(8,128)(2,1)S(1)} collective-permute-done((bf16[2,128,512]{2,1,0:T(8,128)(2,1)S(1)}, bf16[2,128,512]{2,1,0:T(8,128)(2,1)S(1)}, u32[]{:S(2)}, u32[]{:S(2)}) %collective-permute-start.14) | collective-permute-done | bytes 262176 | tf_op jit(solution)/shard_map/ppermute | solution.py:411
  95.9 1.0 %assemble.1 = (bf16[128,2048]{1,0:T(8,128)(2,1)}, bf16[128,2048]{1,0:T(8,128)(2,1)}) custom-call(bf16[2,128,512]{2,1,0:T(8,128)(2,1)S(1)} %collective-permute-done.11.g0, bf16[2,128,512]{2,1,0:T(8,128)(2,1)S(1)} %collective-permute-done.12.g1, bf16[2,128,512]{2,1,0:T(8,128)(2,1)S(1)} %collective-permute-done.13.g2, ...), custom_call_target="tpu_custom_call" | custom-call | tf_op jit(solution)/shard_map/assemble/pallas_call | solution.py:311
  97.0 0.7 total.1
  (42 shorter events, 4.5 us)
Async XLA Ops:
  0.6 0.8 copy-start.2
  1.4 0.8 copy-start.3
  3.1 12.0 %copy-start = (bf16[1,128,2048]{2,1,0:T(8,128)(2,1)S(1)}, bf16[1,128,2048]{2,1,0:T(8,128)(2,1)}, u32[]{:S(2)}) copy-start(bf16[1,128,2048]{2,1,0:T(8,128)(2,1)} %param.6) | copy-start | bytes 1572868
  3.1 12.0 %copy-start.1 = (bf16[1,128,2048]{2,1,0:T(8,128)(2,1)S(1)}, bf16[1,128,2048]{2,1,0:T(8,128)(2,1)}, u32[]{:S(2)}) copy-start(bf16[1,128,2048]{2,1,0:T(8,128)(2,1)} %param.11) | copy-start | bytes 1572868
  3.1 28.3 %all-to-all-start = ((bf16[32,64,128]{2,1,0:T(8,128)(2,1)}), bf16[32,64,128]{2,1,0:T(8,128)(2,1)S(1)}, u32[]{:S(2)}, u32[]{:S(2)}) async-start(bf16[32,64,128]{2,1,0:T(8,128)(2,1)} %bitcast.3), calls=%async_computation | async-start | bytes 1048576 | tf_op jit(solution)/shard_map/all_to_all | solution.py:350
  15.4 20.0 %collective-permute-start.7 = (bf16[2,128,512]{2,1,0:T(8,128)(2,1)S(1)}, bf16[2,128,512]{2,1,0:T(8,128)(2,1)S(1)}, u32[]{:S(2)}, u32[]{:S(2)}) collective-permute-start(bf16[2,128,512]{2,1,0:T(8,128)(2,1)S(1)} %get-tuple-element.18), channel_id=1, source_target_pairs={{0,0},{1,128},{2,2},{3,130},{4,4},{5,132},{6,6},{7,134},{64,1},{65... | collective-permute-start | bytes 786440 | tf_op jit(solution)/shard_map/ppermute | solution.py:367
  21.1 15.1 %collective-permute-start.8 = (bf16[2,128,512]{2,1,0:T(8,128)(2,1)S(1)}, bf16[2,128,512]{2,1,0:T(8,128)(2,1)S(1)}, u32[]{:S(2)}, u32[]{:S(2)}) collective-permute-start(bf16[2,128,512]{2,1,0:T(8,128)(2,1)S(1)} %get-tuple-element.19), channel_id=1, source_target_pairs={{0,1},{1,129},{2,3},{3,131},{4,5},{5,133},{6,7},{7,135},{64,64},{6... | collective-permute-start | bytes 786440 | tf_op jit(solution)/shard_map/ppermute | solution.py:367
  24.0 16.1 %collective-permute-start.9 = (bf16[2,128,512]{2,1,0:T(8,128)(2,1)S(1)}, bf16[2,128,512]{2,1,0:T(8,128)(2,1)S(1)}, u32[]{:S(2)}, u32[]{:S(2)}) collective-permute-start(bf16[2,128,512]{2,1,0:T(8,128)(2,1)S(1)} %get-tuple-element.20), channel_id=1, source_target_pairs={{0,64},{1,192},{2,66},{3,194},{4,68},{5,196},{6,70},{7,198},{64,65... | collective-permute-start | bytes 786440 | tf_op jit(solution)/shard_map/ppermute | solution.py:367
  24.2 0.7 copy-start.4
  31.6 9.8 %collective-permute-start.1 = (bf16[20,2,16,128]{3,2,1,0:T(8,128)(2,1)S(1)}, bf16[20,2,16,128]{3,2,1,0:T(8,128)(2,1)S(1)}, u32[]{:S(2)}, u32[]{:S(2)}) collective-permute-start(bf16[20,2,16,128]{3,2,1,0:T(8,128)(2,1)S(1)} %bitcast.84), channel_id=1, source_target_pairs={{0,128},{64,192},{128,0},{192,64},{1,129},{65,193},{129,1},{193,65... | collective-permute-start | bytes 491528 | tf_op jit(solution)/shard_map/ppermute | solution.py:324
  34.6 1.5 %copy-start.5 = (s32[1024]{0:T(1024)S(1)}, s32[1024]{0:T(1024)}, u32[]{:S(2)}) copy-start(s32[1024]{0:T(1024)} %param.9) | copy-start | bytes 12292
  34.6 7.4 %collective-permute-start.2 = (bf16[20,2,16,128]{3,2,1,0:T(8,128)(2,1)S(1)}, bf16[20,2,16,128]{3,2,1,0:T(8,128)(2,1)S(1)}, u32[]{:S(2)}, u32[]{:S(2)}) collective-permute-start(bf16[20,2,16,128]{3,2,1,0:T(8,128)(2,1)S(1)} %bitcast.83), channel_id=1, source_target_pairs={{0,192},{64,0},{128,64},{192,128},{1,193},{65,1},{129,65},{193,129... | collective-permute-start | bytes 491528 | tf_op jit(solution)/shard_map/ppermute | solution.py:324
  35.4 8.9 %collective-permute-start = (bf16[20,2,16,128]{3,2,1,0:T(8,128)(2,1)S(1)}, bf16[20,2,16,128]{3,2,1,0:T(8,128)(2,1)S(1)}, u32[]{:S(2)}, u32[]{:S(2)}) collective-permute-start(bf16[20,2,16,128]{3,2,1,0:T(8,128)(2,1)S(1)} %bitcast.85), channel_id=1, source_target_pairs={{0,64},{64,128},{128,192},{192,0},{1,65},{65,129},{129,193},{193,1... | collective-permute-start | bytes 491528 | tf_op jit(solution)/shard_map/ppermute | solution.py:324
  36.1 11.6 %collective-permute-start.10 = (bf16[2,128,512]{2,1,0:T(8,128)(2,1)S(1)}, bf16[2,128,512]{2,1,0:T(8,128)(2,1)S(1)}, u32[]{:S(2)}, u32[]{:S(2)}) collective-permute-start(bf16[2,128,512]{2,1,0:T(8,128)(2,1)S(1)} %get-tuple-element.21), channel_id=1, source_target_pairs={{0,65},{1,193},{2,67},{3,195},{4,69},{5,197},{6,71},{7,199},{64,0}... | collective-permute-start | bytes 786440 | tf_op jit(solution)/shard_map/ppermute | solution.py:367
  40.1 7.7 %collective-permute-start.3 = (bf16[20,2,16,128]{3,2,1,0:T(8,128)(2,1)S(1)}, bf16[20,2,16,128]{3,2,1,0:T(8,128)(2,1)S(1)}, u32[]{:S(2)}, u32[]{:S(2)}) collective-permute-start(bf16[20,2,16,128]{3,2,1,0:T(8,128)(2,1)S(1)} %bitcast.74), channel_id=1, source_target_pairs={{0,1},{1,0},{2,3},{3,2},{4,5},{5,4},{6,7},{7,6},{8,9},{9,8},{10,11... | collective-permute-start | bytes 491528 | tf_op jit(solution)/shard_map/ppermute | solution.py:329
  41.4 6.4 %collective-permute-start.5 = (bf16[20,2,16,128]{3,2,1,0:T(8,128)(2,1)S(1)}, bf16[20,2,16,128]{3,2,1,0:T(8,128)(2,1)S(1)}, u32[]{:S(2)}, u32[]{:S(2)}) collective-permute-start(bf16[20,2,16,128]{3,2,1,0:T(8,128)(2,1)S(1)} %collective-permute-done.1.a2), channel_id=1, source_target_pairs={{0,1},{1,0},{2,3},{3,2},{4,5},{5,4},{6,7},{7,6},{8,9},{9,8},{10,11... | collective-permute-start | bytes 491528 | tf_op jit(solution)/shard_map/ppermute | solution.py:329
  42.0 5.8 %collective-permute-start.6 = (bf16[20,2,16,128]{3,2,1,0:T(8,128)(2,1)S(1)}, bf16[20,2,16,128]{3,2,1,0:T(8,128)(2,1)S(1)}, u32[]{:S(2)}, u32[]{:S(2)}) collective-permute-start(bf16[20,2,16,128]{3,2,1,0:T(8,128)(2,1)S(1)} %collective-permute-done.2.a3), channel_id=1, source_target_pairs={{0,1},{1,0},{2,3},{3,2},{4,5},{5,4},{6,7},{7,6},{8,9},{9,8},{10,11... | collective-permute-start | bytes 491528 | tf_op jit(solution)/shard_map/ppermute | solution.py:329
  44.3 4.4 %collective-permute-start.4 = (bf16[20,2,16,128]{3,2,1,0:T(8,128)(2,1)S(1)}, bf16[20,2,16,128]{3,2,1,0:T(8,128)(2,1)S(1)}, u32[]{:S(2)}, u32[]{:S(2)}) collective-permute-start(bf16[20,2,16,128]{3,2,1,0:T(8,128)(2,1)S(1)} %collective-permute-done.a1), channel_id=1, source_target_pairs={{0,1},{1,0},{2,3},{3,2},{4,5},{5,4},{6,7},{7,6},{8,9},{9,8},{10,11... | collective-permute-start | bytes 491528 | tf_op jit(solution)/shard_map/ppermute | solution.py:329
  55.2 2.2 %collective-permute-start.15 = (bf16[4,2,20,16,128]{4,3,2,1,0:T(8,128)(2,1)S(1)}, bf16[4,2,20,16,128]{4,3,2,1,0:T(8,128)(2,1)S(1)}, u32[]{:S(2)}, u32[]{:S(2)}) collective-permute-start(bf16[4,2,20,16,128]{4,3,2,1,0:T(8,128)(2,1)S(1)} %get-tuple-element.29), channel_id=1, source_target_pairs={{0,1},{1,0},{2,3},{3,2},{4,5},{5,4},{6,7},{7,6},{8,9},{9,8},{10,11... | collective-permute-start | bytes 1966088 | tf_op jit(solution)/shard_map/ppermute | solution.py:329
  57.5 5.5 %collective-permute-start.18 = (bf16[2,20,16,128]{3,2,1,0:T(8,128)(2,1)S(1)}, bf16[2,20,16,128]{3,2,1,0:T(8,128)(2,1)S(1)}, u32[]{:S(2)}, u32[]{:S(2)}) collective-permute-start(bf16[2,20,16,128]{3,2,1,0:T(8,128)(2,1)S(1)} %get-tuple-element.32), channel_id=1, source_target_pairs={{0,192},{64,0},{128,64},{192,128},{1,193},{65,1},{129,65},{193,129... | collective-permute-start | bytes 491528 | tf_op jit(solution)/shard_map/ppermute | solution.py:324
  58.0 6.8 %collective-permute-start.17 = (bf16[2,20,16,128]{3,2,1,0:T(8,128)(2,1)S(1)}, bf16[2,20,16,128]{3,2,1,0:T(8,128)(2,1)S(1)}, u32[]{:S(2)}, u32[]{:S(2)}) collective-permute-start(bf16[2,20,16,128]{3,2,1,0:T(8,128)(2,1)S(1)} %get-tuple-element.33), channel_id=1, source_target_pairs={{0,128},{64,192},{128,0},{192,64},{1,129},{65,193},{129,1},{193,65... | collective-permute-start | bytes 491528 | tf_op jit(solution)/shard_map/ppermute | solution.py:324
  59.9 9.1 %collective-permute-start.16 = (bf16[2,20,16,128]{3,2,1,0:T(8,128)(2,1)S(1)}, bf16[2,20,16,128]{3,2,1,0:T(8,128)(2,1)S(1)}, u32[]{:S(2)}, u32[]{:S(2)}) collective-permute-start(bf16[2,20,16,128]{3,2,1,0:T(8,128)(2,1)S(1)} %get-tuple-element.34), channel_id=1, source_target_pairs={{0,64},{64,128},{128,192},{192,0},{1,65},{65,129},{129,193},{193,1... | collective-permute-start | bytes 491528 | tf_op jit(solution)/shard_map/ppermute | solution.py:324
  71.5 25.5 %all-to-all-start.1 = ((bf16[32,64,128]{2,1,0:T(8,128)(2,1)}), bf16[32,64,128]{2,1,0:T(8,128)(2,1)S(1)}, u32[]{:S(2)}, u32[]{:S(2)}) async-start(bf16[32,64,128]{2,1,0:T(8,128)(2,1)} %bitcast.23), calls=%async_computation.1 | async-start | bytes 1048576 | tf_op jit(solution)/shard_map/all_to_all | solution.py:350
  76.9 11.8 %collective-permute-start.11 = (bf16[2,128,512]{2,1,0:T(8,128)(2,1)S(1)}, bf16[2,128,512]{2,1,0:T(8,128)(2,1)S(1)}, u32[]{:S(2)}, u32[]{:S(2)}) collective-permute-start(bf16[2,128,512]{2,1,0:T(8,128)(2,1)S(1)} %get-tuple-element.22), channel_id=1, source_target_pairs={{0,0},{128,1},{2,2},{130,3},{4,4},{132,5},{6,6},{134,7},{1,64},{12... | collective-permute-start | bytes 786440 | tf_op jit(solution)/shard_map/ppermute | solution.py:411
  81.5 10.6 %collective-permute-start.12 = (bf16[2,128,512]{2,1,0:T(8,128)(2,1)S(1)}, bf16[2,128,512]{2,1,0:T(8,128)(2,1)S(1)}, u32[]{:S(2)}, u32[]{:S(2)}) collective-permute-start(bf16[2,128,512]{2,1,0:T(8,128)(2,1)S(1)} %get-tuple-element.23), channel_id=1, source_target_pairs={{1,0},{129,1},{3,2},{131,3},{5,4},{133,5},{7,6},{135,7},{64,64},{1... | collective-permute-start | bytes 786440 | tf_op jit(solution)/shard_map/ppermute | solution.py:411
  83.4 11.2 %collective-permute-start.13 = (bf16[2,128,512]{2,1,0:T(8,128)(2,1)S(1)}, bf16[2,128,512]{2,1,0:T(8,128)(2,1)S(1)}, u32[]{:S(2)}, u32[]{:S(2)}) collective-permute-start(bf16[2,128,512]{2,1,0:T(8,128)(2,1)S(1)} %get-tuple-element.24), channel_id=1, source_target_pairs={{64,0},{192,1},{66,2},{194,3},{68,4},{196,5},{70,6},{198,7},{65,64... | collective-permute-start | bytes 786440 | tf_op jit(solution)/shard_map/ppermute | solution.py:411
  85.8 10.1 %collective-permute-start.14 = (bf16[2,128,512]{2,1,0:T(8,128)(2,1)S(1)}, bf16[2,128,512]{2,1,0:T(8,128)(2,1)S(1)}, u32[]{:S(2)}, u32[]{:S(2)}) collective-permute-start(bf16[2,128,512]{2,1,0:T(8,128)(2,1)S(1)} %get-tuple-element.25), channel_id=1, source_target_pairs={{65,0},{193,1},{67,2},{195,3},{69,4},{197,5},{71,6},{199,7},{0,64}... | collective-permute-start | bytes 786440 | tf_op jit(solution)/shard_map/ppermute | solution.py:411

commit v5 on v4

--- a/solution.py
+++ b/solution.py
@@ -57,36 +57,62 @@
     return pipe, core, lax.rem(pipe, 2) * CORES + core
 
 
-def spread_kernel(key_in, value_in, sent, key, value, sems):
-    ctx_count = sent.shape[0] // TILES
-    run_copies([(key_in, key), (value_in, value)], sems)
-    for x in range(TILES):
-        for kind, rows in enumerate((key, value)):
+def spread_kernel(kv_in, sent, kv, tiles, sem, sems):
+    count = tiles.shape[0]
+    run_copies([(kv_in, kv)], sem)
+    for x in range(count):
+        for kind in range(2):
             for j in range(2):
                 head = 2 * x + j
-                block = rows[:, head * HEAD_DIM:(head + 1) * HEAD_DIM]
-                for c in range(ctx_count):
-                    sent[c * TILES + x, kind, j] = block
-
-
-def spread(key, value, ctx_count):
+                tiles[x, kind, j] = kv[kind, :, head * HEAD_DIM:(head + 1) * HEAD_DIM]
+    run_copies(
+        [(tiles, sent.at[pl.ds(c * count, count)]) for c in range(sent.shape[0] // count)], sems
+    )
+
+
+def spread(kv, ctx_count):
     return pl.pallas_call(
         spread_kernel,
         out_shape=shape(ctx_count * TILES, 2, 2, TILE, HEAD_DIM),
-        in_specs=[HBM, HBM],
-        out_specs=VMEM,
-        scratch_shapes=[pltpu.VMEM(key.shape, bf16)] * 2 + [pltpu.SemaphoreType.DMA((2,))],
+        in_specs=[ANY],
+        out_specs=ANY,
+        scratch_shapes=[
+            pltpu.VMEM(kv.shape, bf16),
+            pltpu.VMEM((TILES, 2, 2, TILE, HEAD_DIM), bf16),
+            pltpu.SemaphoreType.DMA((1,)),
+            pltpu.SemaphoreType.DMA((ctx_count,)),
+        ],
         compiler_params=PARAMS,
         name="spread",
-    )(key, value)
+    )(kv)
+
+
+LAYER_OF = ((1, 2, 0, 3), (3, 0, 1, 2), (2, 1, 3, 0), (0, 3, 2, 1))
+GROUP_OF = tuple(tuple(row.index(l) for l in range(LAYERS)) for row in LAYER_OF)
+
+
+def chosen(row, index):
+    value = jnp.int32(row[0])
+    for i in range(1, len(row)):
+        value = jnp.where(index == i, row[i], value)
+    return value
+
+
+def group_of(m):
+    pipe, core, _ = place_of()
+    return chosen(GROUP_OF[m], lax.rem(pipe + 2 * core, LAYERS))
+
+
+def layer_of(m):
+    pipe, _, group = place_of()
+    return lax.rem(chosen(LAYER_OF[m], group) + 2 * (pipe // 2), LAYERS)
 
 
 def pieces_kernel(query, cot, p0, p1, p2, p3, sems):
-    me = lax.axis_index("pipe")
     width = p0.shape[2]
     pairs = []
     for m, piece in enumerate((p0, p1, p2, p3)):
-        column = pl.multiple_of(lax.rem(me + m, LAYERS) * width, width)
+        column = pl.multiple_of(group_of(m) * width, width)
         for i, whole in enumerate((query, cot)):
             pairs.append((whole.at[:, pl.ds(column, width)], piece.at[i]))
     run_copies(pairs, sems)
@@ -124,7 +150,7 @@
         for d, x in enumerate((b0, b1, b2, b3)):
             pairs.append((x.at[:, k], kv.at[k, back(pipe, d), :, 1 - core]))
     for m, x in enumerate((q0, q1, q2, q3)):
-        pairs.append((x, qc.at[back(group, m)]))
+        pairs.append((x, qc.at[layer_of(m)]))
     pairs.append((bias_in, bias))
     run_copies(pairs, sems)
 
@@ -194,7 +220,7 @@
             pairs.append((dkv.at[k, l, :, 1 - core], give.at[d, k]))
             pairs.append((dkv.at[k, l, :, core], keep.at[d, k]))
     for m, x in enumerate((og0, og1, og2, og3)):
-        pairs.append((og.at[back(group, m)], x))
+        pairs.append((og.at[layer_of(m)], x))
     run_copies(pairs, out_sems)
 
 
@@ -226,14 +252,15 @@
     )(bias, *mine, *theirs, *qc_parts)
 
 
-def place_kernel(order, p0, p1, p2, p3, sent, parts, sems):
+def place_kernel(order_in, p0, p1, p2, p3, sent_out, order, parts, sent, sems, out_sems):
     pipe, _, _ = place_of()
 
     def clear():
         sent[...] = jnp.zeros(sent.shape, bf16)
 
     run_copies(
-        [
+        [(order_in, order)]
+        + [
             (x, parts.at[lax.rem(pipe + LAYERS - d, LAYERS)])
             for d, x in enumerate((p0, p1, p2, p3))
         ],
@@ -253,15 +280,21 @@
                 for k in range(2):
                     sent[c * TILES:(c + 1) * TILES, k, head] = total[k]
 
+    run_copies([(sent, sent_out)], out_sems)
+
 
 def place(order, parts):
     return pl.pallas_call(
         place_kernel,
         out_shape=shape(order.shape[0] * TILES, 2, 2, TILE, HEAD_DIM),
-        in_specs=[SMEM] + [ANY] * LAYERS,
-        out_specs=VMEM,
+        in_specs=[ANY] * (1 + LAYERS),
+        out_specs=ANY,
         scratch_shapes=[
-            pltpu.VMEM((LAYERS,) + parts[0].shape, bf16), pltpu.SemaphoreType.DMA((LAYERS,))
+            pltpu.SMEM(order.shape, jnp.int32),
+            pltpu.VMEM((LAYERS,) + parts[0].shape, bf16),
+            pltpu.VMEM((order.shape[0] * TILES, 2, 2, TILE, HEAD_DIM), bf16),
+            pltpu.SemaphoreType.DMA((1 + LAYERS,)),
+            pltpu.SemaphoreType.DMA((1,)),
         ],
         compiler_params=PARAMS,
         name="place",
@@ -296,11 +329,10 @@
 
 
 def assemble_kernel(g0, g1, g2, g3, out, grad_query, sems):
-    me = lax.axis_index("pipe")
     width = g0.shape[2]
     pairs = []
     for m, piece in enumerate((g0, g1, g2, g3)):
-        column = pl.multiple_of(lax.rem(me + m, LAYERS) * width, width)
+        column = pl.multiple_of(group_of(m) * width, width)
         for i, whole in enumerate((out, grad_query)):
             pairs.append((piece.at[i], whole.at[:, pl.ds(column, width)]))
     run_copies(pairs, sems)
@@ -329,14 +361,22 @@
     return lax.ppermute(block, "tp", [(i, i ^ 1) for i in range(size)])
 
 
-def group_pairs(m):
+def sent_over(block, pairs):
     tp_count = lax.axis_size("tp")
+    route = [
+        (a * tp_count + x + b, c * tp_count + x + d)
+        for (a, b), (c, d) in pairs
+        for x in range(0, tp_count, CORES)
+    ]
+    return lax.ppermute(block, ("pipe", "tp"), route)
+
+
+def round_pairs(m):
     pairs = []
     for l in range(LAYERS):
-        for tp in range(tp_count):
-            group = (l + m) % LAYERS
-            pipe = 2 * (tp % 2) + group // 2
-            pairs.append((l * tp_count + tp, pipe * tp_count + tp - tp % 2 + group % 2))
+        for core in range(CORES):
+            group = GROUP_OF[m][(l + 2 * core) % LAYERS]
+            pairs.append(((l, core), (2 * core + group // CORES, group % CORES)))
     return pairs
 
 
@@ -362,11 +402,9 @@
     layer = lax.axis_index("pipe")
     rows = query_in.shape[1]
 
-    got = exchanged(spread(key_in[0], value_in[0], ctx_count))
-    qc_parts = [
-        lax.ppermute(piece, ("pipe", "tp"), group_pairs(m))
-        for m, piece in enumerate(pieces_of(query_in[0], out_cot[0]))
-    ]
+    got = exchanged(spread(jnp.concatenate([key_in, value_in]), ctx_count))
+    pieces = pieces_of(query_in[0], out_cot[0])
+    qc_parts = [sent_over(pieces[m], round_pairs(m)) for m in range(LAYERS)]
 
     position = stretch_order[lax.axis_index("ctx")]
     block_ids = jnp.arange(ctx_count, dtype=jnp.int32)
@@ -408,8 +446,7 @@
     grad_key, grad_value = total(exchanged(place(stretch_order, parts)))
     out, grad_query = assemble(
         [
-            lax.ppermute(x, ("pipe", "tp"), [(b, a) for a, b in group_pairs(m)])
-            for m, x in enumerate(groups)
+            sent_over(groups[m], [(b, a) for a, b in round_pairs(m)]) for m in range(LAYERS)
         ]
     )
     return (out[None], grad_query[None], grad_key[None], grad_value[None])

time: 98.5 us -> 94.6 us (0.960)
  starting transfers between devices: 56.7 us -> 49.3 us
  waiting for transfers between devices: 19.4 us -> 24.5 us
  local copies, waits for them, and re-layouts: 3.65 us -> 2.15 us
    ppermute x5, starting transfers between devices: 8.04 us -> 1.73 us  [swapped(): return lax.ppermute(block, 'tp', [(i, i ^ 1) for i in range(size)])]
    ppermute x8, waiting for transfers between devices: 7.2 us -> 10.5 us  [sent_over(): return lax.ppermute(block, ('pipe', 'tp'), route)]
    unnamed x16 -> x12, local copies, waits for them, and re-layouts: 2.29 us -> 0.79 us
    all_to_all x2, waiting for transfers between devices: 0.57 us -> 2.01 us  [exchanged(): lax.all_to_all(flat, ('ctx', 'tp'), split_axis=0, concat_axis=0, axis_ind...]
    ppermute x8, starting transfers between devices: 24.3 us -> 22.9 us  [sent_over(): return lax.ppermute(block, ('pipe', 'tp'), route)]
    ppermute x6, starting transfers between devices: 6.87 us -> 7.9 us  [moved(): lax.ppermute(block, 'pipe', [(i, (i + distance) % size) for i in range(si...]
where the time goes in v5:
time: 94.6 us; the launch traced here: 94.1 us
  starting transfers between devices  49.3 us (52%)
  waiting for transfers between devices  24.5 us (26%)
  Pallas kernels  11.4 us (12%)
  between operations  5.49 us (6%)
  local copies, waits for them, and re-layouts  2.15 us (2%)
  other arithmetic  1.27 us (1%)
    ppermute x8, starting transfers between devices, sent_over(): return lax.ppermute(block, ('pipe', 'tp'), route)  22.9 us
    all_to_all x2, starting transfers between devices, exchanged(): lax.all_to_all(flat, ('ctx', 'tp'), split_axis=0, concat_axis=0, axis_ind...  16.8 us
    ppermute x8, waiting for transfers between devices, sent_over(): return lax.ppermute(block, ('pipe', 'tp'), route)  10.5 us
    ppermute x6, waiting for transfers between devices, moved(): lax.ppermute(block, 'pipe', [(i, (i + distance) % size) for i in range(si...  9.87 us
    ppermute x6, starting transfers between devices, moved(): lax.ppermute(block, 'pipe', [(i, (i + distance) % size) for i in range(si...  7.9 us
    pallas_call x1, Pallas kernels, run_layers(): pl.pallas_call(layers_kernel, out_shape=(kv_shape, kv_shape) + (shape(2,...  6.53 us
    ppermute x5, waiting for transfers between devices, swapped(): return lax.ppermute(block, 'tp', [(i, i ^ 1) for i in range(size)])  2.09 us
    all_to_all x2, waiting for transfers between devices, exchanged(): lax.all_to_all(flat, ('ctx', 'tp'), split_axis=0, concat_axis=0, axis_ind...  2.01 us
  transfers between devices with their start and end apart: 21, of which 9 were waited for; matrix products, arithmetic and copies ran while one was open for 2% of the time, Pallas kernels for 1%

profile of v5, /device:TPU:1, one launch (start us, length us, event | category | flops | bytes accessed | tf_op | source)
XLA Modules:
  0.0 94.1 jit_solution(7541652617703418062)
XLA Ops:
  0.6 0.8 pad_maximum_fusion.kv_in
  1.4 0.9 %spread.1 = bf16[32,2,2,16,128]{4,3,2,1,0:T(8,128)(2,1)} custom-call(bf16[2,16,1024]{2,1,0:T(8,128)(2,1)S(1)} %pad_maximum_fusion.kv_in), custom_call_target="tpu_custom_call" | custom-call | tf_op jit(solution)/shard_map/spread/pallas_call | solution.py:74
  2.4 12.0 %all-to-all-start = ((bf16[32,64,128]{2,1,0:T(8,128)(2,1)}), bf16[32,64,128]{2,1,0:T(8,128)(2,1)S(1)}, u32[]{:S(2)}, u32[]{:S(2)}) async-start(bf16[32,64,128]{2,1,0:T(8,128)(2,1)} %bitcast.1), calls=%async_computation | async-start | bytes 1048576 | tf_op jit(solution)/shard_map/all_to_all | solution.py:390
  14.7 3.0 %collective-permute-start.7 = (bf16[2,128,512]{2,1,0:T(8,128)(2,1)S(1)}, bf16[2,128,512]{2,1,0:T(8,128)(2,1)S(1)}, u32[]{:S(2)}, u32[]{:S(2)}) collective-permute-start(bf16[2,128,512]{2,1,0:T(8,128)(2,1)S(1)} %get-tuple-element.18), channel_id=1, source_target_pairs={{0,64},{2,66},{4,68},{6,70},{1,129},{3,131},{5,133},{7,135},{64,0}... | collective-permute-start | bytes 786440 | tf_op jit(solution)/shard_map/ppermute | solution.py:371
  17.7 3.0 %collective-permute-start.8 = (bf16[2,128,512]{2,1,0:T(8,128)(2,1)S(1)}, bf16[2,128,512]{2,1,0:T(8,128)(2,1)S(1)}, u32[]{:S(2)}, u32[]{:S(2)}) collective-permute-start(bf16[2,128,512]{2,1,0:T(8,128)(2,1)S(1)} %get-tuple-element.19), channel_id=1, source_target_pairs={{0,1},{2,3},{4,5},{6,7},{1,193},{3,195},{5,197},{7,199},{64,64},{6... | collective-permute-start | bytes 786440 | tf_op jit(solution)/shard_map/ppermute | solution.py:371
  20.7 1.4 %collective-permute-start.9 = (bf16[2,128,512]{2,1,0:T(8,128)(2,1)S(1)}, bf16[2,128,512]{2,1,0:T(8,128)(2,1)S(1)}, u32[]{:S(2)}, u32[]{:S(2)}) collective-permute-start(bf16[2,128,512]{2,1,0:T(8,128)(2,1)S(1)} %get-tuple-element.20), channel_id=1, source_target_pairs={{0,65},{2,67},{4,69},{6,71},{1,128},{3,130},{5,132},{7,134},{64,1}... | collective-permute-start | bytes 786440 | tf_op jit(solution)/shard_map/ppermute | solution.py:371
  22.2 0.7 copy-done.2
  22.8 0.6 dynamic_slice.66
  24.9 0.7 fusion.6
  28.7 2.0 %all-to-all-done = bf16[32,64,128]{2,1,0:T(8,128)(2,1)S(1)} async-done(((bf16[32,64,128]{2,1,0:T(8,128)(2,1)}), bf16[32,64,128]{2,1,0:T(8,128)(2,1)S(1)}, u32[]{:S(2)}, u32[]{:S(2)}) %all-to-all-start) | async-done | bytes 524320 | tf_op jit(solution)/shard_map/all_to_all | solution.py:390
  30.9 3.0 %collective-permute-start.1 = (bf16[20,2,16,128]{3,2,1,0:T(8,128)(2,1)S(1)}, bf16[20,2,16,128]{3,2,1,0:T(8,128)(2,1)S(1)}, u32[]{:S(2)}, u32[]{:S(2)}) collective-permute-start(bf16[20,2,16,128]{3,2,1,0:T(8,128)(2,1)S(1)} %bitcast.80), channel_id=1, source_target_pairs={{0,128},{64,192},{128,0},{192,64},{1,129},{65,193},{129,1},{193,65... | collective-permute-start | bytes 491528 | tf_op jit(solution)/shard_map/ppermute | solution.py:356
  33.9 0.8 collective-permute-start.2
  34.7 0.7 collective-permute-start
  35.4 7.0 %collective-permute-start.10 = (bf16[2,128,512]{2,1,0:T(8,128)(2,1)S(1)}, bf16[2,128,512]{2,1,0:T(8,128)(2,1)S(1)}, u32[]{:S(2)}, u32[]{:S(2)}) collective-permute-start(bf16[2,128,512]{2,1,0:T(8,128)(2,1)S(1)} %get-tuple-element.21), channel_id=1, source_target_pairs={{0,0},{2,2},{4,4},{6,6},{1,192},{3,194},{5,196},{7,198},{64,65},{6... | collective-permute-start | bytes 786440 | tf_op jit(solution)/shard_map/ppermute | solution.py:371
  42.6 0.5 collective-permute-start.5
  43.2 1.0 %collective-permute-start.4 = (bf16[20,2,16,128]{3,2,1,0:T(8,128)(2,1)S(1)}, bf16[20,2,16,128]{3,2,1,0:T(8,128)(2,1)S(1)}, u32[]{:S(2)}, u32[]{:S(2)}) collective-permute-start(bf16[20,2,16,128]{3,2,1,0:T(8,128)(2,1)S(1)} %collective-permute-done.a1), channel_id=1, source_target_pairs={{0,1},{1,0},{2,3},{3,2},{4,5},{5,4},{6,7},{7,6},{8,9},{9,8},{10,11... | collective-permute-start | bytes 491528 | tf_op jit(solution)/shard_map/ppermute | solution.py:361
  44.3 2.2 %collective-permute-done.10.q3 = bf16[2,128,512]{2,1,0:T(8,128)(2,1)S(1)} collective-permute-done((bf16[2,128,512]{2,1,0:T(8,128)(2,1)S(1)}, bf16[2,128,512]{2,1,0:T(8,128)(2,1)S(1)}, u32[]{:S(2)}, u32[]{:S(2)}) %collective-permute-start.10) | collective-permute-done | bytes 262176 | tf_op jit(solution)/shard_map/ppermute | solution.py:371
  46.5 6.5 %layers.1 = (bf16[4,2,20,16,128]{4,3,2,1,0:T(8,128)(2,1)S(1)}, bf16[4,2,20,16,128]{4,3,2,1,0:T(8,128)(2,1)S(1)}, bf16[2,128,512]{2,1,0:T(8,128)(2,1)S(1)}, bf16[...) custom-call(f32[128,640]{1,0:T(8,128)S(1)} %fusion.1.bias_in, ...), custom_call_target="tpu_custom_call" | custom-call | tf_op jit(solution)/shard_map/layers/pallas_call | solution.py:231
  53.1 2.1 %collective-permute-done.15 = bf16[4,2,20,16,128]{4,3,2,1,0:T(8,128)(2,1)S(1)} collective-permute-done((bf16[4,2,20,16,128]{4,3,2,1,0:T(8,128)(2,1)S(1)}, bf16[4,2,20,16,128]{4,3,2,1,0:T(8,128)(2,1)S(1)}, u32[]{:S(2)}, u32[]{:S(2)}) %collective-permute-start.15) | collective-permute-done | bytes 655392 | tf_op jit(solution)/shard_map/ppermute | solution.py:361
  55.4 2.8 %collective-permute-start.18 = (bf16[2,20,16,128]{3,2,1,0:T(8,128)(2,1)S(1)}, bf16[2,20,16,128]{3,2,1,0:T(8,128)(2,1)S(1)}, u32[]{:S(2)}, u32[]{:S(2)}) collective-permute-start(bf16[2,20,16,128]{3,2,1,0:T(8,128)(2,1)S(1)} %get-tuple-element.32), channel_id=1, source_target_pairs={{0,192},{64,0},{128,64},{192,128},{1,193},{65,1},{129,65},{193,129... | collective-permute-start | bytes 491528 | tf_op jit(solution)/shard_map/ppermute | solution.py:356
  58.2 0.7 collective-permute-start.16
  58.8 5.9 %collective-permute-done.18.p3 = bf16[2,20,16,128]{3,2,1,0:T(8,128)(2,1)S(1)} collective-permute-done((bf16[2,20,16,128]{3,2,1,0:T(8,128)(2,1)S(1)}, bf16[2,20,16,128]{3,2,1,0:T(8,128)(2,1)S(1)}, u32[]{:S(2)}, u32[]{:S(2)}) %collective-permute-start.18) | collective-permute-done | bytes 163872 | tf_op jit(solution)/shard_map/ppermute | solution.py:356
  64.9 3.9 %collective-permute-done.16.p1 = bf16[2,20,16,128]{3,2,1,0:T(8,128)(2,1)S(1)} collective-permute-done((bf16[2,20,16,128]{3,2,1,0:T(8,128)(2,1)S(1)}, bf16[2,20,16,128]{3,2,1,0:T(8,128)(2,1)S(1)}, u32[]{:S(2)}, u32[]{:S(2)}) %collective-permute-start.16) | collective-permute-done | bytes 163872 | tf_op jit(solution)/shard_map/ppermute | solution.py:356
  68.7 1.9 %place.1 = bf16[32,2,2,16,128]{4,3,2,1,0:T(8,128)(2,1)} custom-call(s32[8]{0:T(128)S(1)} %copy-done.2, bf16[2,20,16,128]{3,2,1,0:T(8,128)(2,1)S(1)} %get-tuple-element.35.p0, bf16[2,20,16,128]{3,2,1,0:T(8,128)(2,1)S(1)} %collective-permute-done.16.p1, bf16[2,20,16,128]{3,2,1,0:T(8,128)(2,1)S(1)} %collective-permute-done.17.p2, ...), custom_call_target="tpu_custom_call" | custom-call | tf_op jit(solution)/shard_map/place/pallas_call | solution.py:287
  70.6 4.8 %all-to-all-start.1 = ((bf16[32,64,128]{2,1,0:T(8,128)(2,1)}), bf16[32,64,128]{2,1,0:T(8,128)(2,1)S(1)}, u32[]{:S(2)}, u32[]{:S(2)}) async-start(bf16[32,64,128]{2,1,0:T(8,128)(2,1)} %bitcast.21), calls=%async_computation.1 | async-start | bytes 1048576 | tf_op jit(solution)/shard_map/all_to_all | solution.py:390
  75.4 1.2 %collective-permute-start.11 = (bf16[2,128,512]{2,1,0:T(8,128)(2,1)S(1)}, bf16[2,128,512]{2,1,0:T(8,128)(2,1)S(1)}, u32[]{:S(2)}, u32[]{:S(2)}) collective-permute-start(bf16[2,128,512]{2,1,0:T(8,128)(2,1)S(1)} %get-tuple-element.22), channel_id=1, source_target_pairs={{64,0},{66,2},{68,4},{70,6},{129,1},{131,3},{133,5},{135,7},{0,64}... | collective-permute-start | bytes 786440 | tf_op jit(solution)/shard_map/ppermute | solution.py:371
  76.5 1.9 %collective-permute-start.12 = (bf16[2,128,512]{2,1,0:T(8,128)(2,1)S(1)}, bf16[2,128,512]{2,1,0:T(8,128)(2,1)S(1)}, u32[]{:S(2)}, u32[]{:S(2)}) collective-permute-start(bf16[2,128,512]{2,1,0:T(8,128)(2,1)S(1)} %get-tuple-element.23), channel_id=1, source_target_pairs={{1,0},{3,2},{5,4},{7,6},{193,1},{195,3},{197,5},{199,7},{64,64},{6... | collective-permute-start | bytes 786440 | tf_op jit(solution)/shard_map/ppermute | solution.py:371
  78.7 5.1 %collective-permute-start.14 = (bf16[2,128,512]{2,1,0:T(8,128)(2,1)S(1)}, bf16[2,128,512]{2,1,0:T(8,128)(2,1)S(1)}, u32[]{:S(2)}, u32[]{:S(2)}) collective-permute-start(bf16[2,128,512]{2,1,0:T(8,128)(2,1)S(1)} %get-tuple-element.25), channel_id=1, source_target_pairs={{0,0},{2,2},{4,4},{6,6},{192,1},{194,3},{196,5},{198,7},{65,64},{6... | collective-permute-start | bytes 786440 | tf_op jit(solution)/shard_map/ppermute | solution.py:371
  84.0 7.4 %collective-permute-done.12.g1 = bf16[2,128,512]{2,1,0:T(8,128)(2,1)S(1)} collective-permute-done((bf16[2,128,512]{2,1,0:T(8,128)(2,1)S(1)}, bf16[2,128,512]{2,1,0:T(8,128)(2,1)S(1)}, u32[]{:S(2)}, u32[]{:S(2)}) %collective-permute-start.12) | collective-permute-done | bytes 262176 | tf_op jit(solution)/shard_map/ppermute | solution.py:371
  91.3 0.8 collective-permute-done.14.g3
  92.1 1.0 %assemble.1 = (bf16[128,2048]{1,0:T(8,128)(2,1)}, bf16[128,2048]{1,0:T(8,128)(2,1)}) custom-call(bf16[2,128,512]{2,1,0:T(8,128)(2,1)S(1)} %collective-permute-done.11.g0, bf16[2,128,512]{2,1,0:T(8,128)(2,1)S(1)} %collective-permute-done.12.g1, bf16[2,128,512]{2,1,0:T(8,128)(2,1)S(1)} %collective-permute-done.13.g2, ...), custom_call_target="tpu_custom_call" | custom-call | tf_op jit(solution)/shard_map/assemble/pallas_call | solution.py:343
  93.2 0.7 total.1
  (39 shorter events, 1.8 us)
Async XLA Ops:
  2.4 12.0 %copy-start = (bf16[1,128,2048]{2,1,0:T(8,128)(2,1)S(1)}, bf16[1,128,2048]{2,1,0:T(8,128)(2,1)}, u32[]{:S(2)}) copy-start(bf16[1,128,2048]{2,1,0:T(8,128)(2,1)} %param.6) | copy-start | bytes 1572868
  2.4 12.0 %copy-start.1 = (bf16[1,128,2048]{2,1,0:T(8,128)(2,1)S(1)}, bf16[1,128,2048]{2,1,0:T(8,128)(2,1)}, u32[]{:S(2)}) copy-start(bf16[1,128,2048]{2,1,0:T(8,128)(2,1)} %param.11) | copy-start | bytes 1572868
  2.4 28.3 %all-to-all-start = ((bf16[32,64,128]{2,1,0:T(8,128)(2,1)}), bf16[32,64,128]{2,1,0:T(8,128)(2,1)S(1)}, u32[]{:S(2)}, u32[]{:S(2)}) async-start(bf16[32,64,128]{2,1,0:T(8,128)(2,1)} %bitcast.1), calls=%async_computation | async-start | bytes 1048576 | tf_op jit(solution)/shard_map/all_to_all | solution.py:390
  14.7 19.9 %collective-permute-start.7 = (bf16[2,128,512]{2,1,0:T(8,128)(2,1)S(1)}, bf16[2,128,512]{2,1,0:T(8,128)(2,1)S(1)}, u32[]{:S(2)}, u32[]{:S(2)}) collective-permute-start(bf16[2,128,512]{2,1,0:T(8,128)(2,1)S(1)} %get-tuple-element.18), channel_id=1, source_target_pairs={{0,64},{2,66},{4,68},{6,70},{1,129},{3,131},{5,133},{7,135},{64,0}... | collective-permute-start | bytes 786440 | tf_op jit(solution)/shard_map/ppermute | solution.py:371
  17.7 17.7 %collective-permute-start.8 = (bf16[2,128,512]{2,1,0:T(8,128)(2,1)S(1)}, bf16[2,128,512]{2,1,0:T(8,128)(2,1)S(1)}, u32[]{:S(2)}, u32[]{:S(2)}) collective-permute-start(bf16[2,128,512]{2,1,0:T(8,128)(2,1)S(1)} %get-tuple-element.19), channel_id=1, source_target_pairs={{0,1},{2,3},{4,5},{6,7},{1,193},{3,195},{5,197},{7,199},{64,64},{6... | collective-permute-start | bytes 786440 | tf_op jit(solution)/shard_map/ppermute | solution.py:371
  20.7 21.7 %collective-permute-start.9 = (bf16[2,128,512]{2,1,0:T(8,128)(2,1)S(1)}, bf16[2,128,512]{2,1,0:T(8,128)(2,1)S(1)}, u32[]{:S(2)}, u32[]{:S(2)}) collective-permute-start(bf16[2,128,512]{2,1,0:T(8,128)(2,1)S(1)} %get-tuple-element.20), channel_id=1, source_target_pairs={{0,65},{2,67},{4,69},{6,71},{1,128},{3,130},{5,132},{7,134},{64,1}... | collective-permute-start | bytes 786440 | tf_op jit(solution)/shard_map/ppermute | solution.py:371
  22.2 0.7 copy-start.2
  30.9 11.7 %collective-permute-start.1 = (bf16[20,2,16,128]{3,2,1,0:T(8,128)(2,1)S(1)}, bf16[20,2,16,128]{3,2,1,0:T(8,128)(2,1)S(1)}, u32[]{:S(2)}, u32[]{:S(2)}) collective-permute-start(bf16[20,2,16,128]{3,2,1,0:T(8,128)(2,1)S(1)} %bitcast.80), channel_id=1, source_target_pairs={{0,128},{64,192},{128,0},{192,64},{1,129},{65,193},{129,1},{193,65... | collective-permute-start | bytes 491528 | tf_op jit(solution)/shard_map/ppermute | solution.py:356
  33.9 1.5 %copy-start.3 = (s32[1024]{0:T(1024)S(1)}, s32[1024]{0:T(1024)}, u32[]{:S(2)}) copy-start(s32[1024]{0:T(1024)} %param.9) | copy-start | bytes 12292
  33.9 9.2 %collective-permute-start.2 = (bf16[20,2,16,128]{3,2,1,0:T(8,128)(2,1)S(1)}, bf16[20,2,16,128]{3,2,1,0:T(8,128)(2,1)S(1)}, u32[]{:S(2)}, u32[]{:S(2)}) collective-permute-start(bf16[20,2,16,128]{3,2,1,0:T(8,128)(2,1)S(1)} %bitcast.79), channel_id=1, source_target_pairs={{0,192},{64,0},{128,64},{192,128},{1,193},{65,1},{129,65},{193,129... | collective-permute-start | bytes 491528 | tf_op jit(solution)/shard_map/ppermute | solution.py:356
  34.7 8.5 %collective-permute-start = (bf16[20,2,16,128]{3,2,1,0:T(8,128)(2,1)S(1)}, bf16[20,2,16,128]{3,2,1,0:T(8,128)(2,1)S(1)}, u32[]{:S(2)}, u32[]{:S(2)}) collective-permute-start(bf16[20,2,16,128]{3,2,1,0:T(8,128)(2,1)S(1)} %bitcast.81), channel_id=1, source_target_pairs={{0,64},{64,128},{128,192},{192,0},{1,65},{65,129},{129,193},{193,1... | collective-permute-start | bytes 491528 | tf_op jit(solution)/shard_map/ppermute | solution.py:356
  35.4 11.0 %collective-permute-start.10 = (bf16[2,128,512]{2,1,0:T(8,128)(2,1)S(1)}, bf16[2,128,512]{2,1,0:T(8,128)(2,1)S(1)}, u32[]{:S(2)}, u32[]{:S(2)}) collective-permute-start(bf16[2,128,512]{2,1,0:T(8,128)(2,1)S(1)} %get-tuple-element.21), channel_id=1, source_target_pairs={{0,0},{2,2},{4,4},{6,6},{1,192},{3,194},{5,196},{7,198},{64,65},{6... | collective-permute-start | bytes 786440 | tf_op jit(solution)/shard_map/ppermute | solution.py:371
  42.5 4.0 %collective-permute-start.3 = (bf16[20,2,16,128]{3,2,1,0:T(8,128)(2,1)S(1)}, bf16[20,2,16,128]{3,2,1,0:T(8,128)(2,1)S(1)}, u32[]{:S(2)}, u32[]{:S(2)}) collective-permute-start(bf16[20,2,16,128]{3,2,1,0:T(8,128)(2,1)S(1)} %bitcast.72), channel_id=1, source_target_pairs={{0,1},{1,0},{2,3},{3,2},{4,5},{5,4},{6,7},{7,6},{8,9},{9,8},{10,11... | collective-permute-start | bytes 491528 | tf_op jit(solution)/shard_map/ppermute | solution.py:361
  42.6 3.9 %collective-permute-start.5 = (bf16[20,2,16,128]{3,2,1,0:T(8,128)(2,1)S(1)}, bf16[20,2,16,128]{3,2,1,0:T(8,128)(2,1)S(1)}, u32[]{:S(2)}, u32[]{:S(2)}) collective-permute-start(bf16[20,2,16,128]{3,2,1,0:T(8,128)(2,1)S(1)} %collective-permute-done.1.a2), channel_id=1, source_target_pairs={{0,1},{1,0},{2,3},{3,2},{4,5},{5,4},{6,7},{7,6},{8,9},{9,8},{10,11... | collective-permute-start | bytes 491528 | tf_op jit(solution)/shard_map/ppermute | solution.py:361
  43.1 3.4 %collective-permute-start.6 = (bf16[20,2,16,128]{3,2,1,0:T(8,128)(2,1)S(1)}, bf16[20,2,16,128]{3,2,1,0:T(8,128)(2,1)S(1)}, u32[]{:S(2)}, u32[]{:S(2)}) collective-permute-start(bf16[20,2,16,128]{3,2,1,0:T(8,128)(2,1)S(1)} %collective-permute-done.2.a3), channel_id=1, source_target_pairs={{0,1},{1,0},{2,3},{3,2},{4,5},{5,4},{6,7},{7,6},{8,9},{9,8},{10,11... | collective-permute-start | bytes 491528 | tf_op jit(solution)/shard_map/ppermute | solution.py:361
  43.2 3.3 %collective-permute-start.4 = (bf16[20,2,16,128]{3,2,1,0:T(8,128)(2,1)S(1)}, bf16[20,2,16,128]{3,2,1,0:T(8,128)(2,1)S(1)}, u32[]{:S(2)}, u32[]{:S(2)}) collective-permute-start(bf16[20,2,16,128]{3,2,1,0:T(8,128)(2,1)S(1)} %collective-permute-done.a1), channel_id=1, source_target_pairs={{0,1},{1,0},{2,3},{3,2},{4,5},{5,4},{6,7},{7,6},{8,9},{9,8},{10,11... | collective-permute-start | bytes 491528 | tf_op jit(solution)/shard_map/ppermute | solution.py:361
  53.0 2.2 %collective-permute-start.15 = (bf16[4,2,20,16,128]{4,3,2,1,0:T(8,128)(2,1)S(1)}, bf16[4,2,20,16,128]{4,3,2,1,0:T(8,128)(2,1)S(1)}, u32[]{:S(2)}, u32[]{:S(2)}) collective-permute-start(bf16[4,2,20,16,128]{4,3,2,1,0:T(8,128)(2,1)S(1)} %get-tuple-element.29), channel_id=1, source_target_pairs={{0,1},{1,0},{2,3},{3,2},{4,5},{5,4},{6,7},{7,6},{8,9},{9,8},{10,11... | collective-permute-start | bytes 1966088 | tf_op jit(solution)/shard_map/ppermute | solution.py:361
  55.4 9.3 %collective-permute-start.18 = (bf16[2,20,16,128]{3,2,1,0:T(8,128)(2,1)S(1)}, bf16[2,20,16,128]{3,2,1,0:T(8,128)(2,1)S(1)}, u32[]{:S(2)}, u32[]{:S(2)}) collective-permute-start(bf16[2,20,16,128]{3,2,1,0:T(8,128)(2,1)S(1)} %get-tuple-element.32), channel_id=1, source_target_pairs={{0,192},{64,0},{128,64},{192,128},{1,193},{65,1},{129,65},{193,129... | collective-permute-start | bytes 491528 | tf_op jit(solution)/shard_map/ppermute | solution.py:356
  58.2 6.7 %collective-permute-start.17 = (bf16[2,20,16,128]{3,2,1,0:T(8,128)(2,1)S(1)}, bf16[2,20,16,128]{3,2,1,0:T(8,128)(2,1)S(1)}, u32[]{:S(2)}, u32[]{:S(2)}) collective-permute-start(bf16[2,20,16,128]{3,2,1,0:T(8,128)(2,1)S(1)} %get-tuple-element.33), channel_id=1, source_target_pairs={{0,128},{64,192},{128,0},{192,64},{1,129},{65,193},{129,1},{193,65... | collective-permute-start | bytes 491528 | tf_op jit(solution)/shard_map/ppermute | solution.py:356
  58.2 10.5 %collective-permute-start.16 = (bf16[2,20,16,128]{3,2,1,0:T(8,128)(2,1)S(1)}, bf16[2,20,16,128]{3,2,1,0:T(8,128)(2,1)S(1)}, u32[]{:S(2)}, u32[]{:S(2)}) collective-permute-start(bf16[2,20,16,128]{3,2,1,0:T(8,128)(2,1)S(1)} %get-tuple-element.34), channel_id=1, source_target_pairs={{0,64},{64,128},{128,192},{192,0},{1,65},{65,129},{129,193},{193,1... | collective-permute-start | bytes 491528 | tf_op jit(solution)/shard_map/ppermute | solution.py:356
  70.6 22.6 %all-to-all-start.1 = ((bf16[32,64,128]{2,1,0:T(8,128)(2,1)}), bf16[32,64,128]{2,1,0:T(8,128)(2,1)S(1)}, u32[]{:S(2)}, u32[]{:S(2)}) async-start(bf16[32,64,128]{2,1,0:T(8,128)(2,1)} %bitcast.21), calls=%async_computation.1 | async-start | bytes 1048576 | tf_op jit(solution)/shard_map/all_to_all | solution.py:390
  75.4 8.6 %collective-permute-start.11 = (bf16[2,128,512]{2,1,0:T(8,128)(2,1)S(1)}, bf16[2,128,512]{2,1,0:T(8,128)(2,1)S(1)}, u32[]{:S(2)}, u32[]{:S(2)}) collective-permute-start(bf16[2,128,512]{2,1,0:T(8,128)(2,1)S(1)} %get-tuple-element.22), channel_id=1, source_target_pairs={{64,0},{66,2},{68,4},{70,6},{129,1},{131,3},{133,5},{135,7},{0,64}... | collective-permute-start | bytes 786440 | tf_op jit(solution)/shard_map/ppermute | solution.py:371
  76.5 14.8 %collective-permute-start.12 = (bf16[2,128,512]{2,1,0:T(8,128)(2,1)S(1)}, bf16[2,128,512]{2,1,0:T(8,128)(2,1)S(1)}, u32[]{:S(2)}, u32[]{:S(2)}) collective-permute-start(bf16[2,128,512]{2,1,0:T(8,128)(2,1)S(1)} %get-tuple-element.23), channel_id=1, source_target_pairs={{1,0},{3,2},{5,4},{7,6},{193,1},{195,3},{197,5},{199,7},{64,64},{6... | collective-permute-start | bytes 786440 | tf_op jit(solution)/shard_map/ppermute | solution.py:371
  78.4 12.9 %collective-permute-start.13 = (bf16[2,128,512]{2,1,0:T(8,128)(2,1)S(1)}, bf16[2,128,512]{2,1,0:T(8,128)(2,1)S(1)}, u32[]{:S(2)}, u32[]{:S(2)}) collective-permute-start(bf16[2,128,512]{2,1,0:T(8,128)(2,1)S(1)} %get-tuple-element.24), channel_id=1, source_target_pairs={{65,0},{67,2},{69,4},{71,6},{128,1},{130,3},{132,5},{134,7},{1,64}... | collective-permute-start | bytes 786440 | tf_op jit(solution)/shard_map/ppermute | solution.py:371
  78.7 13.4 %collective-permute-start.14 = (bf16[2,128,512]{2,1,0:T(8,128)(2,1)S(1)}, bf16[2,128,512]{2,1,0:T(8,128)(2,1)S(1)}, u32[]{:S(2)}, u32[]{:S(2)}) collective-permute-start(bf16[2,128,512]{2,1,0:T(8,128)(2,1)S(1)} %get-tuple-element.25), channel_id=1, source_target_pairs={{0,0},{2,2},{4,4},{6,6},{192,1},{194,3},{196,5},{198,7},{65,64},{6... | collective-permute-start | bytes 786440 | tf_op jit(solution)/shard_map/ppermute | solution.py:371

commit v6 on v5

--- a/solution.py
+++ b/solution.py
@@ -268,7 +268,7 @@
         clear,
     )
     first = order[lax.axis_index("ctx")] - REACH
-    for c in range(sent.shape[0] // TILES):
+    for c in range(sent.shape[1]):
         j = order[c] - first
 
         @pl.when((j >= 0) & (j <= REACH))
@@ -278,7 +278,7 @@
                 total = parts[2 * head, :, at].astype(f32) + parts[2 * head + 1, :, at].astype(f32)
                 total = total.astype(bf16)
                 for k in range(2):
-                    sent[c * TILES:(c + 1) * TILES, k, head] = total[k]
+                    sent[:, c, k, head] = total[k]
 
     run_copies([(sent, sent_out)], out_sems)
 
@@ -286,13 +286,13 @@
 def place(order, parts):
     return pl.pallas_call(
         place_kernel,
-        out_shape=shape(order.shape[0] * TILES, 2, 2, TILE, HEAD_DIM),
+        out_shape=shape(TILES, order.shape[0], 2, 2, TILE, HEAD_DIM),
         in_specs=[ANY] * (1 + LAYERS),
         out_specs=ANY,
         scratch_shapes=[
             pltpu.SMEM(order.shape, jnp.int32),
             pltpu.VMEM((LAYERS,) + parts[0].shape, bf16),
-            pltpu.VMEM((order.shape[0] * TILES, 2, 2, TILE, HEAD_DIM), bf16),
+            pltpu.VMEM((TILES, order.shape[0], 2, 2, TILE, HEAD_DIM), bf16),
             pltpu.SemaphoreType.DMA((1 + LAYERS,)),
             pltpu.SemaphoreType.DMA((1,)),
         ],
@@ -306,9 +306,9 @@
     copy.start()
     copy.wait()
     for x in range(TILES):
-        total = got[x].astype(f32)
-        for c in range(1, got.shape[0] // TILES):
-            total = total + got[c * TILES + x].astype(f32)
+        total = got[x, 0].astype(f32)
+        for c in range(1, got.shape[1]):
+            total = total + got[x, c].astype(f32)
         total = total.astype(bf16)
         for kind, whole in enumerate((grad_key, grad_value)):
             for j in range(2):
@@ -386,7 +386,20 @@
         [c * tp_count + tp for c in range(ctx_count) for tp in range(core, tp_count, CORES)]
         for core in range(CORES)
     ]
-    flat = block.reshape(block.shape[0], -1, HEAD_DIM)
+    flat = block.reshape(TILES * ctx_count, -1, HEAD_DIM)
+    got = lax.all_to_all(
+        flat, ("ctx", "tp"), split_axis=0, concat_axis=0, axis_index_groups=groups, tiled=True
+    )
+    return got.reshape(block.shape)
+
+
+def exchanged_by_x(block):
+    ctx_count, tp_count = lax.axis_size("ctx"), lax.axis_size("tp")
+    groups = [
+        [c * tp_count + tp for tp in range(core, tp_count, CORES) for c in range(ctx_count)]
+        for core in range(CORES)
+    ]
+    flat = block.reshape(TILES * ctx_count, -1, HEAD_DIM)
     got = lax.all_to_all(
         flat, ("ctx", "tp"), split_axis=0, concat_axis=0, axis_index_groups=groups, tiled=True
     )
@@ -443,7 +456,7 @@
     ]
     parts = [sums[0]] + [moved(sums[d], d) for d in (1, 3, 2)]
     parts = [parts[0], parts[1], parts[3], parts[2]]
-    grad_key, grad_value = total(exchanged(place(stretch_order, parts)))
+    grad_key, grad_value = total(exchanged_by_x(place(stretch_order, parts)))
     out, grad_query = assemble(
         [
             sent_over(groups[m], [(b, a) for a, b in round_pairs(m)]) for m in range(LAYERS)

time: 94.6 us -> 94.6 us (level)
    all_to_all x0 -> x1, starting transfers between devices: none -> 4.77 us  [exchanged_by_x(): lax.all_to_all(flat, ('ctx', 'tp'), split_axis=0, concat_axis=0, axis_ind...]
    all_to_all x2 -> x1, starting transfers between devices: 16.8 us -> 12 us  [exchanged(): lax.all_to_all(flat, ('ctx', 'tp'), split_axis=0, concat_axis=0, axis_ind...]
    all_to_all x2 -> x1, waiting for transfers between devices: 2.01 us -> 2 us  [exchanged(): lax.all_to_all(flat, ('ctx', 'tp'), split_axis=0, concat_axis=0, axis_ind...]
where the time goes in v6:
time: 94.6 us; the launch traced here: 94.1 us
  starting transfers between devices  49.3 us (52%)
  waiting for transfers between devices  24.5 us (26%)
  Pallas kernels  11.4 us (12%)
  between operations  5.49 us (6%)
  local copies, waits for them, and re-layouts  2.15 us (2%)
  other arithmetic  1.27 us (1%)
    ppermute x8, starting transfers between devices, sent_over(): return lax.ppermute(block, ('pipe', 'tp'), route)  22.9 us
    all_to_all x1, starting transfers between devices, exchanged(): lax.all_to_all(flat, ('ctx', 'tp'), split_axis=0, concat_axis=0, axis_ind...  12 us
    ppermute x8, waiting for transfers between devices, sent_over(): return lax.ppermute(block, ('pipe', 'tp'), route)  10.5 us
    ppermute x6, waiting for transfers between devices, moved(): lax.ppermute(block, 'pipe', [(i, (i + distance) % size) for i in range(si...  9.87 us
    ppermute x6, starting transfers between devices, moved(): lax.ppermute(block, 'pipe', [(i, (i + distance) % size) for i in range(si...  7.9 us
    pallas_call x1, Pallas kernels, run_layers(): pl.pallas_call(layers_kernel, out_shape=(kv_shape, kv_shape) + (shape(2,...  6.53 us
    all_to_all x1, starting transfers between devices, exchanged_by_x(): lax.all_to_all(flat, ('ctx', 'tp'), split_axis=0, concat_axis=0, axis_ind...  4.77 us
    ppermute x5, waiting for transfers between devices, swapped(): return lax.ppermute(block, 'tp', [(i, i ^ 1) for i in range(size)])  2.09 us
  transfers between devices with their start and end apart: 21, of which 9 were waited for; matrix products, arithmetic and copies ran while one was open for 2% of the time, Pallas kernels for 1%

profile of v6, /device:TPU:1, one launch (start us, length us, event | category | flops | bytes accessed | tf_op | source)
XLA Modules:
  0.0 94.1 jit_solution(4737381837410458213)
XLA Ops:
  0.6 0.8 pad_maximum_fusion.kv_in
  1.4 0.9 %spread.1 = bf16[32,2,2,16,128]{4,3,2,1,0:T(8,128)(2,1)} custom-call(bf16[2,16,1024]{2,1,0:T(8,128)(2,1)S(1)} %pad_maximum_fusion.kv_in), custom_call_target="tpu_custom_call" | custom-call | tf_op jit(solution)/shard_map/spread/pallas_call | solution.py:74
  2.4 12.0 %all-to-all-start = ((bf16[32,64,128]{2,1,0:T(8,128)(2,1)}), bf16[32,64,128]{2,1,0:T(8,128)(2,1)S(1)}, u32[]{:S(2)}, u32[]{:S(2)}) async-start(bf16[32,64,128]{2,1,0:T(8,128)(2,1)} %bitcast.1), calls=%async_computation | async-start | bytes 1048576 | tf_op jit(solution)/shard_map/all_to_all | solution.py:390
  14.7 3.0 %collective-permute-start.7 = (bf16[2,128,512]{2,1,0:T(8,128)(2,1)S(1)}, bf16[2,128,512]{2,1,0:T(8,128)(2,1)S(1)}, u32[]{:S(2)}, u32[]{:S(2)}) collective-permute-start(bf16[2,128,512]{2,1,0:T(8,128)(2,1)S(1)} %get-tuple-element.18), channel_id=1, source_target_pairs={{0,64},{2,66},{4,68},{6,70},{1,129},{3,131},{5,133},{7,135},{64,0}... | collective-permute-start | bytes 786440 | tf_op jit(solution)/shard_map/ppermute | solution.py:371
  17.7 3.0 %collective-permute-start.8 = (bf16[2,128,512]{2,1,0:T(8,128)(2,1)S(1)}, bf16[2,128,512]{2,1,0:T(8,128)(2,1)S(1)}, u32[]{:S(2)}, u32[]{:S(2)}) collective-permute-start(bf16[2,128,512]{2,1,0:T(8,128)(2,1)S(1)} %get-tuple-element.19), channel_id=1, source_target_pairs={{0,1},{2,3},{4,5},{6,7},{1,193},{3,195},{5,197},{7,199},{64,64},{6... | collective-permute-start | bytes 786440 | tf_op jit(solution)/shard_map/ppermute | solution.py:371
  20.7 1.4 %collective-permute-start.9 = (bf16[2,128,512]{2,1,0:T(8,128)(2,1)S(1)}, bf16[2,128,512]{2,1,0:T(8,128)(2,1)S(1)}, u32[]{:S(2)}, u32[]{:S(2)}) collective-permute-start(bf16[2,128,512]{2,1,0:T(8,128)(2,1)S(1)} %get-tuple-element.20), channel_id=1, source_target_pairs={{0,65},{2,67},{4,69},{6,71},{1,128},{3,130},{5,132},{7,134},{64,1}... | collective-permute-start | bytes 786440 | tf_op jit(solution)/shard_map/ppermute | solution.py:371
  22.2 0.7 copy-done.2
  22.8 0.6 dynamic_slice.66
  24.9 0.7 fusion.6
  28.7 2.0 %all-to-all-done = bf16[32,64,128]{2,1,0:T(8,128)(2,1)S(1)} async-done(((bf16[32,64,128]{2,1,0:T(8,128)(2,1)}), bf16[32,64,128]{2,1,0:T(8,128)(2,1)S(1)}, u32[]{:S(2)}, u32[]{:S(2)}) %all-to-all-start) | async-done | bytes 524320 | tf_op jit(solution)/shard_map/all_to_all | solution.py:390
  30.9 3.0 %collective-permute-start.1 = (bf16[20,2,16,128]{3,2,1,0:T(8,128)(2,1)S(1)}, bf16[20,2,16,128]{3,2,1,0:T(8,128)(2,1)S(1)}, u32[]{:S(2)}, u32[]{:S(2)}) collective-permute-start(bf16[20,2,16,128]{3,2,1,0:T(8,128)(2,1)S(1)} %bitcast.80), channel_id=1, source_target_pairs={{0,128},{64,192},{128,0},{192,64},{1,129},{65,193},{129,1},{193,65... | collective-permute-start | bytes 491528 | tf_op jit(solution)/shard_map/ppermute | solution.py:356
  33.9 0.8 collective-permute-start.2
  34.7 0.7 collective-permute-start
  35.4 7.0 %collective-permute-start.10 = (bf16[2,128,512]{2,1,0:T(8,128)(2,1)S(1)}, bf16[2,128,512]{2,1,0:T(8,128)(2,1)S(1)}, u32[]{:S(2)}, u32[]{:S(2)}) collective-permute-start(bf16[2,128,512]{2,1,0:T(8,128)(2,1)S(1)} %get-tuple-element.21), channel_id=1, source_target_pairs={{0,0},{2,2},{4,4},{6,6},{1,192},{3,194},{5,196},{7,198},{64,65},{6... | collective-permute-start | bytes 786440 | tf_op jit(solution)/shard_map/ppermute | solution.py:371
  42.6 0.5 collective-permute-start.5
  43.2 1.0 %collective-permute-start.4 = (bf16[20,2,16,128]{3,2,1,0:T(8,128)(2,1)S(1)}, bf16[20,2,16,128]{3,2,1,0:T(8,128)(2,1)S(1)}, u32[]{:S(2)}, u32[]{:S(2)}) collective-permute-start(bf16[20,2,16,128]{3,2,1,0:T(8,128)(2,1)S(1)} %collective-permute-done.a1), channel_id=1, source_target_pairs={{0,1},{1,0},{2,3},{3,2},{4,5},{5,4},{6,7},{7,6},{8,9},{9,8},{10,11... | collective-permute-start | bytes 491528 | tf_op jit(solution)/shard_map/ppermute | solution.py:361
  44.3 2.2 %collective-permute-done.10.q3 = bf16[2,128,512]{2,1,0:T(8,128)(2,1)S(1)} collective-permute-done((bf16[2,128,512]{2,1,0:T(8,128)(2,1)S(1)}, bf16[2,128,512]{2,1,0:T(8,128)(2,1)S(1)}, u32[]{:S(2)}, u32[]{:S(2)}) %collective-permute-start.10) | collective-permute-done | bytes 262176 | tf_op jit(solution)/shard_map/ppermute | solution.py:371
  46.5 6.5 %layers.1 = (bf16[4,2,20,16,128]{4,3,2,1,0:T(8,128)(2,1)S(1)}, bf16[4,2,20,16,128]{4,3,2,1,0:T(8,128)(2,1)S(1)}, bf16[2,128,512]{2,1,0:T(8,128)(2,1)S(1)}, bf16[...) custom-call(f32[128,640]{1,0:T(8,128)S(1)} %fusion.1.bias_in, ...), custom_call_target="tpu_custom_call" | custom-call | tf_op jit(solution)/shard_map/layers/pallas_call | solution.py:231
  53.1 2.1 %collective-permute-done.15 = bf16[4,2,20,16,128]{4,3,2,1,0:T(8,128)(2,1)S(1)} collective-permute-done((bf16[4,2,20,16,128]{4,3,2,1,0:T(8,128)(2,1)S(1)}, bf16[4,2,20,16,128]{4,3,2,1,0:T(8,128)(2,1)S(1)}, u32[]{:S(2)}, u32[]{:S(2)}) %collective-permute-start.15) | collective-permute-done | bytes 655392 | tf_op jit(solution)/shard_map/ppermute | solution.py:361
  55.4 2.8 %collective-permute-start.18 = (bf16[2,20,16,128]{3,2,1,0:T(8,128)(2,1)S(1)}, bf16[2,20,16,128]{3,2,1,0:T(8,128)(2,1)S(1)}, u32[]{:S(2)}, u32[]{:S(2)}) collective-permute-start(bf16[2,20,16,128]{3,2,1,0:T(8,128)(2,1)S(1)} %get-tuple-element.32), channel_id=1, source_target_pairs={{0,192},{64,0},{128,64},{192,128},{1,193},{65,1},{129,65},{193,129... | collective-permute-start | bytes 491528 | tf_op jit(solution)/shard_map/ppermute | solution.py:356
  58.2 0.7 collective-permute-start.16
  58.8 5.9 %collective-permute-done.18.p3 = bf16[2,20,16,128]{3,2,1,0:T(8,128)(2,1)S(1)} collective-permute-done((bf16[2,20,16,128]{3,2,1,0:T(8,128)(2,1)S(1)}, bf16[2,20,16,128]{3,2,1,0:T(8,128)(2,1)S(1)}, u32[]{:S(2)}, u32[]{:S(2)}) %collective-permute-start.18) | collective-permute-done | bytes 163872 | tf_op jit(solution)/shard_map/ppermute | solution.py:356
  64.9 3.9 %collective-permute-done.16.p1 = bf16[2,20,16,128]{3,2,1,0:T(8,128)(2,1)S(1)} collective-permute-done((bf16[2,20,16,128]{3,2,1,0:T(8,128)(2,1)S(1)}, bf16[2,20,16,128]{3,2,1,0:T(8,128)(2,1)S(1)}, u32[]{:S(2)}, u32[]{:S(2)}) %collective-permute-start.16) | collective-permute-done | bytes 163872 | tf_op jit(solution)/shard_map/ppermute | solution.py:356
  68.7 1.9 %place.1 = bf16[4,8,2,2,16,128]{5,4,3,2,1,0:T(8,128)(2,1)} custom-call(s32[8]{0:T(128)S(1)} %copy-done.2, bf16[2,20,16,128]{3,2,1,0:T(8,128)(2,1)S(1)} %get-tuple-element.35.p0, bf16[2,20,16,128]{3,2,1,0:T(8,128)(2,1)S(1)} %collective-permute-done.16.p1, bf16[2,20,16,128]{3,2,1,0:T(8,128)(2,1)S(1)} %collective-permute-done.17.p2, ...), custom_call_target="tpu_custom_call" | custom-call | tf_op jit(solution)/shard_map/place/pallas_call | solution.py:287
  70.6 4.8 %all-to-all-start.1 = ((bf16[32,64,128]{2,1,0:T(8,128)(2,1)}), bf16[32,64,128]{2,1,0:T(8,128)(2,1)S(1)}, u32[]{:S(2)}, u32[]{:S(2)}) async-start(bf16[32,64,128]{2,1,0:T(8,128)(2,1)} %bitcast.21), calls=%async_computation.1 | async-start | bytes 1048576 | tf_op jit(solution)/shard_map/all_to_all | solution.py:403
  75.4 1.2 %collective-permute-start.11 = (bf16[2,128,512]{2,1,0:T(8,128)(2,1)S(1)}, bf16[2,128,512]{2,1,0:T(8,128)(2,1)S(1)}, u32[]{:S(2)}, u32[]{:S(2)}) collective-permute-start(bf16[2,128,512]{2,1,0:T(8,128)(2,1)S(1)} %get-tuple-element.22), channel_id=1, source_target_pairs={{64,0},{66,2},{68,4},{70,6},{129,1},{131,3},{133,5},{135,7},{0,64}... | collective-permute-start | bytes 786440 | tf_op jit(solution)/shard_map/ppermute | solution.py:371
  76.5 1.9 %collective-permute-start.12 = (bf16[2,128,512]{2,1,0:T(8,128)(2,1)S(1)}, bf16[2,128,512]{2,1,0:T(8,128)(2,1)S(1)}, u32[]{:S(2)}, u32[]{:S(2)}) collective-permute-start(bf16[2,128,512]{2,1,0:T(8,128)(2,1)S(1)} %get-tuple-element.23), channel_id=1, source_target_pairs={{1,0},{3,2},{5,4},{7,6},{193,1},{195,3},{197,5},{199,7},{64,64},{6... | collective-permute-start | bytes 786440 | tf_op jit(solution)/shard_map/ppermute | solution.py:371
  78.7 5.1 %collective-permute-start.14 = (bf16[2,128,512]{2,1,0:T(8,128)(2,1)S(1)}, bf16[2,128,512]{2,1,0:T(8,128)(2,1)S(1)}, u32[]{:S(2)}, u32[]{:S(2)}) collective-permute-start(bf16[2,128,512]{2,1,0:T(8,128)(2,1)S(1)} %get-tuple-element.25), channel_id=1, source_target_pairs={{0,0},{2,2},{4,4},{6,6},{192,1},{194,3},{196,5},{198,7},{65,64},{6... | collective-permute-start | bytes 786440 | tf_op jit(solution)/shard_map/ppermute | solution.py:371
  84.0 7.3 %collective-permute-done.12.g1 = bf16[2,128,512]{2,1,0:T(8,128)(2,1)S(1)} collective-permute-done((bf16[2,128,512]{2,1,0:T(8,128)(2,1)S(1)}, bf16[2,128,512]{2,1,0:T(8,128)(2,1)S(1)}, u32[]{:S(2)}, u32[]{:S(2)}) %collective-permute-start.12) | collective-permute-done | bytes 262176 | tf_op jit(solution)/shard_map/ppermute | solution.py:371
  91.3 0.8 collective-permute-done.14.g3
  92.1 1.0 %assemble.1 = (bf16[128,2048]{1,0:T(8,128)(2,1)}, bf16[128,2048]{1,0:T(8,128)(2,1)}) custom-call(bf16[2,128,512]{2,1,0:T(8,128)(2,1)S(1)} %collective-permute-done.11.g0, bf16[2,128,512]{2,1,0:T(8,128)(2,1)S(1)} %collective-permute-done.12.g1, bf16[2,128,512]{2,1,0:T(8,128)(2,1)S(1)} %collective-permute-done.13.g2, ...), custom_call_target="tpu_custom_call" | custom-call | tf_op jit(solution)/shard_map/assemble/pallas_call | solution.py:343
  93.2 0.7 total.1
  (39 shorter events, 1.9 us)
Async XLA Ops:
  2.4 12.0 %copy-start = (bf16[1,128,2048]{2,1,0:T(8,128)(2,1)S(1)}, bf16[1,128,2048]{2,1,0:T(8,128)(2,1)}, u32[]{:S(2)}) copy-start(bf16[1,128,2048]{2,1,0:T(8,128)(2,1)} %param.6) | copy-start | bytes 1572868
  2.4 12.0 %copy-start.1 = (bf16[1,128,2048]{2,1,0:T(8,128)(2,1)S(1)}, bf16[1,128,2048]{2,1,0:T(8,128)(2,1)}, u32[]{:S(2)}) copy-start(bf16[1,128,2048]{2,1,0:T(8,128)(2,1)} %param.11) | copy-start | bytes 1572868
  2.4 28.3 %all-to-all-start = ((bf16[32,64,128]{2,1,0:T(8,128)(2,1)}), bf16[32,64,128]{2,1,0:T(8,128)(2,1)S(1)}, u32[]{:S(2)}, u32[]{:S(2)}) async-start(bf16[32,64,128]{2,1,0:T(8,128)(2,1)} %bitcast.1), calls=%async_computation | async-start | bytes 1048576 | tf_op jit(solution)/shard_map/all_to_all | solution.py:390
  14.7 19.9 %collective-permute-start.7 = (bf16[2,128,512]{2,1,0:T(8,128)(2,1)S(1)}, bf16[2,128,512]{2,1,0:T(8,128)(2,1)S(1)}, u32[]{:S(2)}, u32[]{:S(2)}) collective-permute-start(bf16[2,128,512]{2,1,0:T(8,128)(2,1)S(1)} %get-tuple-element.18), channel_id=1, source_target_pairs={{0,64},{2,66},{4,68},{6,70},{1,129},{3,131},{5,133},{7,135},{64,0}... | collective-permute-start | bytes 786440 | tf_op jit(solution)/shard_map/ppermute | solution.py:371
  17.7 17.7 %collective-permute-start.8 = (bf16[2,128,512]{2,1,0:T(8,128)(2,1)S(1)}, bf16[2,128,512]{2,1,0:T(8,128)(2,1)S(1)}, u32[]{:S(2)}, u32[]{:S(2)}) collective-permute-start(bf16[2,128,512]{2,1,0:T(8,128)(2,1)S(1)} %get-tuple-element.19), channel_id=1, source_target_pairs={{0,1},{2,3},{4,5},{6,7},{1,193},{3,195},{5,197},{7,199},{64,64},{6... | collective-permute-start | bytes 786440 | tf_op jit(solution)/shard_map/ppermute | solution.py:371
  20.7 21.7 %collective-permute-start.9 = (bf16[2,128,512]{2,1,0:T(8,128)(2,1)S(1)}, bf16[2,128,512]{2,1,0:T(8,128)(2,1)S(1)}, u32[]{:S(2)}, u32[]{:S(2)}) collective-permute-start(bf16[2,128,512]{2,1,0:T(8,128)(2,1)S(1)} %get-tuple-element.20), channel_id=1, source_target_pairs={{0,65},{2,67},{4,69},{6,71},{1,128},{3,130},{5,132},{7,134},{64,1}... | collective-permute-start | bytes 786440 | tf_op jit(solution)/shard_map/ppermute | solution.py:371
  22.2 0.7 copy-start.2
  30.9 11.7 %collective-permute-start.1 = (bf16[20,2,16,128]{3,2,1,0:T(8,128)(2,1)S(1)}, bf16[20,2,16,128]{3,2,1,0:T(8,128)(2,1)S(1)}, u32[]{:S(2)}, u32[]{:S(2)}) collective-permute-start(bf16[20,2,16,128]{3,2,1,0:T(8,128)(2,1)S(1)} %bitcast.80), channel_id=1, source_target_pairs={{0,128},{64,192},{128,0},{192,64},{1,129},{65,193},{129,1},{193,65... | collective-permute-start | bytes 491528 | tf_op jit(solution)/shard_map/ppermute | solution.py:356
  33.9 1.5 %copy-start.3 = (s32[1024]{0:T(1024)S(1)}, s32[1024]{0:T(1024)}, u32[]{:S(2)}) copy-start(s32[1024]{0:T(1024)} %param.9) | copy-start | bytes 12292
  33.9 9.2 %collective-permute-start.2 = (bf16[20,2,16,128]{3,2,1,0:T(8,128)(2,1)S(1)}, bf16[20,2,16,128]{3,2,1,0:T(8,128)(2,1)S(1)}, u32[]{:S(2)}, u32[]{:S(2)}) collective-permute-start(bf16[20,2,16,128]{3,2,1,0:T(8,128)(2,1)S(1)} %bitcast.79), channel_id=1, source_target_pairs={{0,192},{64,0},{128,64},{192,128},{1,193},{65,1},{129,65},{193,129... | collective-permute-start | bytes 491528 | tf_op jit(solution)/shard_map/ppermute | solution.py:356
  34.7 8.5 %collective-permute-start = (bf16[20,2,16,128]{3,2,1,0:T(8,128)(2,1)S(1)}, bf16[20,2,16,128]{3,2,1,0:T(8,128)(2,1)S(1)}, u32[]{:S(2)}, u32[]{:S(2)}) collective-permute-start(bf16[20,2,16,128]{3,2,1,0:T(8,128)(2,1)S(1)} %bitcast.81), channel_id=1, source_target_pairs={{0,64},{64,128},{128,192},{192,0},{1,65},{65,129},{129,193},{193,1... | collective-permute-start | bytes 491528 | tf_op jit(solution)/shard_map/ppermute | solution.py:356
  35.4 11.0 %collective-permute-start.10 = (bf16[2,128,512]{2,1,0:T(8,128)(2,1)S(1)}, bf16[2,128,512]{2,1,0:T(8,128)(2,1)S(1)}, u32[]{:S(2)}, u32[]{:S(2)}) collective-permute-start(bf16[2,128,512]{2,1,0:T(8,128)(2,1)S(1)} %get-tuple-element.21), channel_id=1, source_target_pairs={{0,0},{2,2},{4,4},{6,6},{1,192},{3,194},{5,196},{7,198},{64,65},{6... | collective-permute-start | bytes 786440 | tf_op jit(solution)/shard_map/ppermute | solution.py:371
  42.5 4.0 %collective-permute-start.3 = (bf16[20,2,16,128]{3,2,1,0:T(8,128)(2,1)S(1)}, bf16[20,2,16,128]{3,2,1,0:T(8,128)(2,1)S(1)}, u32[]{:S(2)}, u32[]{:S(2)}) collective-permute-start(bf16[20,2,16,128]{3,2,1,0:T(8,128)(2,1)S(1)} %bitcast.72), channel_id=1, source_target_pairs={{0,1},{1,0},{2,3},{3,2},{4,5},{5,4},{6,7},{7,6},{8,9},{9,8},{10,11... | collective-permute-start | bytes 491528 | tf_op jit(solution)/shard_map/ppermute | solution.py:361
  42.6 3.9 %collective-permute-start.5 = (bf16[20,2,16,128]{3,2,1,0:T(8,128)(2,1)S(1)}, bf16[20,2,16,128]{3,2,1,0:T(8,128)(2,1)S(1)}, u32[]{:S(2)}, u32[]{:S(2)}) collective-permute-start(bf16[20,2,16,128]{3,2,1,0:T(8,128)(2,1)S(1)} %collective-permute-done.1.a2), channel_id=1, source_target_pairs={{0,1},{1,0},{2,3},{3,2},{4,5},{5,4},{6,7},{7,6},{8,9},{9,8},{10,11... | collective-permute-start | bytes 491528 | tf_op jit(solution)/shard_map/ppermute | solution.py:361
  43.1 3.4 %collective-permute-start.6 = (bf16[20,2,16,128]{3,2,1,0:T(8,128)(2,1)S(1)}, bf16[20,2,16,128]{3,2,1,0:T(8,128)(2,1)S(1)}, u32[]{:S(2)}, u32[]{:S(2)}) collective-permute-start(bf16[20,2,16,128]{3,2,1,0:T(8,128)(2,1)S(1)} %collective-permute-done.2.a3), channel_id=1, source_target_pairs={{0,1},{1,0},{2,3},{3,2},{4,5},{5,4},{6,7},{7,6},{8,9},{9,8},{10,11... | collective-permute-start | bytes 491528 | tf_op jit(solution)/shard_map/ppermute | solution.py:361
  43.2 3.3 %collective-permute-start.4 = (bf16[20,2,16,128]{3,2,1,0:T(8,128)(2,1)S(1)}, bf16[20,2,16,128]{3,2,1,0:T(8,128)(2,1)S(1)}, u32[]{:S(2)}, u32[]{:S(2)}) collective-permute-start(bf16[20,2,16,128]{3,2,1,0:T(8,128)(2,1)S(1)} %collective-permute-done.a1), channel_id=1, source_target_pairs={{0,1},{1,0},{2,3},{3,2},{4,5},{5,4},{6,7},{7,6},{8,9},{9,8},{10,11... | collective-permute-start | bytes 491528 | tf_op jit(solution)/shard_map/ppermute | solution.py:361
  53.0 2.2 %collective-permute-start.15 = (bf16[4,2,20,16,128]{4,3,2,1,0:T(8,128)(2,1)S(1)}, bf16[4,2,20,16,128]{4,3,2,1,0:T(8,128)(2,1)S(1)}, u32[]{:S(2)}, u32[]{:S(2)}) collective-permute-start(bf16[4,2,20,16,128]{4,3,2,1,0:T(8,128)(2,1)S(1)} %get-tuple-element.29), channel_id=1, source_target_pairs={{0,1},{1,0},{2,3},{3,2},{4,5},{5,4},{6,7},{7,6},{8,9},{9,8},{10,11... | collective-permute-start | bytes 1966088 | tf_op jit(solution)/shard_map/ppermute | solution.py:361
  55.4 9.3 %collective-permute-start.18 = (bf16[2,20,16,128]{3,2,1,0:T(8,128)(2,1)S(1)}, bf16[2,20,16,128]{3,2,1,0:T(8,128)(2,1)S(1)}, u32[]{:S(2)}, u32[]{:S(2)}) collective-permute-start(bf16[2,20,16,128]{3,2,1,0:T(8,128)(2,1)S(1)} %get-tuple-element.32), channel_id=1, source_target_pairs={{0,192},{64,0},{128,64},{192,128},{1,193},{65,1},{129,65},{193,129... | collective-permute-start | bytes 491528 | tf_op jit(solution)/shard_map/ppermute | solution.py:356
  58.2 6.7 %collective-permute-start.17 = (bf16[2,20,16,128]{3,2,1,0:T(8,128)(2,1)S(1)}, bf16[2,20,16,128]{3,2,1,0:T(8,128)(2,1)S(1)}, u32[]{:S(2)}, u32[]{:S(2)}) collective-permute-start(bf16[2,20,16,128]{3,2,1,0:T(8,128)(2,1)S(1)} %get-tuple-element.33), channel_id=1, source_target_pairs={{0,128},{64,192},{128,0},{192,64},{1,129},{65,193},{129,1},{193,65... | collective-permute-start | bytes 491528 | tf_op jit(solution)/shard_map/ppermute | solution.py:356
  58.2 10.5 %collective-permute-start.16 = (bf16[2,20,16,128]{3,2,1,0:T(8,128)(2,1)S(1)}, bf16[2,20,16,128]{3,2,1,0:T(8,128)(2,1)S(1)}, u32[]{:S(2)}, u32[]{:S(2)}) collective-permute-start(bf16[2,20,16,128]{3,2,1,0:T(8,128)(2,1)S(1)} %get-tuple-element.34), channel_id=1, source_target_pairs={{0,64},{64,128},{128,192},{192,0},{1,65},{65,129},{129,193},{193,1... | collective-permute-start | bytes 491528 | tf_op jit(solution)/shard_map/ppermute | solution.py:356
  70.6 22.6 %all-to-all-start.1 = ((bf16[32,64,128]{2,1,0:T(8,128)(2,1)}), bf16[32,64,128]{2,1,0:T(8,128)(2,1)S(1)}, u32[]{:S(2)}, u32[]{:S(2)}) async-start(bf16[32,64,128]{2,1,0:T(8,128)(2,1)} %bitcast.21), calls=%async_computation.1 | async-start | bytes 1048576 | tf_op jit(solution)/shard_map/all_to_all | solution.py:403
  75.4 8.7 %collective-permute-start.11 = (bf16[2,128,512]{2,1,0:T(8,128)(2,1)S(1)}, bf16[2,128,512]{2,1,0:T(8,128)(2,1)S(1)}, u32[]{:S(2)}, u32[]{:S(2)}) collective-permute-start(bf16[2,128,512]{2,1,0:T(8,128)(2,1)S(1)} %get-tuple-element.22), channel_id=1, source_target_pairs={{64,0},{66,2},{68,4},{70,6},{129,1},{131,3},{133,5},{135,7},{0,64}... | collective-permute-start | bytes 786440 | tf_op jit(solution)/shard_map/ppermute | solution.py:371
  76.5 14.8 %collective-permute-start.12 = (bf16[2,128,512]{2,1,0:T(8,128)(2,1)S(1)}, bf16[2,128,512]{2,1,0:T(8,128)(2,1)S(1)}, u32[]{:S(2)}, u32[]{:S(2)}) collective-permute-start(bf16[2,128,512]{2,1,0:T(8,128)(2,1)S(1)} %get-tuple-element.23), channel_id=1, source_target_pairs={{1,0},{3,2},{5,4},{7,6},{193,1},{195,3},{197,5},{199,7},{64,64},{6... | collective-permute-start | bytes 786440 | tf_op jit(solution)/shard_map/ppermute | solution.py:371
  78.4 12.9 %collective-permute-start.13 = (bf16[2,128,512]{2,1,0:T(8,128)(2,1)S(1)}, bf16[2,128,512]{2,1,0:T(8,128)(2,1)S(1)}, u32[]{:S(2)}, u32[]{:S(2)}) collective-permute-start(bf16[2,128,512]{2,1,0:T(8,128)(2,1)S(1)} %get-tuple-element.24), channel_id=1, source_target_pairs={{65,0},{67,2},{69,4},{71,6},{128,1},{130,3},{132,5},{134,7},{1,64}... | collective-permute-start | bytes 786440 | tf_op jit(solution)/shard_map/ppermute | solution.py:371
  78.7 13.4 %collective-permute-start.14 = (bf16[2,128,512]{2,1,0:T(8,128)(2,1)S(1)}, bf16[2,128,512]{2,1,0:T(8,128)(2,1)S(1)}, u32[]{:S(2)}, u32[]{:S(2)}) collective-permute-start(bf16[2,128,512]{2,1,0:T(8,128)(2,1)S(1)} %get-tuple-element.25), channel_id=1, source_target_pairs={{0,0},{2,2},{4,4},{6,6},{192,1},{194,3},{196,5},{198,7},{65,64},{6... | collective-permute-start | bytes 786440 | tf_op jit(solution)/shard_map/ppermute | solution.py:371

commit v7 on v6

--- a/solution.py
+++ b/solution.py
@@ -252,35 +252,51 @@
     )(bias, *mine, *theirs, *qc_parts)
 
 
-def place_kernel(order_in, p0, p1, p2, p3, sent_out, order, parts, sent, sems, out_sems):
+def place_kernel(
+    order_in, p0, p1, p2, p3, sent_out, order, parts, sent, order_sem, sems, out_sems
+):
     pipe, _, _ = place_of()
-
-    def clear():
-        sent[...] = jnp.zeros(sent.shape, bf16)
-
-    run_copies(
-        [(order_in, order)]
-        + [
-            (x, parts.at[lax.rem(pipe + LAYERS - d, LAYERS)])
-            for d, x in enumerate((p0, p1, p2, p3))
-        ],
-        sems,
-        clear,
-    )
+    order_copy = pltpu.make_async_copy(order_in, order, order_sem)
+    order_copy.start()
+    copies = [
+        pltpu.make_async_copy(
+            x, parts.at[lax.rem(pipe + LAYERS - d, LAYERS)], sems.at[d]
+        )
+        for d, x in enumerate((p0, p1, p2, p3))
+    ]
+    for copy in copies:
+        copy.start()
+    sent[...] = jnp.zeros(sent.shape, bf16)
+    order_copy.wait()
     first = order[lax.axis_index("ctx")] - REACH
-    for c in range(sent.shape[1]):
-        j = order[c] - first
-
-        @pl.when((j >= 0) & (j <= REACH))
-        def _():
+    outs = [
+        pltpu.make_async_copy(sent.at[:, c], sent_out.at[:, c], out_sems.at[c])
+        for c in range(sent.shape[1])
+    ]
+    steps = [order[c] - first for c in range(sent.shape[1])]
+    nears = [(j >= 0) & (j <= REACH) for j in steps]
+    for near, out in zip(nears, outs):
+
+        @pl.when(jnp.logical_not(near))
+        def _(out=out):
+            out.start()
+
+    for copy in copies:
+        copy.wait()
+    for c, (j, near, out) in enumerate(zip(steps, nears, outs)):
+
+        @pl.when(near)
+        def _(c=c, j=j, out=out):
             at = pl.ds(j * TILES, TILES)
             for head in range(2):
                 total = parts[2 * head, :, at].astype(f32) + parts[2 * head + 1, :, at].astype(f32)
                 total = total.astype(bf16)
                 for k in range(2):
                     sent[:, c, k, head] = total[k]
-
-    run_copies([(sent, sent_out)], out_sems)
+            out.start()
+
+    for out in outs:
+        out.wait()
 
 
 def place(order, parts):
@@ -293,8 +309,9 @@
             pltpu.SMEM(order.shape, jnp.int32),
             pltpu.VMEM((LAYERS,) + parts[0].shape, bf16),
             pltpu.VMEM((TILES, order.shape[0], 2, 2, TILE, HEAD_DIM), bf16),
-            pltpu.SemaphoreType.DMA((1 + LAYERS,)),
-            pltpu.SemaphoreType.DMA((1,)),
+            pltpu.SemaphoreType.DMA,
+            pltpu.SemaphoreType.DMA((LAYERS,)),
+            pltpu.SemaphoreType.DMA(order.shape),
         ],
         compiler_params=PARAMS,
         name="place",

time: 94.6 us -> 94.5 us (level)
  no operation moved by 1% of the time
where the time goes in v7:
time: 94.5 us; the launch traced here: 94 us
  starting transfers between devices  49.3 us (52%)
  waiting for transfers between devices  24.5 us (26%)
  Pallas kernels  11.3 us (12%)
  between operations  5.49 us (6%)
  local copies, waits for them, and re-layouts  2.15 us (2%)
  other arithmetic  1.27 us (1%)
    ppermute x8, starting transfers between devices, sent_over(): return lax.ppermute(block, ('pipe', 'tp'), route)  22.9 us
    all_to_all x1, starting transfers between devices, exchanged(): lax.all_to_all(flat, ('ctx', 'tp'), split_axis=0, concat_axis=0, axis_ind...  12 us
    ppermute x8, waiting for transfers between devices, sent_over(): return lax.ppermute(block, ('pipe', 'tp'), route)  10.5 us
    ppermute x6, waiting for transfers between devices, moved(): lax.ppermute(block, 'pipe', [(i, (i + distance) % size) for i in range(si...  9.87 us
    ppermute x6, starting transfers between devices, moved(): lax.ppermute(block, 'pipe', [(i, (i + distance) % size) for i in range(si...  7.9 us
    pallas_call x1, Pallas kernels, run_layers(): pl.pallas_call(layers_kernel, out_shape=(kv_shape, kv_shape) + (shape(2,...  6.53 us
    all_to_all x1, starting transfers between devices, exchanged_by_x(): lax.all_to_all(flat, ('ctx', 'tp'), split_axis=0, concat_axis=0, axis_ind...  4.76 us
    ppermute x5, waiting for transfers between devices, swapped(): return lax.ppermute(block, 'tp', [(i, i ^ 1) for i in range(size)])  2.09 us
  transfers between devices with their start and end apart: 21, of which 9 were waited for; matrix products, arithmetic and copies ran while one was open for 2% of the time, Pallas kernels for 1%

profile of v7, /device:TPU:1, one launch (start us, length us, event | category | flops | bytes accessed | tf_op | source)
XLA Modules:
  0.0 94.0 jit_solution(13230458005342316039)
XLA Ops:
  0.6 0.8 pad_maximum_fusion.kv_in
  1.4 0.9 %spread.1 = bf16[32,2,2,16,128]{4,3,2,1,0:T(8,128)(2,1)} custom-call(bf16[2,16,1024]{2,1,0:T(8,128)(2,1)S(1)} %pad_maximum_fusion.kv_in), custom_call_target="tpu_custom_call" | custom-call | tf_op jit(solution)/shard_map/spread/pallas_call | solution.py:74
  2.4 12.0 %all-to-all-start = ((bf16[32,64,128]{2,1,0:T(8,128)(2,1)}), bf16[32,64,128]{2,1,0:T(8,128)(2,1)S(1)}, u32[]{:S(2)}, u32[]{:S(2)}) async-start(bf16[32,64,128]{2,1,0:T(8,128)(2,1)} %bitcast.1), calls=%async_computation | async-start | bytes 1048576 | tf_op jit(solution)/shard_map/all_to_all | solution.py:407
  14.7 3.0 %collective-permute-start.7 = (bf16[2,128,512]{2,1,0:T(8,128)(2,1)S(1)}, bf16[2,128,512]{2,1,0:T(8,128)(2,1)S(1)}, u32[]{:S(2)}, u32[]{:S(2)}) collective-permute-start(bf16[2,128,512]{2,1,0:T(8,128)(2,1)S(1)} %get-tuple-element.18), channel_id=1, source_target_pairs={{0,64},{2,66},{4,68},{6,70},{1,129},{3,131},{5,133},{7,135},{64,0}... | collective-permute-start | bytes 786440 | tf_op jit(solution)/shard_map/ppermute | solution.py:388
  17.7 3.0 %collective-permute-start.8 = (bf16[2,128,512]{2,1,0:T(8,128)(2,1)S(1)}, bf16[2,128,512]{2,1,0:T(8,128)(2,1)S(1)}, u32[]{:S(2)}, u32[]{:S(2)}) collective-permute-start(bf16[2,128,512]{2,1,0:T(8,128)(2,1)S(1)} %get-tuple-element.19), channel_id=1, source_target_pairs={{0,1},{2,3},{4,5},{6,7},{1,193},{3,195},{5,197},{7,199},{64,64},{6... | collective-permute-start | bytes 786440 | tf_op jit(solution)/shard_map/ppermute | solution.py:388
  20.7 1.4 %collective-permute-start.9 = (bf16[2,128,512]{2,1,0:T(8,128)(2,1)S(1)}, bf16[2,128,512]{2,1,0:T(8,128)(2,1)S(1)}, u32[]{:S(2)}, u32[]{:S(2)}) collective-permute-start(bf16[2,128,512]{2,1,0:T(8,128)(2,1)S(1)} %get-tuple-element.20), channel_id=1, source_target_pairs={{0,65},{2,67},{4,69},{6,71},{1,128},{3,130},{5,132},{7,134},{64,1}... | collective-permute-start | bytes 786440 | tf_op jit(solution)/shard_map/ppermute | solution.py:388
  22.2 0.7 copy-done.2
  22.8 0.6 dynamic_slice.66
  24.9 0.7 fusion.6
  28.7 2.0 %all-to-all-done = bf16[32,64,128]{2,1,0:T(8,128)(2,1)S(1)} async-done(((bf16[32,64,128]{2,1,0:T(8,128)(2,1)}), bf16[32,64,128]{2,1,0:T(8,128)(2,1)S(1)}, u32[]{:S(2)}, u32[]{:S(2)}) %all-to-all-start) | async-done | bytes 524320 | tf_op jit(solution)/shard_map/all_to_all | solution.py:407
  30.9 3.0 %collective-permute-start.1 = (bf16[20,2,16,128]{3,2,1,0:T(8,128)(2,1)S(1)}, bf16[20,2,16,128]{3,2,1,0:T(8,128)(2,1)S(1)}, u32[]{:S(2)}, u32[]{:S(2)}) collective-permute-start(bf16[20,2,16,128]{3,2,1,0:T(8,128)(2,1)S(1)} %bitcast.80), channel_id=1, source_target_pairs={{0,128},{64,192},{128,0},{192,64},{1,129},{65,193},{129,1},{193,65... | collective-permute-start | bytes 491528 | tf_op jit(solution)/shard_map/ppermute | solution.py:373
  33.9 0.8 collective-permute-start.2
  34.7 0.7 collective-permute-start
  35.4 7.0 %collective-permute-start.10 = (bf16[2,128,512]{2,1,0:T(8,128)(2,1)S(1)}, bf16[2,128,512]{2,1,0:T(8,128)(2,1)S(1)}, u32[]{:S(2)}, u32[]{:S(2)}) collective-permute-start(bf16[2,128,512]{2,1,0:T(8,128)(2,1)S(1)} %get-tuple-element.21), channel_id=1, source_target_pairs={{0,0},{2,2},{4,4},{6,6},{1,192},{3,194},{5,196},{7,198},{64,65},{6... | collective-permute-start | bytes 786440 | tf_op jit(solution)/shard_map/ppermute | solution.py:388
  42.6 0.5 collective-permute-start.5
  43.2 1.0 %collective-permute-start.4 = (bf16[20,2,16,128]{3,2,1,0:T(8,128)(2,1)S(1)}, bf16[20,2,16,128]{3,2,1,0:T(8,128)(2,1)S(1)}, u32[]{:S(2)}, u32[]{:S(2)}) collective-permute-start(bf16[20,2,16,128]{3,2,1,0:T(8,128)(2,1)S(1)} %collective-permute-done.a1), channel_id=1, source_target_pairs={{0,1},{1,0},{2,3},{3,2},{4,5},{5,4},{6,7},{7,6},{8,9},{9,8},{10,11... | collective-permute-start | bytes 491528 | tf_op jit(solution)/shard_map/ppermute | solution.py:378
  44.3 2.2 %collective-permute-done.10.q3 = bf16[2,128,512]{2,1,0:T(8,128)(2,1)S(1)} collective-permute-done((bf16[2,128,512]{2,1,0:T(8,128)(2,1)S(1)}, bf16[2,128,512]{2,1,0:T(8,128)(2,1)S(1)}, u32[]{:S(2)}, u32[]{:S(2)}) %collective-permute-start.10) | collective-permute-done | bytes 262176 | tf_op jit(solution)/shard_map/ppermute | solution.py:388
  46.5 6.5 %layers.1 = (bf16[4,2,20,16,128]{4,3,2,1,0:T(8,128)(2,1)S(1)}, bf16[4,2,20,16,128]{4,3,2,1,0:T(8,128)(2,1)S(1)}, bf16[2,128,512]{2,1,0:T(8,128)(2,1)S(1)}, bf16[...) custom-call(f32[128,640]{1,0:T(8,128)S(1)} %fusion.1.bias_in, ...), custom_call_target="tpu_custom_call" | custom-call | tf_op jit(solution)/shard_map/layers/pallas_call | solution.py:231
  53.1 2.1 %collective-permute-done.15 = bf16[4,2,20,16,128]{4,3,2,1,0:T(8,128)(2,1)S(1)} collective-permute-done((bf16[4,2,20,16,128]{4,3,2,1,0:T(8,128)(2,1)S(1)}, bf16[4,2,20,16,128]{4,3,2,1,0:T(8,128)(2,1)S(1)}, u32[]{:S(2)}, u32[]{:S(2)}) %collective-permute-start.15) | collective-permute-done | bytes 655392 | tf_op jit(solution)/shard_map/ppermute | solution.py:378
  55.4 2.8 %collective-permute-start.18 = (bf16[2,20,16,128]{3,2,1,0:T(8,128)(2,1)S(1)}, bf16[2,20,16,128]{3,2,1,0:T(8,128)(2,1)S(1)}, u32[]{:S(2)}, u32[]{:S(2)}) collective-permute-start(bf16[2,20,16,128]{3,2,1,0:T(8,128)(2,1)S(1)} %get-tuple-element.32), channel_id=1, source_target_pairs={{0,192},{64,0},{128,64},{192,128},{1,193},{65,1},{129,65},{193,129... | collective-permute-start | bytes 491528 | tf_op jit(solution)/shard_map/ppermute | solution.py:373
  58.2 0.7 collective-permute-start.16
  58.8 5.9 %collective-permute-done.18.p3 = bf16[2,20,16,128]{3,2,1,0:T(8,128)(2,1)S(1)} collective-permute-done((bf16[2,20,16,128]{3,2,1,0:T(8,128)(2,1)S(1)}, bf16[2,20,16,128]{3,2,1,0:T(8,128)(2,1)S(1)}, u32[]{:S(2)}, u32[]{:S(2)}) %collective-permute-start.18) | collective-permute-done | bytes 163872 | tf_op jit(solution)/shard_map/ppermute | solution.py:373
  64.9 3.9 %collective-permute-done.16.p1 = bf16[2,20,16,128]{3,2,1,0:T(8,128)(2,1)S(1)} collective-permute-done((bf16[2,20,16,128]{3,2,1,0:T(8,128)(2,1)S(1)}, bf16[2,20,16,128]{3,2,1,0:T(8,128)(2,1)S(1)}, u32[]{:S(2)}, u32[]{:S(2)}) %collective-permute-start.16) | collective-permute-done | bytes 163872 | tf_op jit(solution)/shard_map/ppermute | solution.py:373
  68.7 1.8 %place.1 = bf16[4,8,2,2,16,128]{5,4,3,2,1,0:T(8,128)(2,1)} custom-call(s32[8]{0:T(128)S(1)} %copy-done.2, bf16[2,20,16,128]{3,2,1,0:T(8,128)(2,1)S(1)} %get-tuple-element.35.p0, bf16[2,20,16,128]{3,2,1,0:T(8,128)(2,1)S(1)} %collective-permute-done.16.p1, bf16[2,20,16,128]{3,2,1,0:T(8,128)(2,1)S(1)} %collective-permute-done.17.p2, ...), custom_call_target="tpu_custom_call" | custom-call | tf_op jit(solution)/shard_map/place/pallas_call | solution.py:303
  70.5 4.8 %all-to-all-start.1 = ((bf16[32,64,128]{2,1,0:T(8,128)(2,1)}), bf16[32,64,128]{2,1,0:T(8,128)(2,1)S(1)}, u32[]{:S(2)}, u32[]{:S(2)}) async-start(bf16[32,64,128]{2,1,0:T(8,128)(2,1)} %bitcast.21), calls=%async_computation.1 | async-start | bytes 1048576 | tf_op jit(solution)/shard_map/all_to_all | solution.py:420
  75.3 1.2 %collective-permute-start.11 = (bf16[2,128,512]{2,1,0:T(8,128)(2,1)S(1)}, bf16[2,128,512]{2,1,0:T(8,128)(2,1)S(1)}, u32[]{:S(2)}, u32[]{:S(2)}) collective-permute-start(bf16[2,128,512]{2,1,0:T(8,128)(2,1)S(1)} %get-tuple-element.22), channel_id=1, source_target_pairs={{64,0},{66,2},{68,4},{70,6},{129,1},{131,3},{133,5},{135,7},{0,64}... | collective-permute-start | bytes 786440 | tf_op jit(solution)/shard_map/ppermute | solution.py:388
  76.5 1.9 %collective-permute-start.12 = (bf16[2,128,512]{2,1,0:T(8,128)(2,1)S(1)}, bf16[2,128,512]{2,1,0:T(8,128)(2,1)S(1)}, u32[]{:S(2)}, u32[]{:S(2)}) collective-permute-start(bf16[2,128,512]{2,1,0:T(8,128)(2,1)S(1)} %get-tuple-element.23), channel_id=1, source_target_pairs={{1,0},{3,2},{5,4},{7,6},{193,1},{195,3},{197,5},{199,7},{64,64},{6... | collective-permute-start | bytes 786440 | tf_op jit(solution)/shard_map/ppermute | solution.py:388
  78.7 5.1 %collective-permute-start.14 = (bf16[2,128,512]{2,1,0:T(8,128)(2,1)S(1)}, bf16[2,128,512]{2,1,0:T(8,128)(2,1)S(1)}, u32[]{:S(2)}, u32[]{:S(2)}) collective-permute-start(bf16[2,128,512]{2,1,0:T(8,128)(2,1)S(1)} %get-tuple-element.25), channel_id=1, source_target_pairs={{0,0},{2,2},{4,4},{6,6},{192,1},{194,3},{196,5},{198,7},{65,64},{6... | collective-permute-start | bytes 786440 | tf_op jit(solution)/shard_map/ppermute | solution.py:388
  84.0 7.3 %collective-permute-done.12.g1 = bf16[2,128,512]{2,1,0:T(8,128)(2,1)S(1)} collective-permute-done((bf16[2,128,512]{2,1,0:T(8,128)(2,1)S(1)}, bf16[2,128,512]{2,1,0:T(8,128)(2,1)S(1)}, u32[]{:S(2)}, u32[]{:S(2)}) %collective-permute-start.12) | collective-permute-done | bytes 262176 | tf_op jit(solution)/shard_map/ppermute | solution.py:388
  91.3 0.8 collective-permute-done.14.g3
  92.1 1.0 %assemble.1 = (bf16[128,2048]{1,0:T(8,128)(2,1)}, bf16[128,2048]{1,0:T(8,128)(2,1)}) custom-call(bf16[2,128,512]{2,1,0:T(8,128)(2,1)S(1)} %collective-permute-done.11.g0, bf16[2,128,512]{2,1,0:T(8,128)(2,1)S(1)} %collective-permute-done.12.g1, bf16[2,128,512]{2,1,0:T(8,128)(2,1)S(1)} %collective-permute-done.13.g2, ...), custom_call_target="tpu_custom_call" | custom-call | tf_op jit(solution)/shard_map/assemble/pallas_call | solution.py:360
  93.1 0.7 total.1
  (39 shorter events, 1.9 us)
Async XLA Ops:
  2.4 12.0 %copy-start = (bf16[1,128,2048]{2,1,0:T(8,128)(2,1)S(1)}, bf16[1,128,2048]{2,1,0:T(8,128)(2,1)}, u32[]{:S(2)}) copy-start(bf16[1,128,2048]{2,1,0:T(8,128)(2,1)} %param.6) | copy-start | bytes 1572868
  2.4 12.0 %copy-start.1 = (bf16[1,128,2048]{2,1,0:T(8,128)(2,1)S(1)}, bf16[1,128,2048]{2,1,0:T(8,128)(2,1)}, u32[]{:S(2)}) copy-start(bf16[1,128,2048]{2,1,0:T(8,128)(2,1)} %param.11) | copy-start | bytes 1572868
  2.4 28.3 %all-to-all-start = ((bf16[32,64,128]{2,1,0:T(8,128)(2,1)}), bf16[32,64,128]{2,1,0:T(8,128)(2,1)S(1)}, u32[]{:S(2)}, u32[]{:S(2)}) async-start(bf16[32,64,128]{2,1,0:T(8,128)(2,1)} %bitcast.1), calls=%async_computation | async-start | bytes 1048576 | tf_op jit(solution)/shard_map/all_to_all | solution.py:407
  14.7 19.9 %collective-permute-start.7 = (bf16[2,128,512]{2,1,0:T(8,128)(2,1)S(1)}, bf16[2,128,512]{2,1,0:T(8,128)(2,1)S(1)}, u32[]{:S(2)}, u32[]{:S(2)}) collective-permute-start(bf16[2,128,512]{2,1,0:T(8,128)(2,1)S(1)} %get-tuple-element.18), channel_id=1, source_target_pairs={{0,64},{2,66},{4,68},{6,70},{1,129},{3,131},{5,133},{7,135},{64,0}... | collective-permute-start | bytes 786440 | tf_op jit(solution)/shard_map/ppermute | solution.py:388
  17.7 17.7 %collective-permute-start.8 = (bf16[2,128,512]{2,1,0:T(8,128)(2,1)S(1)}, bf16[2,128,512]{2,1,0:T(8,128)(2,1)S(1)}, u32[]{:S(2)}, u32[]{:S(2)}) collective-permute-start(bf16[2,128,512]{2,1,0:T(8,128)(2,1)S(1)} %get-tuple-element.19), channel_id=1, source_target_pairs={{0,1},{2,3},{4,5},{6,7},{1,193},{3,195},{5,197},{7,199},{64,64},{6... | collective-permute-start | bytes 786440 | tf_op jit(solution)/shard_map/ppermute | solution.py:388
  20.7 21.7 %collective-permute-start.9 = (bf16[2,128,512]{2,1,0:T(8,128)(2,1)S(1)}, bf16[2,128,512]{2,1,0:T(8,128)(2,1)S(1)}, u32[]{:S(2)}, u32[]{:S(2)}) collective-permute-start(bf16[2,128,512]{2,1,0:T(8,128)(2,1)S(1)} %get-tuple-element.20), channel_id=1, source_target_pairs={{0,65},{2,67},{4,69},{6,71},{1,128},{3,130},{5,132},{7,134},{64,1}... | collective-permute-start | bytes 786440 | tf_op jit(solution)/shard_map/ppermute | solution.py:388
  22.2 0.7 copy-start.2
  30.9 11.7 %collective-permute-start.1 = (bf16[20,2,16,128]{3,2,1,0:T(8,128)(2,1)S(1)}, bf16[20,2,16,128]{3,2,1,0:T(8,128)(2,1)S(1)}, u32[]{:S(2)}, u32[]{:S(2)}) collective-permute-start(bf16[20,2,16,128]{3,2,1,0:T(8,128)(2,1)S(1)} %bitcast.80), channel_id=1, source_target_pairs={{0,128},{64,192},{128,0},{192,64},{1,129},{65,193},{129,1},{193,65... | collective-permute-start | bytes 491528 | tf_op jit(solution)/shard_map/ppermute | solution.py:373
  33.9 1.5 %copy-start.3 = (s32[1024]{0:T(1024)S(1)}, s32[1024]{0:T(1024)}, u32[]{:S(2)}) copy-start(s32[1024]{0:T(1024)} %param.9) | copy-start | bytes 12292
  33.9 9.2 %collective-permute-start.2 = (bf16[20,2,16,128]{3,2,1,0:T(8,128)(2,1)S(1)}, bf16[20,2,16,128]{3,2,1,0:T(8,128)(2,1)S(1)}, u32[]{:S(2)}, u32[]{:S(2)}) collective-permute-start(bf16[20,2,16,128]{3,2,1,0:T(8,128)(2,1)S(1)} %bitcast.79), channel_id=1, source_target_pairs={{0,192},{64,0},{128,64},{192,128},{1,193},{65,1},{129,65},{193,129... | collective-permute-start | bytes 491528 | tf_op jit(solution)/shard_map/ppermute | solution.py:373
  34.7 8.5 %collective-permute-start = (bf16[20,2,16,128]{3,2,1,0:T(8,128)(2,1)S(1)}, bf16[20,2,16,128]{3,2,1,0:T(8,128)(2,1)S(1)}, u32[]{:S(2)}, u32[]{:S(2)}) collective-permute-start(bf16[20,2,16,128]{3,2,1,0:T(8,128)(2,1)S(1)} %bitcast.81), channel_id=1, source_target_pairs={{0,64},{64,128},{128,192},{192,0},{1,65},{65,129},{129,193},{193,1... | collective-permute-start | bytes 491528 | tf_op jit(solution)/shard_map/ppermute | solution.py:373
  35.4 11.0 %collective-permute-start.10 = (bf16[2,128,512]{2,1,0:T(8,128)(2,1)S(1)}, bf16[2,128,512]{2,1,0:T(8,128)(2,1)S(1)}, u32[]{:S(2)}, u32[]{:S(2)}) collective-permute-start(bf16[2,128,512]{2,1,0:T(8,128)(2,1)S(1)} %get-tuple-element.21), channel_id=1, source_target_pairs={{0,0},{2,2},{4,4},{6,6},{1,192},{3,194},{5,196},{7,198},{64,65},{6... | collective-permute-start | bytes 786440 | tf_op jit(solution)/shard_map/ppermute | solution.py:388
  42.5 4.0 %collective-permute-start.3 = (bf16[20,2,16,128]{3,2,1,0:T(8,128)(2,1)S(1)}, bf16[20,2,16,128]{3,2,1,0:T(8,128)(2,1)S(1)}, u32[]{:S(2)}, u32[]{:S(2)}) collective-permute-start(bf16[20,2,16,128]{3,2,1,0:T(8,128)(2,1)S(1)} %bitcast.72), channel_id=1, source_target_pairs={{0,1},{1,0},{2,3},{3,2},{4,5},{5,4},{6,7},{7,6},{8,9},{9,8},{10,11... | collective-permute-start | bytes 491528 | tf_op jit(solution)/shard_map/ppermute | solution.py:378
  42.6 3.9 %collective-permute-start.5 = (bf16[20,2,16,128]{3,2,1,0:T(8,128)(2,1)S(1)}, bf16[20,2,16,128]{3,2,1,0:T(8,128)(2,1)S(1)}, u32[]{:S(2)}, u32[]{:S(2)}) collective-permute-start(bf16[20,2,16,128]{3,2,1,0:T(8,128)(2,1)S(1)} %collective-permute-done.1.a2), channel_id=1, source_target_pairs={{0,1},{1,0},{2,3},{3,2},{4,5},{5,4},{6,7},{7,6},{8,9},{9,8},{10,11... | collective-permute-start | bytes 491528 | tf_op jit(solution)/shard_map/ppermute | solution.py:378
  43.1 3.4 %collective-permute-start.6 = (bf16[20,2,16,128]{3,2,1,0:T(8,128)(2,1)S(1)}, bf16[20,2,16,128]{3,2,1,0:T(8,128)(2,1)S(1)}, u32[]{:S(2)}, u32[]{:S(2)}) collective-permute-start(bf16[20,2,16,128]{3,2,1,0:T(8,128)(2,1)S(1)} %collective-permute-done.2.a3), channel_id=1, source_target_pairs={{0,1},{1,0},{2,3},{3,2},{4,5},{5,4},{6,7},{7,6},{8,9},{9,8},{10,11... | collective-permute-start | bytes 491528 | tf_op jit(solution)/shard_map/ppermute | solution.py:378
  43.2 3.3 %collective-permute-start.4 = (bf16[20,2,16,128]{3,2,1,0:T(8,128)(2,1)S(1)}, bf16[20,2,16,128]{3,2,1,0:T(8,128)(2,1)S(1)}, u32[]{:S(2)}, u32[]{:S(2)}) collective-permute-start(bf16[20,2,16,128]{3,2,1,0:T(8,128)(2,1)S(1)} %collective-permute-done.a1), channel_id=1, source_target_pairs={{0,1},{1,0},{2,3},{3,2},{4,5},{5,4},{6,7},{7,6},{8,9},{9,8},{10,11... | collective-permute-start | bytes 491528 | tf_op jit(solution)/shard_map/ppermute | solution.py:378
  53.0 2.2 %collective-permute-start.15 = (bf16[4,2,20,16,128]{4,3,2,1,0:T(8,128)(2,1)S(1)}, bf16[4,2,20,16,128]{4,3,2,1,0:T(8,128)(2,1)S(1)}, u32[]{:S(2)}, u32[]{:S(2)}) collective-permute-start(bf16[4,2,20,16,128]{4,3,2,1,0:T(8,128)(2,1)S(1)} %get-tuple-element.29), channel_id=1, source_target_pairs={{0,1},{1,0},{2,3},{3,2},{4,5},{5,4},{6,7},{7,6},{8,9},{9,8},{10,11... | collective-permute-start | bytes 1966088 | tf_op jit(solution)/shard_map/ppermute | solution.py:378
  55.4 9.3 %collective-permute-start.18 = (bf16[2,20,16,128]{3,2,1,0:T(8,128)(2,1)S(1)}, bf16[2,20,16,128]{3,2,1,0:T(8,128)(2,1)S(1)}, u32[]{:S(2)}, u32[]{:S(2)}) collective-permute-start(bf16[2,20,16,128]{3,2,1,0:T(8,128)(2,1)S(1)} %get-tuple-element.32), channel_id=1, source_target_pairs={{0,192},{64,0},{128,64},{192,128},{1,193},{65,1},{129,65},{193,129... | collective-permute-start | bytes 491528 | tf_op jit(solution)/shard_map/ppermute | solution.py:373
  58.2 6.7 %collective-permute-start.17 = (bf16[2,20,16,128]{3,2,1,0:T(8,128)(2,1)S(1)}, bf16[2,20,16,128]{3,2,1,0:T(8,128)(2,1)S(1)}, u32[]{:S(2)}, u32[]{:S(2)}) collective-permute-start(bf16[2,20,16,128]{3,2,1,0:T(8,128)(2,1)S(1)} %get-tuple-element.33), channel_id=1, source_target_pairs={{0,128},{64,192},{128,0},{192,64},{1,129},{65,193},{129,1},{193,65... | collective-permute-start | bytes 491528 | tf_op jit(solution)/shard_map/ppermute | solution.py:373
  58.2 10.5 %collective-permute-start.16 = (bf16[2,20,16,128]{3,2,1,0:T(8,128)(2,1)S(1)}, bf16[2,20,16,128]{3,2,1,0:T(8,128)(2,1)S(1)}, u32[]{:S(2)}, u32[]{:S(2)}) collective-permute-start(bf16[2,20,16,128]{3,2,1,0:T(8,128)(2,1)S(1)} %get-tuple-element.34), channel_id=1, source_target_pairs={{0,64},{64,128},{128,192},{192,0},{1,65},{65,129},{129,193},{193,1... | collective-permute-start | bytes 491528 | tf_op jit(solution)/shard_map/ppermute | solution.py:373
  70.5 22.6 %all-to-all-start.1 = ((bf16[32,64,128]{2,1,0:T(8,128)(2,1)}), bf16[32,64,128]{2,1,0:T(8,128)(2,1)S(1)}, u32[]{:S(2)}, u32[]{:S(2)}) async-start(bf16[32,64,128]{2,1,0:T(8,128)(2,1)} %bitcast.21), calls=%async_computation.1 | async-start | bytes 1048576 | tf_op jit(solution)/shard_map/all_to_all | solution.py:420
  75.3 8.7 %collective-permute-start.11 = (bf16[2,128,512]{2,1,0:T(8,128)(2,1)S(1)}, bf16[2,128,512]{2,1,0:T(8,128)(2,1)S(1)}, u32[]{:S(2)}, u32[]{:S(2)}) collective-permute-start(bf16[2,128,512]{2,1,0:T(8,128)(2,1)S(1)} %get-tuple-element.22), channel_id=1, source_target_pairs={{64,0},{66,2},{68,4},{70,6},{129,1},{131,3},{133,5},{135,7},{0,64}... | collective-permute-start | bytes 786440 | tf_op jit(solution)/shard_map/ppermute | solution.py:388
  76.5 14.8 %collective-permute-start.12 = (bf16[2,128,512]{2,1,0:T(8,128)(2,1)S(1)}, bf16[2,128,512]{2,1,0:T(8,128)(2,1)S(1)}, u32[]{:S(2)}, u32[]{:S(2)}) collective-permute-start(bf16[2,128,512]{2,1,0:T(8,128)(2,1)S(1)} %get-tuple-element.23), channel_id=1, source_target_pairs={{1,0},{3,2},{5,4},{7,6},{193,1},{195,3},{197,5},{199,7},{64,64},{6... | collective-permute-start | bytes 786440 | tf_op jit(solution)/shard_map/ppermute | solution.py:388
  78.4 12.9 %collective-permute-start.13 = (bf16[2,128,512]{2,1,0:T(8,128)(2,1)S(1)}, bf16[2,128,512]{2,1,0:T(8,128)(2,1)S(1)}, u32[]{:S(2)}, u32[]{:S(2)}) collective-permute-start(bf16[2,128,512]{2,1,0:T(8,128)(2,1)S(1)} %get-tuple-element.24), channel_id=1, source_target_pairs={{65,0},{67,2},{69,4},{71,6},{128,1},{130,3},{132,5},{134,7},{1,64}... | collective-permute-start | bytes 786440 | tf_op jit(solution)/shard_map/ppermute | solution.py:388
  78.7 13.4 %collective-permute-start.14 = (bf16[2,128,512]{2,1,0:T(8,128)(2,1)S(1)}, bf16[2,128,512]{2,1,0:T(8,128)(2,1)S(1)}, u32[]{:S(2)}, u32[]{:S(2)}) collective-permute-start(bf16[2,128,512]{2,1,0:T(8,128)(2,1)S(1)} %get-tuple-element.25), channel_id=1, source_target_pairs={{0,0},{2,2},{4,4},{6,6},{192,1},{194,3},{196,5},{198,7},{65,64},{6... | collective-permute-start | bytes 786440 | tf_op jit(solution)/shard_map/ppermute | solution.py:388

commit v8 on v7

--- a/solution.py
+++ b/solution.py
@@ -318,11 +318,14 @@
     )(order, *parts)
 
 
-def total_kernel(got_in, grad_key, grad_value, got, sem):
-    copy = pltpu.make_async_copy(got_in, got, sem)
-    copy.start()
-    copy.wait()
+def total_kernel(got_in, grad_key, grad_value, got, sems):
+    copies = [
+        pltpu.make_async_copy(got_in.at[x], got.at[x], sems.at[x]) for x in range(TILES)
+    ]
+    for copy in copies:
+        copy.start()
     for x in range(TILES):
+        copies[x].wait()
         total = got[x, 0].astype(f32)
         for c in range(1, got.shape[1]):
             total = total + got[x, c].astype(f32)
@@ -339,7 +342,7 @@
         out_shape=(shape(TILE, TILES * 2 * HEAD_DIM),) * 2,
         in_specs=[ANY],
         out_specs=(VMEM, VMEM),
-        scratch_shapes=[pltpu.VMEM(got.shape, bf16), pltpu.SemaphoreType.DMA],
+        scratch_shapes=[pltpu.VMEM(got.shape, bf16), pltpu.SemaphoreType.DMA((TILES,))],
         compiler_params=PARAMS,
         name="total",
     )(got)

time: 94.5 us -> 95.2 us (level)
  no operation moved by 1% of the time
where the time goes in v8:
time: 95.2 us; the launch traced here: 94.7 us
  starting transfers between devices  49.3 us (52%)
  waiting for transfers between devices  24.5 us (26%)
  Pallas kernels  12 us (13%)
  between operations  5.49 us (6%)
  local copies, waits for them, and re-layouts  2.15 us (2%)
  other arithmetic  1.27 us (1%)
    ppermute x8, starting transfers between devices, sent_over(): return lax.ppermute(block, ('pipe', 'tp'), route)  22.9 us
    all_to_all x1, starting transfers between devices, exchanged(): lax.all_to_all(flat, ('ctx', 'tp'), split_axis=0, concat_axis=0, axis_ind...  12 us
    ppermute x8, waiting for transfers between devices, sent_over(): return lax.ppermute(block, ('pipe', 'tp'), route)  10.5 us
    ppermute x6, waiting for transfers between devices, moved(): lax.ppermute(block, 'pipe', [(i, (i + distance) % size) for i in range(si...  9.87 us
    ppermute x6, starting transfers between devices, moved(): lax.ppermute(block, 'pipe', [(i, (i + distance) % size) for i in range(si...  7.9 us
    pallas_call x1, Pallas kernels, run_layers(): pl.pallas_call(layers_kernel, out_shape=(kv_shape, kv_shape) + (shape(2,...  6.53 us
    all_to_all x1, starting transfers between devices, exchanged_by_x(): lax.all_to_all(flat, ('ctx', 'tp'), split_axis=0, concat_axis=0, axis_ind...  4.74 us
    ppermute x5, waiting for transfers between devices, swapped(): return lax.ppermute(block, 'tp', [(i, i ^ 1) for i in range(size)])  2.09 us
  transfers between devices with their start and end apart: 21, of which 9 were waited for; matrix products, arithmetic and copies ran while one was open for 2% of the time, Pallas kernels for 1%

profile of v8, /device:TPU:1, one launch (start us, length us, event | category | flops | bytes accessed | tf_op | source)
XLA Modules:
  0.0 94.7 jit_solution(14171167892892705782)
XLA Ops:
  0.6 0.8 pad_maximum_fusion.kv_in
  1.4 0.9 %spread.1 = bf16[32,2,2,16,128]{4,3,2,1,0:T(8,128)(2,1)} custom-call(bf16[2,16,1024]{2,1,0:T(8,128)(2,1)S(1)} %pad_maximum_fusion.kv_in), custom_call_target="tpu_custom_call" | custom-call | tf_op jit(solution)/shard_map/spread/pallas_call | solution.py:74
  2.4 12.0 %all-to-all-start = ((bf16[32,64,128]{2,1,0:T(8,128)(2,1)}), bf16[32,64,128]{2,1,0:T(8,128)(2,1)S(1)}, u32[]{:S(2)}, u32[]{:S(2)}) async-start(bf16[32,64,128]{2,1,0:T(8,128)(2,1)} %bitcast.1), calls=%async_computation | async-start | bytes 1048576 | tf_op jit(solution)/shard_map/all_to_all | solution.py:410
  14.7 3.0 %collective-permute-start.7 = (bf16[2,128,512]{2,1,0:T(8,128)(2,1)S(1)}, bf16[2,128,512]{2,1,0:T(8,128)(2,1)S(1)}, u32[]{:S(2)}, u32[]{:S(2)}) collective-permute-start(bf16[2,128,512]{2,1,0:T(8,128)(2,1)S(1)} %get-tuple-element.18), channel_id=1, source_target_pairs={{0,64},{2,66},{4,68},{6,70},{1,129},{3,131},{5,133},{7,135},{64,0}... | collective-permute-start | bytes 786440 | tf_op jit(solution)/shard_map/ppermute | solution.py:391
  17.7 3.0 %collective-permute-start.8 = (bf16[2,128,512]{2,1,0:T(8,128)(2,1)S(1)}, bf16[2,128,512]{2,1,0:T(8,128)(2,1)S(1)}, u32[]{:S(2)}, u32[]{:S(2)}) collective-permute-start(bf16[2,128,512]{2,1,0:T(8,128)(2,1)S(1)} %get-tuple-element.19), channel_id=1, source_target_pairs={{0,1},{2,3},{4,5},{6,7},{1,193},{3,195},{5,197},{7,199},{64,64},{6... | collective-permute-start | bytes 786440 | tf_op jit(solution)/shard_map/ppermute | solution.py:391
  20.7 1.4 %collective-permute-start.9 = (bf16[2,128,512]{2,1,0:T(8,128)(2,1)S(1)}, bf16[2,128,512]{2,1,0:T(8,128)(2,1)S(1)}, u32[]{:S(2)}, u32[]{:S(2)}) collective-permute-start(bf16[2,128,512]{2,1,0:T(8,128)(2,1)S(1)} %get-tuple-element.20), channel_id=1, source_target_pairs={{0,65},{2,67},{4,69},{6,71},{1,128},{3,130},{5,132},{7,134},{64,1}... | collective-permute-start | bytes 786440 | tf_op jit(solution)/shard_map/ppermute | solution.py:391
  22.2 0.7 copy-done.2
  22.8 0.6 dynamic_slice.66
  24.9 0.7 fusion.6
  28.7 2.0 %all-to-all-done = bf16[32,64,128]{2,1,0:T(8,128)(2,1)S(1)} async-done(((bf16[32,64,128]{2,1,0:T(8,128)(2,1)}), bf16[32,64,128]{2,1,0:T(8,128)(2,1)S(1)}, u32[]{:S(2)}, u32[]{:S(2)}) %all-to-all-start) | async-done | bytes 524320 | tf_op jit(solution)/shard_map/all_to_all | solution.py:410
  30.9 3.0 %collective-permute-start.1 = (bf16[20,2,16,128]{3,2,1,0:T(8,128)(2,1)S(1)}, bf16[20,2,16,128]{3,2,1,0:T(8,128)(2,1)S(1)}, u32[]{:S(2)}, u32[]{:S(2)}) collective-permute-start(bf16[20,2,16,128]{3,2,1,0:T(8,128)(2,1)S(1)} %bitcast.80), channel_id=1, source_target_pairs={{0,128},{64,192},{128,0},{192,64},{1,129},{65,193},{129,1},{193,65... | collective-permute-start | bytes 491528 | tf_op jit(solution)/shard_map/ppermute | solution.py:376
  33.9 0.8 collective-permute-start.2
  34.7 0.7 collective-permute-start
  35.4 7.0 %collective-permute-start.10 = (bf16[2,128,512]{2,1,0:T(8,128)(2,1)S(1)}, bf16[2,128,512]{2,1,0:T(8,128)(2,1)S(1)}, u32[]{:S(2)}, u32[]{:S(2)}) collective-permute-start(bf16[2,128,512]{2,1,0:T(8,128)(2,1)S(1)} %get-tuple-element.21), channel_id=1, source_target_pairs={{0,0},{2,2},{4,4},{6,6},{1,192},{3,194},{5,196},{7,198},{64,65},{6... | collective-permute-start | bytes 786440 | tf_op jit(solution)/shard_map/ppermute | solution.py:391
  42.6 0.5 collective-permute-start.5
  43.2 1.0 %collective-permute-start.4 = (bf16[20,2,16,128]{3,2,1,0:T(8,128)(2,1)S(1)}, bf16[20,2,16,128]{3,2,1,0:T(8,128)(2,1)S(1)}, u32[]{:S(2)}, u32[]{:S(2)}) collective-permute-start(bf16[20,2,16,128]{3,2,1,0:T(8,128)(2,1)S(1)} %collective-permute-done.a1), channel_id=1, source_target_pairs={{0,1},{1,0},{2,3},{3,2},{4,5},{5,4},{6,7},{7,6},{8,9},{9,8},{10,11... | collective-permute-start | bytes 491528 | tf_op jit(solution)/shard_map/ppermute | solution.py:381
  44.3 2.2 %collective-permute-done.10.q3 = bf16[2,128,512]{2,1,0:T(8,128)(2,1)S(1)} collective-permute-done((bf16[2,128,512]{2,1,0:T(8,128)(2,1)S(1)}, bf16[2,128,512]{2,1,0:T(8,128)(2,1)S(1)}, u32[]{:S(2)}, u32[]{:S(2)}) %collective-permute-start.10) | collective-permute-done | bytes 262176 | tf_op jit(solution)/shard_map/ppermute | solution.py:391
  46.5 6.5 %layers.1 = (bf16[4,2,20,16,128]{4,3,2,1,0:T(8,128)(2,1)S(1)}, bf16[4,2,20,16,128]{4,3,2,1,0:T(8,128)(2,1)S(1)}, bf16[2,128,512]{2,1,0:T(8,128)(2,1)S(1)}, bf16[...) custom-call(f32[128,640]{1,0:T(8,128)S(1)} %fusion.1.bias_in, ...), custom_call_target="tpu_custom_call" | custom-call | tf_op jit(solution)/shard_map/layers/pallas_call | solution.py:231
  53.1 2.1 %collective-permute-done.15 = bf16[4,2,20,16,128]{4,3,2,1,0:T(8,128)(2,1)S(1)} collective-permute-done((bf16[4,2,20,16,128]{4,3,2,1,0:T(8,128)(2,1)S(1)}, bf16[4,2,20,16,128]{4,3,2,1,0:T(8,128)(2,1)S(1)}, u32[]{:S(2)}, u32[]{:S(2)}) %collective-permute-start.15) | collective-permute-done | bytes 655392 | tf_op jit(solution)/shard_map/ppermute | solution.py:381
  55.4 2.8 %collective-permute-start.18 = (bf16[2,20,16,128]{3,2,1,0:T(8,128)(2,1)S(1)}, bf16[2,20,16,128]{3,2,1,0:T(8,128)(2,1)S(1)}, u32[]{:S(2)}, u32[]{:S(2)}) collective-permute-start(bf16[2,20,16,128]{3,2,1,0:T(8,128)(2,1)S(1)} %get-tuple-element.32), channel_id=1, source_target_pairs={{0,192},{64,0},{128,64},{192,128},{1,193},{65,1},{129,65},{193,129... | collective-permute-start | bytes 491528 | tf_op jit(solution)/shard_map/ppermute | solution.py:376
  58.2 0.7 collective-permute-start.16
  58.8 5.9 %collective-permute-done.18.p3 = bf16[2,20,16,128]{3,2,1,0:T(8,128)(2,1)S(1)} collective-permute-done((bf16[2,20,16,128]{3,2,1,0:T(8,128)(2,1)S(1)}, bf16[2,20,16,128]{3,2,1,0:T(8,128)(2,1)S(1)}, u32[]{:S(2)}, u32[]{:S(2)}) %collective-permute-start.18) | collective-permute-done | bytes 163872 | tf_op jit(solution)/shard_map/ppermute | solution.py:376
  64.9 3.9 %collective-permute-done.16.p1 = bf16[2,20,16,128]{3,2,1,0:T(8,128)(2,1)S(1)} collective-permute-done((bf16[2,20,16,128]{3,2,1,0:T(8,128)(2,1)S(1)}, bf16[2,20,16,128]{3,2,1,0:T(8,128)(2,1)S(1)}, u32[]{:S(2)}, u32[]{:S(2)}) %collective-permute-start.16) | collective-permute-done | bytes 163872 | tf_op jit(solution)/shard_map/ppermute | solution.py:376
  68.7 1.8 %place.1 = bf16[4,8,2,2,16,128]{5,4,3,2,1,0:T(8,128)(2,1)} custom-call(s32[8]{0:T(128)S(1)} %copy-done.2, bf16[2,20,16,128]{3,2,1,0:T(8,128)(2,1)S(1)} %get-tuple-element.35.p0, bf16[2,20,16,128]{3,2,1,0:T(8,128)(2,1)S(1)} %collective-permute-done.16.p1, bf16[2,20,16,128]{3,2,1,0:T(8,128)(2,1)S(1)} %collective-permute-done.17.p2, ...), custom_call_target="tpu_custom_call" | custom-call | tf_op jit(solution)/shard_map/place/pallas_call | solution.py:303
  70.5 4.7 %all-to-all-start.1 = ((bf16[32,64,128]{2,1,0:T(8,128)(2,1)}), bf16[32,64,128]{2,1,0:T(8,128)(2,1)S(1)}, u32[]{:S(2)}, u32[]{:S(2)}) async-start(bf16[32,64,128]{2,1,0:T(8,128)(2,1)} %bitcast.21), calls=%async_computation.1 | async-start | bytes 1048576 | tf_op jit(solution)/shard_map/all_to_all | solution.py:423
  75.3 1.2 %collective-permute-start.11 = (bf16[2,128,512]{2,1,0:T(8,128)(2,1)S(1)}, bf16[2,128,512]{2,1,0:T(8,128)(2,1)S(1)}, u32[]{:S(2)}, u32[]{:S(2)}) collective-permute-start(bf16[2,128,512]{2,1,0:T(8,128)(2,1)S(1)} %get-tuple-element.22), channel_id=1, source_target_pairs={{64,0},{66,2},{68,4},{70,6},{129,1},{131,3},{133,5},{135,7},{0,64}... | collective-permute-start | bytes 786440 | tf_op jit(solution)/shard_map/ppermute | solution.py:391
  76.5 1.9 %collective-permute-start.12 = (bf16[2,128,512]{2,1,0:T(8,128)(2,1)S(1)}, bf16[2,128,512]{2,1,0:T(8,128)(2,1)S(1)}, u32[]{:S(2)}, u32[]{:S(2)}) collective-permute-start(bf16[2,128,512]{2,1,0:T(8,128)(2,1)S(1)} %get-tuple-element.23), channel_id=1, source_target_pairs={{1,0},{3,2},{5,4},{7,6},{193,1},{195,3},{197,5},{199,7},{64,64},{6... | collective-permute-start | bytes 786440 | tf_op jit(solution)/shard_map/ppermute | solution.py:391
  78.7 5.1 %collective-permute-start.14 = (bf16[2,128,512]{2,1,0:T(8,128)(2,1)S(1)}, bf16[2,128,512]{2,1,0:T(8,128)(2,1)S(1)}, u32[]{:S(2)}, u32[]{:S(2)}) collective-permute-start(bf16[2,128,512]{2,1,0:T(8,128)(2,1)S(1)} %get-tuple-element.25), channel_id=1, source_target_pairs={{0,0},{2,2},{4,4},{6,6},{192,1},{194,3},{196,5},{198,7},{65,64},{6... | collective-permute-start | bytes 786440 | tf_op jit(solution)/shard_map/ppermute | solution.py:391
  84.0 7.3 %collective-permute-done.12.g1 = bf16[2,128,512]{2,1,0:T(8,128)(2,1)S(1)} collective-permute-done((bf16[2,128,512]{2,1,0:T(8,128)(2,1)S(1)}, bf16[2,128,512]{2,1,0:T(8,128)(2,1)S(1)}, u32[]{:S(2)}, u32[]{:S(2)}) %collective-permute-start.12) | collective-permute-done | bytes 262176 | tf_op jit(solution)/shard_map/ppermute | solution.py:391
  91.3 0.8 collective-permute-done.14.g3
  92.1 1.0 %assemble.1 = (bf16[128,2048]{1,0:T(8,128)(2,1)}, bf16[128,2048]{1,0:T(8,128)(2,1)}) custom-call(bf16[2,128,512]{2,1,0:T(8,128)(2,1)S(1)} %collective-permute-done.11.g0, bf16[2,128,512]{2,1,0:T(8,128)(2,1)S(1)} %collective-permute-done.12.g1, bf16[2,128,512]{2,1,0:T(8,128)(2,1)S(1)} %collective-permute-done.13.g2, ...), custom_call_target="tpu_custom_call" | custom-call | tf_op jit(solution)/shard_map/assemble/pallas_call | solution.py:363
  93.1 1.4 %total.1 = (bf16[16,1024]{1,0:T(8,128)(2,1)}, bf16[16,1024]{1,0:T(8,128)(2,1)}) custom-call(bf16[4,8,2,2,16,128]{5,4,3,2,1,0:T(8,128)(2,1)S(1)} %bitcast.69), custom_call_target="tpu_custom_call" | custom-call | tf_op jit(solution)/shard_map/total/pallas_call | solution.py:340
  (39 shorter events, 1.9 us)
Async XLA Ops:
  2.4 12.0 %copy-start = (bf16[1,128,2048]{2,1,0:T(8,128)(2,1)S(1)}, bf16[1,128,2048]{2,1,0:T(8,128)(2,1)}, u32[]{:S(2)}) copy-start(bf16[1,128,2048]{2,1,0:T(8,128)(2,1)} %param.6) | copy-start | bytes 1572868
  2.4 12.0 %copy-start.1 = (bf16[1,128,2048]{2,1,0:T(8,128)(2,1)S(1)}, bf16[1,128,2048]{2,1,0:T(8,128)(2,1)}, u32[]{:S(2)}) copy-start(bf16[1,128,2048]{2,1,0:T(8,128)(2,1)} %param.11) | copy-start | bytes 1572868
  2.4 28.3 %all-to-all-start = ((bf16[32,64,128]{2,1,0:T(8,128)(2,1)}), bf16[32,64,128]{2,1,0:T(8,128)(2,1)S(1)}, u32[]{:S(2)}, u32[]{:S(2)}) async-start(bf16[32,64,128]{2,1,0:T(8,128)(2,1)} %bitcast.1), calls=%async_computation | async-start | bytes 1048576 | tf_op jit(solution)/shard_map/all_to_all | solution.py:410
  14.7 19.9 %collective-permute-start.7 = (bf16[2,128,512]{2,1,0:T(8,128)(2,1)S(1)}, bf16[2,128,512]{2,1,0:T(8,128)(2,1)S(1)}, u32[]{:S(2)}, u32[]{:S(2)}) collective-permute-start(bf16[2,128,512]{2,1,0:T(8,128)(2,1)S(1)} %get-tuple-element.18), channel_id=1, source_target_pairs={{0,64},{2,66},{4,68},{6,70},{1,129},{3,131},{5,133},{7,135},{64,0}... | collective-permute-start | bytes 786440 | tf_op jit(solution)/shard_map/ppermute | solution.py:391
  17.7 17.7 %collective-permute-start.8 = (bf16[2,128,512]{2,1,0:T(8,128)(2,1)S(1)}, bf16[2,128,512]{2,1,0:T(8,128)(2,1)S(1)}, u32[]{:S(2)}, u32[]{:S(2)}) collective-permute-start(bf16[2,128,512]{2,1,0:T(8,128)(2,1)S(1)} %get-tuple-element.19), channel_id=1, source_target_pairs={{0,1},{2,3},{4,5},{6,7},{1,193},{3,195},{5,197},{7,199},{64,64},{6... | collective-permute-start | bytes 786440 | tf_op jit(solution)/shard_map/ppermute | solution.py:391
  20.7 21.7 %collective-permute-start.9 = (bf16[2,128,512]{2,1,0:T(8,128)(2,1)S(1)}, bf16[2,128,512]{2,1,0:T(8,128)(2,1)S(1)}, u32[]{:S(2)}, u32[]{:S(2)}) collective-permute-start(bf16[2,128,512]{2,1,0:T(8,128)(2,1)S(1)} %get-tuple-element.20), channel_id=1, source_target_pairs={{0,65},{2,67},{4,69},{6,71},{1,128},{3,130},{5,132},{7,134},{64,1}... | collective-permute-start | bytes 786440 | tf_op jit(solution)/shard_map/ppermute | solution.py:391
  22.2 0.7 copy-start.2
  30.9 11.7 %collective-permute-start.1 = (bf16[20,2,16,128]{3,2,1,0:T(8,128)(2,1)S(1)}, bf16[20,2,16,128]{3,2,1,0:T(8,128)(2,1)S(1)}, u32[]{:S(2)}, u32[]{:S(2)}) collective-permute-start(bf16[20,2,16,128]{3,2,1,0:T(8,128)(2,1)S(1)} %bitcast.80), channel_id=1, source_target_pairs={{0,128},{64,192},{128,0},{192,64},{1,129},{65,193},{129,1},{193,65... | collective-permute-start | bytes 491528 | tf_op jit(solution)/shard_map/ppermute | solution.py:376
  33.9 1.5 %copy-start.3 = (s32[1024]{0:T(1024)S(1)}, s32[1024]{0:T(1024)}, u32[]{:S(2)}) copy-start(s32[1024]{0:T(1024)} %param.9) | copy-start | bytes 12292
  33.9 9.2 %collective-permute-start.2 = (bf16[20,2,16,128]{3,2,1,0:T(8,128)(2,1)S(1)}, bf16[20,2,16,128]{3,2,1,0:T(8,128)(2,1)S(1)}, u32[]{:S(2)}, u32[]{:S(2)}) collective-permute-start(bf16[20,2,16,128]{3,2,1,0:T(8,128)(2,1)S(1)} %bitcast.79), channel_id=1, source_target_pairs={{0,192},{64,0},{128,64},{192,128},{1,193},{65,1},{129,65},{193,129... | collective-permute-start | bytes 491528 | tf_op jit(solution)/shard_map/ppermute | solution.py:376
  34.7 8.5 %collective-permute-start = (bf16[20,2,16,128]{3,2,1,0:T(8,128)(2,1)S(1)}, bf16[20,2,16,128]{3,2,1,0:T(8,128)(2,1)S(1)}, u32[]{:S(2)}, u32[]{:S(2)}) collective-permute-start(bf16[20,2,16,128]{3,2,1,0:T(8,128)(2,1)S(1)} %bitcast.81), channel_id=1, source_target_pairs={{0,64},{64,128},{128,192},{192,0},{1,65},{65,129},{129,193},{193,1... | collective-permute-start | bytes 491528 | tf_op jit(solution)/shard_map/ppermute | solution.py:376
  35.4 11.0 %collective-permute-start.10 = (bf16[2,128,512]{2,1,0:T(8,128)(2,1)S(1)}, bf16[2,128,512]{2,1,0:T(8,128)(2,1)S(1)}, u32[]{:S(2)}, u32[]{:S(2)}) collective-permute-start(bf16[2,128,512]{2,1,0:T(8,128)(2,1)S(1)} %get-tuple-element.21), channel_id=1, source_target_pairs={{0,0},{2,2},{4,4},{6,6},{1,192},{3,194},{5,196},{7,198},{64,65},{6... | collective-permute-start | bytes 786440 | tf_op jit(solution)/shard_map/ppermute | solution.py:391
  42.5 4.0 %collective-permute-start.3 = (bf16[20,2,16,128]{3,2,1,0:T(8,128)(2,1)S(1)}, bf16[20,2,16,128]{3,2,1,0:T(8,128)(2,1)S(1)}, u32[]{:S(2)}, u32[]{:S(2)}) collective-permute-start(bf16[20,2,16,128]{3,2,1,0:T(8,128)(2,1)S(1)} %bitcast.72), channel_id=1, source_target_pairs={{0,1},{1,0},{2,3},{3,2},{4,5},{5,4},{6,7},{7,6},{8,9},{9,8},{10,11... | collective-permute-start | bytes 491528 | tf_op jit(solution)/shard_map/ppermute | solution.py:381
  42.6 3.9 %collective-permute-start.5 = (bf16[20,2,16,128]{3,2,1,0:T(8,128)(2,1)S(1)}, bf16[20,2,16,128]{3,2,1,0:T(8,128)(2,1)S(1)}, u32[]{:S(2)}, u32[]{:S(2)}) collective-permute-start(bf16[20,2,16,128]{3,2,1,0:T(8,128)(2,1)S(1)} %collective-permute-done.1.a2), channel_id=1, source_target_pairs={{0,1},{1,0},{2,3},{3,2},{4,5},{5,4},{6,7},{7,6},{8,9},{9,8},{10,11... | collective-permute-start | bytes 491528 | tf_op jit(solution)/shard_map/ppermute | solution.py:381
  43.1 3.4 %collective-permute-start.6 = (bf16[20,2,16,128]{3,2,1,0:T(8,128)(2,1)S(1)}, bf16[20,2,16,128]{3,2,1,0:T(8,128)(2,1)S(1)}, u32[]{:S(2)}, u32[]{:S(2)}) collective-permute-start(bf16[20,2,16,128]{3,2,1,0:T(8,128)(2,1)S(1)} %collective-permute-done.2.a3), channel_id=1, source_target_pairs={{0,1},{1,0},{2,3},{3,2},{4,5},{5,4},{6,7},{7,6},{8,9},{9,8},{10,11... | collective-permute-start | bytes 491528 | tf_op jit(solution)/shard_map/ppermute | solution.py:381
  43.2 3.3 %collective-permute-start.4 = (bf16[20,2,16,128]{3,2,1,0:T(8,128)(2,1)S(1)}, bf16[20,2,16,128]{3,2,1,0:T(8,128)(2,1)S(1)}, u32[]{:S(2)}, u32[]{:S(2)}) collective-permute-start(bf16[20,2,16,128]{3,2,1,0:T(8,128)(2,1)S(1)} %collective-permute-done.a1), channel_id=1, source_target_pairs={{0,1},{1,0},{2,3},{3,2},{4,5},{5,4},{6,7},{7,6},{8,9},{9,8},{10,11... | collective-permute-start | bytes 491528 | tf_op jit(solution)/shard_map/ppermute | solution.py:381
  53.0 2.2 %collective-permute-start.15 = (bf16[4,2,20,16,128]{4,3,2,1,0:T(8,128)(2,1)S(1)}, bf16[4,2,20,16,128]{4,3,2,1,0:T(8,128)(2,1)S(1)}, u32[]{:S(2)}, u32[]{:S(2)}) collective-permute-start(bf16[4,2,20,16,128]{4,3,2,1,0:T(8,128)(2,1)S(1)} %get-tuple-element.29), channel_id=1, source_target_pairs={{0,1},{1,0},{2,3},{3,2},{4,5},{5,4},{6,7},{7,6},{8,9},{9,8},{10,11... | collective-permute-start | bytes 1966088 | tf_op jit(solution)/shard_map/ppermute | solution.py:381
  55.4 9.3 %collective-permute-start.18 = (bf16[2,20,16,128]{3,2,1,0:T(8,128)(2,1)S(1)}, bf16[2,20,16,128]{3,2,1,0:T(8,128)(2,1)S(1)}, u32[]{:S(2)}, u32[]{:S(2)}) collective-permute-start(bf16[2,20,16,128]{3,2,1,0:T(8,128)(2,1)S(1)} %get-tuple-element.32), channel_id=1, source_target_pairs={{0,192},{64,0},{128,64},{192,128},{1,193},{65,1},{129,65},{193,129... | collective-permute-start | bytes 491528 | tf_op jit(solution)/shard_map/ppermute | solution.py:376
  58.2 6.7 %collective-permute-start.17 = (bf16[2,20,16,128]{3,2,1,0:T(8,128)(2,1)S(1)}, bf16[2,20,16,128]{3,2,1,0:T(8,128)(2,1)S(1)}, u32[]{:S(2)}, u32[]{:S(2)}) collective-permute-start(bf16[2,20,16,128]{3,2,1,0:T(8,128)(2,1)S(1)} %get-tuple-element.33), channel_id=1, source_target_pairs={{0,128},{64,192},{128,0},{192,64},{1,129},{65,193},{129,1},{193,65... | collective-permute-start | bytes 491528 | tf_op jit(solution)/shard_map/ppermute | solution.py:376
  58.2 10.5 %collective-permute-start.16 = (bf16[2,20,16,128]{3,2,1,0:T(8,128)(2,1)S(1)}, bf16[2,20,16,128]{3,2,1,0:T(8,128)(2,1)S(1)}, u32[]{:S(2)}, u32[]{:S(2)}) collective-permute-start(bf16[2,20,16,128]{3,2,1,0:T(8,128)(2,1)S(1)} %get-tuple-element.34), channel_id=1, source_target_pairs={{0,64},{64,128},{128,192},{192,0},{1,65},{65,129},{129,193},{193,1... | collective-permute-start | bytes 491528 | tf_op jit(solution)/shard_map/ppermute | solution.py:376
  70.5 22.5 %all-to-all-start.1 = ((bf16[32,64,128]{2,1,0:T(8,128)(2,1)}), bf16[32,64,128]{2,1,0:T(8,128)(2,1)S(1)}, u32[]{:S(2)}, u32[]{:S(2)}) async-start(bf16[32,64,128]{2,1,0:T(8,128)(2,1)} %bitcast.21), calls=%async_computation.1 | async-start | bytes 1048576 | tf_op jit(solution)/shard_map/all_to_all | solution.py:423
  75.3 8.7 %collective-permute-start.11 = (bf16[2,128,512]{2,1,0:T(8,128)(2,1)S(1)}, bf16[2,128,512]{2,1,0:T(8,128)(2,1)S(1)}, u32[]{:S(2)}, u32[]{:S(2)}) collective-permute-start(bf16[2,128,512]{2,1,0:T(8,128)(2,1)S(1)} %get-tuple-element.22), channel_id=1, source_target_pairs={{64,0},{66,2},{68,4},{70,6},{129,1},{131,3},{133,5},{135,7},{0,64}... | collective-permute-start | bytes 786440 | tf_op jit(solution)/shard_map/ppermute | solution.py:391
  76.5 14.8 %collective-permute-start.12 = (bf16[2,128,512]{2,1,0:T(8,128)(2,1)S(1)}, bf16[2,128,512]{2,1,0:T(8,128)(2,1)S(1)}, u32[]{:S(2)}, u32[]{:S(2)}) collective-permute-start(bf16[2,128,512]{2,1,0:T(8,128)(2,1)S(1)} %get-tuple-element.23), channel_id=1, source_target_pairs={{1,0},{3,2},{5,4},{7,6},{193,1},{195,3},{197,5},{199,7},{64,64},{6... | collective-permute-start | bytes 786440 | tf_op jit(solution)/shard_map/ppermute | solution.py:391
  78.4 12.9 %collective-permute-start.13 = (bf16[2,128,512]{2,1,0:T(8,128)(2,1)S(1)}, bf16[2,128,512]{2,1,0:T(8,128)(2,1)S(1)}, u32[]{:S(2)}, u32[]{:S(2)}) collective-permute-start(bf16[2,128,512]{2,1,0:T(8,128)(2,1)S(1)} %get-tuple-element.24), channel_id=1, source_target_pairs={{65,0},{67,2},{69,4},{71,6},{128,1},{130,3},{132,5},{134,7},{1,64}... | collective-permute-start | bytes 786440 | tf_op jit(solution)/shard_map/ppermute | solution.py:391
  78.7 13.4 %collective-permute-start.14 = (bf16[2,128,512]{2,1,0:T(8,128)(2,1)S(1)}, bf16[2,128,512]{2,1,0:T(8,128)(2,1)S(1)}, u32[]{:S(2)}, u32[]{:S(2)}) collective-permute-start(bf16[2,128,512]{2,1,0:T(8,128)(2,1)S(1)} %get-tuple-element.25), channel_id=1, source_target_pairs={{0,0},{2,2},{4,4},{6,6},{192,1},{194,3},{196,5},{198,7},{65,64},{6... | collective-permute-start | bytes 786440 | tf_op jit(solution)/shard_map/ppermute | solution.py:391
